TPU v7x, 512 devices: a whole 4x8x8 slice. The times are simulated.
512 devices in a mesh: tiles: 128 (over y, z, core), rep: 4 (over x).
Axes of the slice: x: 4, y: 8, z: 8, core: 2. Of those that a mesh axis runs over, the one named last changes fastest.
Arguments:
- lam_tiles: bfloat16 [2048, 128, 128], P('tiles'), may hold values from -6 to 6
- int_tiles: bfloat16 [2048, 128, 128], P('tiles'), may hold values from -0.0625 to 0.0625
- task_list: int32 [65536, 4], P(('tiles', 'rep')), may hold values from 0 to 2047, as said below
- live_count: int32 [512], P(('tiles', 'rep')), may hold values from 16 to 128, as said below
- tile_mask: int32 [2048], P('tiles'), may hold values 0 or 1
- owner_map: int32 [512], replicated, may hold values from 0 to 511, as said below
Outputs:
- residual: bfloat16 [512, 128, 128], P(('tiles', 'rep'))
Inputs may be any that keep to these rules, and one draw needn't show every extreme that they name: `task_list`: each row is (Lambda tile id, integral tile id, residual tile id, code 0 or 1). The Lambda tiles named by a device lie among the 16 tiles of its index of tiles. The four columns hold ids below 2048, 2048, 512 and 2. Among all slots of the devices that share an index of tiles, the integral tiles named from one owner (id // 16) are one and the same tile, and so are the residual tiles whose position lies in one owner's range (owner_map // 4); every device names every owner of both kinds in its first 128 slots. `live_count`: one device of each index of tiles uses all 128 slots. `owner_map`: A permutation of 0 to 511.
All inputs are finite; a program needn't handle non-finite values. No bound on the sum of `tile_mask` on one device may be relied on, other than what follows from the above.
Results may differ from a plain program's by a relative error of at most 0.001.
Values may be sent and summed in bfloat16 or wider, within the bound.
No kernel may reach another device: no remote copies, remote signals or barrier semaphores. Data moves between devices by JAX's collectives and lax.ppermute only.
A program may use at most 128 MiB of HBM per device.

v0:
```python
import jax
import jax.numpy as jnp
from jax import lax
from jax.sharding import PartitionSpec as P


def positions(rows, owner_map):
    matches = rows[:, 2:3] == jnp.arange(owner_map.shape[0])[None, :]
    return jnp.sum(jnp.where(matches, owner_map[None, :], 0), axis=1)


def on_device(lam_tiles, int_tiles, task_list, live_count, tile_mask, owner_map):
    tile_devs = lax.axis_size("tiles")
    tile_index = lax.axis_index("tiles")
    task_dev = task_list.shape[0]
    lam_dev = lam_tiles.shape[0]
    int_dev = int_tiles.shape[0]
    res_total = owner_map.shape[0]
    res_tile = res_total // tile_devs
    peers = jnp.arange(tile_devs)
    raw_w_owner = task_list[:, 1] // int_dev
    raw_w_local = task_list[:, 1] % int_dev
    raw_places = positions(task_list, owner_map)
    hits_w = raw_w_owner[:, None] == peers[None, :]
    wanted = jnp.max(jnp.where(hits_w, raw_w_local[:, None], -1), axis=0)
    hits_o = (raw_places // res_tile)[:, None] == peers[None, :]
    out_slots = jnp.max(jnp.where(hits_o, (raw_places % res_tile)[:, None], -1), axis=0)
    own_live = live_count[0]
    lam_local = jnp.clip(task_list[:, 0] - tile_index * lam_dev, 0, lam_dev - 1)
    w_owner = task_list[:, 1] // int_dev
    o_owner = positions(task_list, owner_map) // res_tile
    flips = task_list[:, 3]
    alive = jnp.arange(task_dev) < own_live
    asked = lax.all_to_all(
        wanted.reshape(tile_devs, 1), "tiles", split_axis=0, concat_axis=0, tiled=True
    ).reshape(-1)
    picked = int_tiles[jnp.clip(asked, 0, int_dev - 1)]
    picked = jnp.where((asked >= 0)[:, None, None], picked, jnp.zeros_like(picked))
    edge = lam_tiles.shape[1]
    fetched = lax.all_to_all(picked, "tiles", split_axis=0, concat_axis=0, tiled=True)
    mask_hits = lam_local[:, None] == jnp.arange(lam_dev)[None, :]
    kept = jnp.sum(jnp.where(mask_hits, tile_mask[None, :], 0), axis=1)
    scales = (alive & (kept == 1)).astype(jnp.float32)
    width = 64
    blocks = task_dev // width
    starts = jnp.arange(blocks) * width
    items = (
        lam_local.reshape(blocks, width),
        w_owner.reshape(blocks, width),
        o_owner.reshape(blocks, width),
        flips.reshape(blocks, width),
        scales.reshape(blocks, width),
        starts,
    )

    def add_block(totals, item):
        lam_part, w_part, o_part, flip_part, scale_part, block_start = item

        def compute(current):
            left = lam_tiles[lam_part]
            left = jnp.where(flip_part[:, None, None] == 1, jnp.swapaxes(left, 1, 2), left)
            right = fetched[w_part]
            product = jnp.einsum("tik,tkj->tij", left, right, preferred_element_type=jnp.float32)
            product = product * scale_part[:, None, None]
            return current.at[o_part].add(product)

        def unchanged(current):
            return current

        return (lax.cond(block_start < own_live, compute, unchanged, totals), None)

    totals = jnp.zeros((tile_devs, edge, edge), jnp.float32)
    totals, _ = lax.scan(add_block, totals, items)
    slot_column = out_slots.reshape(tile_devs, 1)
    partial_tiles, slot_ids = (
        lax.all_to_all(totals, "tiles", split_axis=0, concat_axis=0, tiled=True),
        lax.all_to_all(slot_column, "tiles", split_axis=0, concat_axis=0, tiled=True),
    )
    slot_hits = (slot_ids == jnp.arange(res_tile)[None, :]).astype(jnp.float32)
    owned = jnp.einsum("sk,sij->kij", slot_hits, partial_tiles, precision=lax.Precision.HIGHEST)
    summed = lax.psum_scatter(owned, "rep", scatter_dimension=0, tiled=True)
    return summed.astype(jnp.bfloat16)


def solution(mesh):
    placed = (
        P("tiles", None, None),
        P("tiles", None, None),
        P(("tiles", "rep"), None),
        P(("tiles", "rep")),
        P("tiles"),
        P(),
    )
    return jax.shard_map(
        on_device,
        mesh=mesh,
        in_specs=placed,
        out_specs=P(("tiles", "rep"), None, None),
        check_vma=False,
    )
```

profile of v0, /device:TPU:1, one launch (start us, length us, event | category | flops | bytes accessed | tf_op | source)
XLA Modules:
  0.0 553.0 jit_solution(8485884722036069006)
XLA Ops:
  6.5 0.0 copy-start
  6.5 0.8 fusion.16
  7.4 0.1 select_reduce_fusion.1
  7.5 0.1 copy.26
  7.6 29.7 %all_to_all.28 = s32[128,1,1]{2,1,0:T(1,128)S(1)} all-to-all(s32[128,1,1]{2,1,0:T(1,128)S(1)} %copy.26), channel_id=1, replica_groups=mesh['tiles'=128,'rep'=4] {'tiles'}, dimensions={0} | all-to-all | bytes 1024 | tf_op jit(solution)/shard_map/all_to_all | solution.py:34
  37.4 2.4 clamp_reduce_fusion
  39.7 0.0 copy-done
  39.8 3.1 gather_fusion.2
  42.8 2.4 compare_reduce_fusion
  45.2 4.5 broadcast_select_fusion
  49.7 0.0 copy-start.2
  49.7 0.0 copy-start.3
  49.7 7.0 %all-to-all-start.2 = ((bf16[128,128,128]{2,1,0:T(8,128)(2,1)}), bf16[128,128,128]{2,1,0:T(8,128)(2,1)}, u32[]{:S(2)}, u32[]{:S(2)}) async-start(bf16[128,128,128]{2,1,0:T(8,128)(2,1)} %broadcast_select_fusion), calls=%async_computation.2 | async-start | bytes 8388608 | tf_op jit(solution)/shard_map/all_to_all | solution.py:40
  56.7 0.0 copy-done.2
  56.7 0.2 select_reduce_fusion
  56.9 0.1 reduce_sum.25
  57.0 0.1 squeeze.41
  57.0 0.0 copy-done.3
  57.0 0.1 select_reduce_fusion.3
  57.1 0.1 eq.120
  57.9 0.1 min.22
  58.0 0.1 reshape_squeeze.3
  58.1 0.1 select_reduce_fusion.2
  58.2 0.8 copy.25
  59.0 93.7 %all-to-all-done.2 = bf16[128,128,128]{2,1,0:T(8,128)(2,1)} async-done(((bf16[128,128,128]{2,1,0:T(8,128)(2,1)}), bf16[128,128,128]{2,1,0:T(8,128)(2,1)}, u32[]{:S(2)}, u32[]{:S(2)}) %all-to-all-start.2) | async-done | bytes 4194336 | tf_op jit(solution)/shard_map/all_to_all | solution.py:40
  152.7 16.7 %all-to-all-start = ((s32[128,1,1]{2,1,0:T(1,128)}), s32[128,1,1]{2,1,0:T(1,128)S(1)}, u32[]{:S(2)}, u32[]{:S(2)}) async-start(s32[128,1,1]{2,1,0:T(1,128)} %copy.25), calls=%async_computation | async-start | bytes 131072 | tf_op jit(solution)/shard_map/all_to_all | solution.py:77
  169.4 0.0 copy-start.1
  169.4 4.3 broadcast_in_dim.102
  173.7 0.0 copy-done.1
  173.7 58.4 %while.13 = (s32[]{:T(128)}, f32[128,128,128]{2,1,0:T(8,128)}, s32[2]{0:T(128)S(1)}, s32[]{:T(128)}, s32[2,64]{1,0:T(2,128)S(1)}, /*index=5*/s32[2,64]{1,0:T(2,1...) while((s32[]{:T(128)}, f32[128,128,128]{2,1,0:T(8,128)}, ...), condition=%wide.region_8.9_spmd, body=%wide.region_4.8_spmd.sunk | while | flops 271583872 | bytes 35663984 | solution.py:73
  173.7 0.6 dynamic_slice.74
  175.6 27.3 %conditional.2 = (f32[128,128,128]{2,1,0:T(8,128)}) conditional(s32[]{:T(128)} %convert_element_type.15, f32[128,128,128]{2,1,0:T(8,128)} %get-tuple-element.279, (s32[2,64]{1,0:T(2,128)S(1)}, s32[]{:T(128)}, s32[2,64]{1,0:T(2,128)S(1)}, s32[2,64]{1,0:T(2,128)S(1)}, bf16[16,128,128]{2,1,0:T(8,128)(2,1)S(1)}, /*index=5*/s32[2,64]{1,0:T(2,128)S(1)}, ...), branch_computations={%region_5.5_spmd, %region_6.7_spmd} | conditional | flops 271583872 | bytes 35663768 | solution.py:70
  175.6 1.0 gather_fusion
  176.6 2.9 copy.23
  179.5 4.4 gather_fusion.1
  183.9 5.4 convolution_multiply_fusion
  189.3 13.6 %scatter_fusion = f32[128,128,128]{2,1,0:T(8,128)} fusion(f32[128,128,128]{2,1,0:T(8,128)} %get-tuple-element.136, s32[64]{0:T(128)S(1)} %get-tuple-element.186, f32[64,128,128]{2,1,0:T(8,128)} %convolution_multiply_fusion), kind=kCustom, calls=%fused_computation.3 | custom fusion | flops 1048576 | bytes 12583168 | tf_op jit(solution)/shard_map/while/body/eval_jaxpr/cond/branch_1_fun/scatter-add | solution.py:65
  202.9 0.6 dynamic_slice.74
  204.7 27.4 %conditional.2 = (f32[128,128,128]{2,1,0:T(8,128)}) conditional(s32[]{:T(128)} %convert_element_type.15, f32[128,128,128]{2,1,0:T(8,128)} %get-tuple-element.279, (s32[2,64]{1,0:T(2,128)S(1)}, s32[]{:T(128)}, s32[2,64]{1,0:T(2,128)S(1)}, s32[2,64]{1,0:T(2,128)S(1)}, bf16[16,128,128]{2,1,0:T(8,128)(2,1)S(1)}, /*index=5*/s32[2,64]{1,0:T(2,128)S(1)}, ...), branch_computations={%region_5.5_spmd, %region_6.7_spmd} | conditional | flops 271583872 | bytes 35663768 | solution.py:70
  204.8 1.0 gather_fusion
  205.7 2.9 copy.23
  208.7 4.4 gather_fusion.1
  213.1 5.4 convolution_multiply_fusion
  218.4 13.7 %scatter_fusion = f32[128,128,128]{2,1,0:T(8,128)} fusion(f32[128,128,128]{2,1,0:T(8,128)} %get-tuple-element.136, s32[64]{0:T(128)S(1)} %get-tuple-element.186, f32[64,128,128]{2,1,0:T(8,128)} %convolution_multiply_fusion), kind=kCustom, calls=%fused_computation.3 | custom fusion | flops 1048576 | bytes 12583168 | tf_op jit(solution)/shard_map/while/body/eval_jaxpr/cond/branch_1_fun/scatter-add | solution.py:65
  232.1 0.0 all-to-all-done
  232.1 14.2 %all-to-all-start.3 = ((f32[128,128,128]{2,1,0:T(8,128)}), f32[128,128,128]{2,1,0:T(8,128)}, u32[]{:S(2)}, u32[]{:S(2)}) async-start(f32[128,128,128]{2,1,0:T(8,128)} %get-tuple-element.158), calls=%async_computation.3 | async-start | bytes 16777216 | tf_op jit(solution)/shard_map/all_to_all | solution.py:76
  246.3 0.0 reduce-scatter.2.cloned.1.call-start
  246.4 2.4 reduce
  248.7 225.6 %all-to-all-done.3 = f32[128,128,128]{2,1,0:T(8,128)} async-done(((f32[128,128,128]{2,1,0:T(8,128)}), f32[128,128,128]{2,1,0:T(8,128)}, u32[]{:S(2)}, u32[]{:S(2)}) %all-to-all-start.3) | async-done | bytes 8388640 | tf_op jit(solution)/shard_map/all_to_all | solution.py:76
  474.4 10.4 %fusion.8 = f32[4,128,128]{2,0,1:T(4,128)S(1)} fusion(f32[128,128,128]{2,1,0:T(8,128)} %all-to-all-done.3, s32[128]{0:T(128)S(1)} %reduce), kind=kOutput, calls=%fused_computation.25 | convolution fusion | flops 100663808 | bytes 8651264 | tf_op jit(solution)/shard_map/sk,sij->kij/dot_general | solution.py:80
  484.8 0.7 copy.28
  485.5 0.0 reduce-scatter.2.cloned.1.call-update
  485.5 59.2 %reduce-scatter.2.cloned.1.call-done = f32[1,128,128]{2,1,0:T(8,128)} async-done(((f32[4,128,128]{2,1,0:T(8,128)}), f32[1,128,128]{2,1,0:T(8,128)}) %reduce-scatter.2.cloned.1.call-update) | async-done | bytes 65552 | tf_op jit(solution)/shard_map/reduce_scatter | solution.py:81
  544.7 1.5 convert_element_type.12
  (20 shorter events, 0.2 us)
Async XLA Ops:
  6.5 33.2 %copy-start = (bf16[16,128,128]{2,1,0:T(8,128)(2,1)S(1)}, bf16[16,128,128]{2,1,0:T(8,128)(2,1)}, u32[]{:S(2)}) copy-start(bf16[16,128,128]{2,1,0:T(8,128)(2,1)} %param.11) | copy-start | bytes 1572868
  49.7 7.0 %copy-start.2 = (s32[512]{0:T(512)S(1)}, s32[512]{0:T(512)}, u32[]{:S(2)}) copy-start(s32[512]{0:T(512)} %param.15) | copy-start | bytes 6148
  49.7 7.4 %copy-start.3 = (s32[16]{0:T(128)S(1)}, s32[16]{0:T(128)}, u32[]{:S(2)}) copy-start(s32[16]{0:T(128)} %param.14) | copy-start | bytes 196
  49.7 103.0 %all-to-all-start.2 = ((bf16[128,128,128]{2,1,0:T(8,128)(2,1)}), bf16[128,128,128]{2,1,0:T(8,128)(2,1)}, u32[]{:S(2)}, u32[]{:S(2)}) async-start(bf16[128,128,128]{2,1,0:T(8,128)(2,1)} %broadcast_select_fusion), calls=%async_computation.2 | async-start | bytes 8388608 | tf_op jit(solution)/shard_map/all_to_all | solution.py:40
  152.7 79.5 %all-to-all-start = ((s32[128,1,1]{2,1,0:T(1,128)}), s32[128,1,1]{2,1,0:T(1,128)S(1)}, u32[]{:S(2)}, u32[]{:S(2)}) async-start(s32[128,1,1]{2,1,0:T(1,128)} %copy.25), calls=%async_computation | async-start | bytes 131072 | tf_op jit(solution)/shard_map/all_to_all | solution.py:77
  169.4 4.3 copy-start.1
  232.1 242.2 %all-to-all-start.3 = ((f32[128,128,128]{2,1,0:T(8,128)}), f32[128,128,128]{2,1,0:T(8,128)}, u32[]{:S(2)}, u32[]{:S(2)}) async-start(f32[128,128,128]{2,1,0:T(8,128)} %get-tuple-element.158), calls=%async_computation.3 | async-start | bytes 16777216 | tf_op jit(solution)/shard_map/all_to_all | solution.py:76
  246.3 298.4 %reduce-scatter.2.cloned.1.call-start = ((), (), s32[]{:S(2)}) async-start(), calls=%async_computation.5 | async-start | bytes 327680 | tf_op jit(solution)/shard_map/reduce_scatter | solution.py:81
Sparse Core Ops, SparseCore 0:
  485.6 59.0 reduce-scatter.1
where the time goes:
time: 555 us; the launch traced here: 553 us
  waiting for transfers between devices  379 us (68%)
  other arithmetic  41.9 us (8%)
  starting transfers between devices  37.9 us (7%)
  blocking collectives  29.7 us (5%)
  local copies, waits for them, and re-layouts  27 us (5%)
  matrix products  21.1 us (4%)
  between operations  14.2 us (3%)
    all_to_all x1, waiting for transfers between devices, on_device(): lax.all_to_all(totals, 'tiles', split_axis=0, concat_axis=0, tiled=True)  226 us
    all_to_all x1, waiting for transfers between devices, on_device(): lax.all_to_all(picked, 'tiles', split_axis=0, concat_axis=0, tiled=True)  93.7 us
    reduce_scatter x1, waiting for transfers between devices, on_device(): summed = lax.psum_scatter(owned, 'rep', scatter_dimension=0, tiled=True)  59.2 us
    all_to_all x1, blocking collectives, on_device(): lax.all_to_all(wanted.reshape(tile_devs, 1), 'tiles', split_axis=0, conca...  29.7 us
    scatter-add x2, other arithmetic, compute(): return current.at[o_part].add(product)  27.3 us
    all_to_all x1, starting transfers between devices, on_device(): lax.all_to_all(slot_column, 'tiles', split_axis=0, concat_axis=0, tiled=T...  16.7 us
    all_to_all x1, starting transfers between devices, on_device(): lax.all_to_all(totals, 'tiles', split_axis=0, concat_axis=0, tiled=True)  14.2 us
  transfers between devices with their start and end apart: 4, of which 3 were waited for; matrix products, arithmetic and copies ran while one was open for 12% of the time, Pallas kernels for 0%

commit v1 on v0

v1 whole, which is shorter than its diff:
```python
import jax
import jax.numpy as jnp
from jax import lax
from jax.experimental import pallas as pl
from jax.experimental.pallas import tpu as pltpu
from jax.sharding import PartitionSpec as P

VMEM = pl.BlockSpec(memory_space=pltpu.VMEM)
SMEM = pl.BlockSpec(memory_space=pltpu.SMEM)


def ring(values, steps):
    reps = lax.axis_size("rep")
    return lax.ppermute(values, "rep", [(i, (i + steps) % reps) for i in range(reps)])


def prepare_lambda(lam_ref, out_ref):
    count = lam_ref.shape[0]
    for tile in range(count):
        out_ref[tile] = lam_ref[tile].T
        out_ref[count + tile] = lam_ref[tile]
    out_ref[2 * count] = jnp.zeros_like(out_ref[2 * count])


def prepare_integrals(start_ref, int_ref, out_ref, turned):
    count, rows, _ = out_ref.shape
    start = pl.multiple_of(start_ref[0], rows)
    for tile in range(count):
        turned[tile] = int_ref[tile].T
        out_ref[tile] = turned[tile, pl.ds(start, rows), :]


def pick(asked_ref, tiles_ref, out_ref):
    def body(peer, carry):
        out_ref[peer] = tiles_ref[asked_ref[peer]]
        return carry

    lax.fori_loop(0, out_ref.shape[0], body, 0, unroll=8)


def contract(variant_ref, source_ref, lam_ref, w_ref, out_ref):
    reps = variant_ref.shape[0]

    def body(owner, carry):
        left = [w_ref[source_ref[r, owner]] for r in range(reps)]
        right = [lam_ref[variant_ref[r, owner]] for r in range(reps)]
        out_ref[owner] = jnp.dot(
            jnp.concatenate(left, axis=1),
            jnp.concatenate(right, axis=0),
            preferred_element_type=jnp.float32,
        )
        return carry

    lax.fori_loop(0, out_ref.shape[0], body, 0, unroll=4)


def add_slots(slot_ref, x_ref, out_ref):
    slots = out_ref.shape[0]

    def body(peer, sums):
        value = x_ref[peer]
        slot = slot_ref[peer]
        return tuple(s + jnp.where(slot == k, value, 0.0) for k, s in enumerate(sums))

    zero = jnp.zeros(x_ref.shape[1:], jnp.float32)
    sums = lax.fori_loop(0, x_ref.shape[0], body, (zero,) * slots, unroll=4)
    for k in range(slots):
        out_ref[k] = sums[k].astype(out_ref.dtype)


def on_device(lam_tiles, int_tiles, task_list, live_count, tile_mask, owner_map):
    tile_devs = lax.axis_size("tiles")
    reps = lax.axis_size("rep")
    tile_index = lax.axis_index("tiles")
    rep_index = lax.axis_index("rep")
    task_dev = task_list.shape[0]
    lam_dev, edge, _ = lam_tiles.shape
    int_dev = int_tiles.shape[0]
    res_tile = owner_map.shape[0] // tile_devs
    rows = edge // reps
    peers = jnp.arange(tile_devs)

    matches = task_list[:, 2:3] == jnp.arange(owner_map.shape[0])[None, :]
    places = jnp.sum(jnp.where(matches, owner_map[None, :], 0), axis=1)
    w_owner = task_list[:, 1] // int_dev
    hits_w = w_owner[:, None] == peers[None, :]
    hits_o = (places // res_tile)[:, None] == peers[None, :]
    asked = jnp.sum(jnp.where(hits_w, (task_list[:, 1] % int_dev)[:, None], 0), axis=0)
    slots = jnp.sum(jnp.where(hits_o, (places % res_tile)[:, None], 0), axis=0)
    request = asked * res_tile + slots
    request = lax.all_to_all(
        request.reshape(tile_devs, 1, 1), "tiles", split_axis=0, concat_axis=0, tiled=True
    ).reshape(-1)

    lam_local = jnp.clip(task_list[:, 0] - tile_index * lam_dev, 0, lam_dev - 1)
    mask_hits = lam_local[:, None] == jnp.arange(lam_dev)[None, :]
    kept = jnp.sum(jnp.where(mask_hits, tile_mask[None, :], 0), axis=1) == 1
    kept = kept & (jnp.arange(task_dev) < live_count[0])
    variant = jnp.where(kept, lam_local + lam_dev * task_list[:, 3], 2 * lam_dev)
    coded = variant * tile_devs + w_owner
    by_owner = jnp.sum(jnp.where(hits_o, coded[:, None], 0), axis=0)
    all_coded = jnp.stack([by_owner] + [ring(by_owner, k) for k in range(1, reps)])

    lam_all = pl.pallas_call(
        prepare_lambda,
        out_shape=jax.ShapeDtypeStruct((2 * lam_dev + 1, edge, edge), jnp.bfloat16),
        in_specs=[VMEM],
        out_specs=VMEM,
        name="prepare_lambda",
    )(lam_tiles)
    columns = pl.pallas_call(
        prepare_integrals,
        out_shape=jax.ShapeDtypeStruct((int_dev, rows, edge), jnp.bfloat16),
        in_specs=[SMEM, VMEM],
        out_specs=VMEM,
        scratch_shapes=[pltpu.VMEM((int_dev, edge, edge), jnp.bfloat16)],
        name="prepare_integrals",
    )((rep_index * rows).reshape(1), int_tiles)
    picked = pl.pallas_call(
        pick,
        out_shape=jax.ShapeDtypeStruct((tile_devs, rows, edge), jnp.bfloat16),
        in_specs=[SMEM, VMEM],
        out_specs=VMEM,
        name="pick",
    )(request // res_tile, columns)
    fetched = lax.all_to_all(picked, "tiles", split_axis=0, concat_axis=0, tiled=True)

    totals = pl.pallas_call(
        contract,
        out_shape=jax.ShapeDtypeStruct((tile_devs, rows, edge), jnp.float32),
        in_specs=[SMEM, SMEM, VMEM, VMEM],
        out_specs=VMEM,
        name="contract",
    )(all_coded // tile_devs, all_coded % tile_devs, lam_all, fetched)
    partial_tiles = lax.all_to_all(totals, "tiles", split_axis=0, concat_axis=0, tiled=True)
    summed = pl.pallas_call(
        add_slots,
        out_shape=jax.ShapeDtypeStruct((res_tile, rows, edge), jnp.bfloat16),
        in_specs=[SMEM, VMEM],
        out_specs=VMEM,
        name="add_slots",
    )(request % res_tile, partial_tiles)
    mine = lax.all_to_all(summed, "rep", split_axis=0, concat_axis=0, tiled=True)
    return mine.reshape(edge, edge).T[None]


def solution(mesh):
    placed = (
        P("tiles", None, None),
        P("tiles", None, None),
        P(("tiles", "rep"), None),
        P(("tiles", "rep")),
        P("tiles"),
        P(),
    )
    return jax.shard_map(
        on_device,
        mesh=mesh,
        in_specs=placed,
        out_specs=P(("tiles", "rep"), None, None),
        check_vma=False,
    )
```

time: 555 us -> 160 us (0.29)
  waiting for transfers between devices: 379 us -> 27.8 us
  blocking collectives: 29.7 us -> 68.4 us
  other arithmetic: 41.9 us -> 6.88 us
  local copies, waits for them, and re-layouts: 27 us -> 2.43 us
  matrix products: 21.1 us -> 0 us
  Pallas kernels: 0 us -> 19 us
  between operations: 14.2 us -> 0.73 us
    all_to_all x2 -> x1, waiting for transfers between devices: 226 us -> 9.65 us  [on_device(): lax.all_to_all(request.reshape(tile_devs, 1, 1), 'tiles', split_axis=0, c...]
    all_to_all x1, waiting for transfers between devices: 93.7 us -> 17.2 us  [on_device(): lax.all_to_all(picked, 'tiles', split_axis=0, concat_axis=0, tiled=True)]
    reduce_scatter x1 -> x0, waiting for transfers between devices: 59.2 us -> none  [on_device(): summed = lax.psum_scatter(owned, 'rep', scatter_dimension=0, tiled=True)]
    all_to_all x1 -> x2, blocking collectives: 29.7 us -> 68.4 us  [the longest x1 60.1 us: on_device(): lax.all_to_all(totals, 'tiles', split_axis=0, concat_axis=0, tiled=True)]
    scatter-add x2 -> x0, other arithmetic: 27.3 us -> none  [compute(): return current.at[o_part].add(product)]
    dot_general x3 -> x0, matrix products: 21.1 us -> none  [the longest x2 10.7 us: compute(): jnp.einsum('tik,tkj->tij', left, right, preferred_element_type=jnp.float32)]
    gather x7 -> x0, local copies, waits for them, and re-layouts: 19.5 us -> none  [the longest x2 8.7 us: compute(): right = fetched[w_part]]
    pallas_call x0 -> x5, Pallas kernels: none -> 19 us  [the longest x1 9.58 us: on_device(): pl.pallas_call(contract, out_shape=jax.ShapeDtypeStruct((tile_devs, rows,...]
  transfers between devices with their start and end apart: 4 -> 5, of which waited for: 3 -> 3; matrix products, arithmetic and copies ran while one was open for 12% -> 0% of each run, Pallas kernels for 0% -> 3%
where the time goes in v1:
time: 160 us; the launch traced here: 159 us
  blocking collectives  68.4 us (43%)
  starting transfers between devices  33.5 us (21%)
  waiting for transfers between devices  27.8 us (17%)
  Pallas kernels  19 us (12%)
  other arithmetic  6.88 us (4%)
  local copies, waits for them, and re-layouts  2.43 us (2%)
    all_to_all x1, blocking collectives, on_device(): lax.all_to_all(totals, 'tiles', split_axis=0, concat_axis=0, tiled=True)  60.1 us
    all_to_all x1, starting transfers between devices, on_device(): lax.all_to_all(request.reshape(tile_devs, 1, 1), 'tiles', split_axis=0, c...  18.4 us
    all_to_all x1, waiting for transfers between devices, on_device(): lax.all_to_all(picked, 'tiles', split_axis=0, concat_axis=0, tiled=True)  17.2 us
    all_to_all x1, waiting for transfers between devices, on_device(): lax.all_to_all(request.reshape(tile_devs, 1, 1), 'tiles', split_axis=0, c...  9.65 us
    pallas_call x1, Pallas kernels, on_device(): pl.pallas_call(contract, out_shape=jax.ShapeDtypeStruct((tile_devs, rows,...  9.58 us
    ppermute x3, starting transfers between devices, ring(): lax.ppermute(values, 'rep', [(i, (i + steps) % reps) for i in range(reps)])  9.33 us
    all_to_all x1, blocking collectives, on_device(): lax.all_to_all(summed, 'rep', split_axis=0, concat_axis=0, tiled=True)  8.31 us
    all_to_all x1, starting transfers between devices, on_device(): lax.all_to_all(picked, 'tiles', split_axis=0, concat_axis=0, tiled=True)  5.72 us
  transfers between devices with their start and end apart: 5, of which 3 were waited for; matrix products, arithmetic and copies ran while one was open for 0% of the time, Pallas kernels for 3%

profile of v1, /device:TPU:1, one launch (start us, length us, event | category | flops | bytes accessed | tf_op | source)
XLA Modules:
  0.0 158.8 jit_solution(5548497931613494063)
XLA Ops:
  0.7 0.8 fusion.2
  1.5 0.9 select_reduce_fusion
  2.3 0.7 select_reduce_fusion.4
  3.1 0.8 add_bitcast_fusion
  3.9 0.2 select_reduce_fusion.1
  4.1 0.7 copy.12
  4.8 18.4 %all-to-all-start = ((s32[128,1,1]{2,1,0:T(1,128)}), s32[128,1,1]{2,1,0:T(1,128)S(1)}, u32[]{:S(2)}, u32[]{:S(2)}) async-start(s32[128,1,1]{2,1,0:T(1,128)} %copy.12), calls=%async_computation | async-start | bytes 131072 | tf_op jit(solution)/shard_map/all_to_all | solution.py:91
  23.2 1.9 %prepare_integrals.1.tiles_ref = bf16[16,32,128]{2,1,0:T(8,128)(2,1)} custom-call(s32[1]{0:T(128)} %bitcast.12.start_ref, bf16[16,128,128]{2,1,0:T(8,128)(2,1)} %int_ref.1), custom_call_target="tpu_custom_call" | custom-call | tf_op jit(solution)/shard_map/prepare_integrals/pallas_call | solution.py:111
  25.1 9.6 %all-to-all-done = s32[128,1,1]{2,1,0:T(1,128)S(1)} async-done(((s32[128,1,1]{2,1,0:T(1,128)}), s32[128,1,1]{2,1,0:T(1,128)S(1)}, u32[]{:S(2)}, u32[]{:S(2)}) %all-to-all-start) | async-done | bytes 544 | tf_op jit(solution)/shard_map/all_to_all | solution.py:91
  34.8 2.3 %reduce = s32[128]{0:T(128)S(1)} reduce(s32[128,1,1]{2,1,0:T(1,128)S(1)} %all-to-all-done, s32[]{:T(128)} %constant.87.clone.1), dimensions={1,2}, to_apply=%all_to_all.12.reduce_sub_computation | reduce | bytes 1028 | tf_op jit(solution)/shard_map/all_to_all | solution.py:91
  37.1 0.5 and_select_fusion
  37.7 2.1 %pick.1 = bf16[128,32,128]{2,1,0:T(8,128)(2,1)} custom-call(s32[128]{0:T(128)} %get-tuple-element.15.asked_ref, bf16[16,32,128]{2,1,0:T(8,128)(2,1)} %prepare_integrals.1.tiles_ref), custom_call_target="tpu_custom_call" | custom-call | tf_op jit(solution)/shard_map/pick/pallas_call | solution.py:119
  39.8 5.7 %all-to-all-start.1 = ((bf16[128,32,128]{2,1,0:T(8,128)(2,1)}), bf16[128,32,128]{2,1,0:T(8,128)(2,1)S(1)}, u32[]{:S(2)}, u32[]{:S(2)}) async-start(bf16[128,32,128]{2,1,0:T(8,128)(2,1)} %pick.1), calls=%async_computation.1 | async-start | bytes 2097152 | tf_op jit(solution)/shard_map/all_to_all | solution.py:126
  45.5 4.4 %collective-permute-start.2 = (s32[128]{0:T(128)S(1)}, s32[128]{0:T(128)S(1)}, u32[]{:S(2)}, u32[]{:S(2)}) collective-permute-start(s32[128]{0:T(128)S(1)} %get-tuple-element.5), channel_id=1, source_target_pairs={{0,3},{1,0},{2,1},{3,2},{4,7},{5,4},{6,5},{7,6},{8,11},{9,8},{10,9... | collective-permute-start | bytes 1544 | tf_op jit(solution)/shard_map/ppermute | solution.py:14
  49.9 2.4 %collective-permute-start.1 = (s32[128]{0:T(128)S(1)}, s32[128]{0:T(128)S(1)}, u32[]{:S(2)}, u32[]{:S(2)}) collective-permute-start(s32[128]{0:T(128)S(1)} %get-tuple-element.5), channel_id=1, source_target_pairs={{0,2},{1,3},{2,0},{3,1},{4,6},{5,7},{6,4},{7,5},{8,10},{9,11},{10,... | collective-permute-start | bytes 1544 | tf_op jit(solution)/shard_map/ppermute | solution.py:14
  52.3 2.5 %collective-permute-start = (s32[128]{0:T(128)S(1)}, s32[128]{0:T(128)S(1)}, u32[]{:S(2)}, u32[]{:S(2)}) collective-permute-start(s32[128]{0:T(128)S(1)} %get-tuple-element.5), channel_id=1, source_target_pairs={{0,1},{1,2},{2,3},{3,0},{4,5},{5,6},{6,7},{7,4},{8,9},{9,10},{10,1... | collective-permute-start | bytes 1544 | tf_op jit(solution)/shard_map/ppermute | solution.py:14
  54.9 2.2 %prepare_lambda.1.lam_ref = bf16[33,128,128]{2,1,0:T(8,128)(2,1)} custom-call(bf16[16,128,128]{2,1,0:T(8,128)(2,1)} %lam_ref.1), custom_call_target="tpu_custom_call" | custom-call | tf_op jit(solution)/shard_map/prepare_lambda/pallas_call | solution.py:104
  57.1 0.0 collective-permute-done.2
  57.1 0.0 collective-permute-done.1
  57.1 1.0 collective-permute-done
  58.1 0.6 add_select_fusion
  58.7 17.2 %all-to-all-done.1.w_ref = bf16[128,32,128]{2,1,0:T(8,128)(2,1)S(1)} async-done(((bf16[128,32,128]{2,1,0:T(8,128)(2,1)}), bf16[128,32,128]{2,1,0:T(8,128)(2,1)S(1)}, u32[]{:S(2)}, u32[]{:S(2)}) %all-to-all-start.1) | async-done | bytes 1048608 | tf_op jit(solution)/shard_map/all_to_all | solution.py:126
  75.9 0.0 copy-start
  75.9 1.0 copy-done
  76.9 9.6 %contract.1 = f32[128,32,128]{2,1,0:T(8,128)} custom-call(s32[4,128]{1,0:T(4,128)} %get-tuple-element.12.variant_ref, s32[4,128]{1,0:T(4,128)} %get-tuple-element.11.source_ref, bf16[33,128,128]{2,1,0:T(8,128)(2,1)} %prepare_lambda.1.lam_ref, bf16[128,32,128]{2,1,0:T(8,128)(2,1)} %copy-done), custom_call_target="tpu_custom_call" | custom-call | tf_op jit(solution)/shard_map/contract/pallas_call | solution.py:128
  86.5 60.1 %all_to_all.20.x_ref = f32[128,32,128]{2,1,0:T(8,128)} all-to-all(f32[128,32,128]{2,1,0:T(8,128)} %contract.1), channel_id=1, replica_groups=mesh['tiles'=128,'rep'=4] {'tiles'}, dimensions={0} | all-to-all | bytes 4194304 | tf_op jit(solution)/shard_map/all_to_all | solution.py:135
  146.5 3.2 %add_slots.1 = bf16[4,32,128]{2,1,0:T(8,128)(2,1)} custom-call(s32[128]{0:T(128)} %get-tuple-element.16.slot_ref, f32[128,32,128]{2,1,0:T(8,128)} %all_to_all.20.x_ref), custom_call_target="tpu_custom_call" | custom-call | tf_op jit(solution)/shard_map/add_slots/pallas_call | solution.py:136
  149.7 8.3 %all_to_all.21 = bf16[4,32,128]{2,1,0:T(8,128)(2,1)S(1)} all-to-all(bf16[4,32,128]{2,1,0:T(8,128)(2,1)} %add_slots.1), channel_id=1, replica_groups=mesh['tiles'=128,'rep'=4] {'rep'}, dimensions={0} | all-to-all | bytes 65536 | tf_op jit(solution)/shard_map/all_to_all | solution.py:143
  158.0 0.7 copy.13
  (2 shorter events, 0.0 us)
Async XLA Ops:
  4.8 30.0 %all-to-all-start = ((s32[128,1,1]{2,1,0:T(1,128)}), s32[128,1,1]{2,1,0:T(1,128)S(1)}, u32[]{:S(2)}, u32[]{:S(2)}) async-start(s32[128,1,1]{2,1,0:T(1,128)} %copy.12), calls=%async_computation | async-start | bytes 131072 | tf_op jit(solution)/shard_map/all_to_all | solution.py:91
  39.8 36.1 %all-to-all-start.1 = ((bf16[128,32,128]{2,1,0:T(8,128)(2,1)}), bf16[128,32,128]{2,1,0:T(8,128)(2,1)S(1)}, u32[]{:S(2)}, u32[]{:S(2)}) async-start(bf16[128,32,128]{2,1,0:T(8,128)(2,1)} %pick.1), calls=%async_computation.1 | async-start | bytes 2097152 | tf_op jit(solution)/shard_map/all_to_all | solution.py:126
  45.5 11.6 %collective-permute-start.2 = (s32[128]{0:T(128)S(1)}, s32[128]{0:T(128)S(1)}, u32[]{:S(2)}, u32[]{:S(2)}) collective-permute-start(s32[128]{0:T(128)S(1)} %get-tuple-element.5), channel_id=1, source_target_pairs={{0,3},{1,0},{2,1},{3,2},{4,7},{5,4},{6,5},{7,6},{8,11},{9,8},{10,9... | collective-permute-start | bytes 1544 | tf_op jit(solution)/shard_map/ppermute | solution.py:14
  49.9 7.2 %collective-permute-start.1 = (s32[128]{0:T(128)S(1)}, s32[128]{0:T(128)S(1)}, u32[]{:S(2)}, u32[]{:S(2)}) collective-permute-start(s32[128]{0:T(128)S(1)} %get-tuple-element.5), channel_id=1, source_target_pairs={{0,2},{1,3},{2,0},{3,1},{4,6},{5,7},{6,4},{7,5},{8,10},{9,11},{10,... | collective-permute-start | bytes 1544 | tf_op jit(solution)/shard_map/ppermute | solution.py:14
  52.3 5.8 %collective-permute-start = (s32[128]{0:T(128)S(1)}, s32[128]{0:T(128)S(1)}, u32[]{:S(2)}, u32[]{:S(2)}) collective-permute-start(s32[128]{0:T(128)S(1)} %get-tuple-element.5), channel_id=1, source_target_pairs={{0,1},{1,2},{2,3},{3,0},{4,5},{5,6},{6,7},{7,4},{8,9},{9,10},{10,1... | collective-permute-start | bytes 1544 | tf_op jit(solution)/shard_map/ppermute | solution.py:14
  75.9 1.0 copy-start

commit v2 on v1

v2 whole, which is shorter than its diff:
```python
import functools

import jax
import jax.numpy as jnp
from jax import lax
from jax.experimental import pallas as pl
from jax.experimental.pallas import tpu as pltpu
from jax.sharding import PartitionSpec as P

VMEM = pl.BlockSpec(memory_space=pltpu.VMEM)
OCTAVE = 256.0
FULL = 32760.0
SMALLEST = 2.0**-120
SMEM = pl.BlockSpec(memory_space=pltpu.SMEM)


def ring(values, steps):
    reps = lax.axis_size("rep")
    return lax.ppermute(values, "rep", [(i, (i + steps) % reps) for i in range(reps)])


def prepare_lambda(lam_ref, out_ref):
    count = lam_ref.shape[0]
    for tile in range(count):
        out_ref[tile] = lam_ref[tile].T
        out_ref[count + tile] = lam_ref[tile]
    out_ref[2 * count] = jnp.zeros_like(out_ref[2 * count])


def prepare_integrals(start_ref, int_ref, out_ref, turned):
    count, rows, _ = out_ref.shape
    start = pl.multiple_of(start_ref[0], rows)
    for tile in range(count):
        turned[tile] = int_ref[tile].T
        out_ref[tile] = turned[tile, pl.ds(start, rows), :]


def read_tasks(live_ref, mask_ref, task_ref, map_ref, request_ref, code_ref, int_dev, res_tile):
    lam_dev = mask_ref.shape[0]
    task_dev = task_ref.shape[1]
    peers = request_ref.shape[0]
    res_total = map_ref.shape[1]
    placed = map_ref[...]
    parts = jnp.concatenate(
        [placed // res_tile, placed % res_tile, jnp.zeros((6, res_total), jnp.int32)], axis=0
    )
    named = lax.broadcasted_iota(jnp.int32, (res_total, task_dev), 0) == task_ref[2:3, :]
    looked_up = jnp.dot(
        parts.astype(jnp.float32).astype(jnp.bfloat16),
        jnp.where(named, 1.0, 0.0).astype(jnp.bfloat16),
        preferred_element_type=jnp.float32,
    ).astype(jnp.int32)
    o_owner, slot = looked_up[0:1, :], looked_up[1:2, :]
    w_ids = task_ref[1:2, :]
    w_owner, w_local = w_ids // int_dev, w_ids % int_dev
    lam_local = task_ref[0:1, :] % lam_dev
    peer = lax.broadcasted_iota(jnp.int32, (peers, task_dev), 0)
    hits_o = peer == o_owner
    wanted = jnp.where(peer == w_owner, w_local * res_tile, 0) + jnp.where(hits_o, slot, 0)
    wanted = jnp.sum(wanted, axis=1, keepdims=True)
    request_ref[...] = jnp.broadcast_to(wanted, (peers, task_dev)).reshape(request_ref.shape)

    kept = jnp.zeros((1, task_dev), jnp.int32)
    for tile in range(lam_dev):
        kept = jnp.where(lam_local == tile, mask_ref[tile], kept)
    live = lax.broadcasted_iota(jnp.int32, (1, task_dev), 1) < live_ref[0]
    variant = jnp.where((kept == 1) & live, lam_local + lam_dev * task_ref[3:4, :], 2 * lam_dev)
    rows = jnp.concatenate([variant, w_owner, jnp.zeros((6, task_dev), jnp.int32)], axis=0)
    by_owner = lax.dot_general(
        rows.astype(jnp.float32).astype(jnp.bfloat16),
        jnp.where(hits_o, 1.0, 0.0).astype(jnp.bfloat16),
        (((1,), (1,)), ((), ())),
        preferred_element_type=jnp.float32,
    ).astype(jnp.int32)
    code_ref[...] = by_owner[0:1, :] * peers + by_owner[1:2, :]


def pick(request_ref, tiles_ref, out_ref, asked_ref, asked, sem, res_tile):
    peers = out_ref.shape[0]
    got = request_ref[...].reshape(peers, peers)
    diagonal = lax.broadcasted_iota(jnp.int32, got.shape, 0) == lax.broadcasted_iota(jnp.int32, got.shape, 1)
    asked_ref[...] = jnp.sum(jnp.where(diagonal, got, 0), axis=0, keepdims=True)
    copy = pltpu.make_async_copy(asked_ref, asked, sem)
    copy.start()
    copy.wait()

    def body(step, carry):
        for k in range(8):
            peer = step * 8 + k
            out_ref[peer] = tiles_ref[asked[0, peer] // res_tile]
        return carry

    lax.fori_loop(0, peers // 8, body, 0)


def contract(*refs):
    *code_refs, lam_ref, w_ref, out_ref = refs
    peers, rows, edge = w_ref.shape
    unroll = 32

    def one(owner):
        codes = [ref[0, owner] for ref in code_refs]
        left = [w_ref[code % peers] for code in codes]
        right = [lam_ref[code // peers] for code in codes]
        total = jnp.dot(
            jnp.concatenate(left, axis=1),
            jnp.concatenate(right, axis=0),
            preferred_element_type=jnp.float32,
        )
        top = jnp.max(jnp.abs(total), axis=0, keepdims=True)
        scale = jnp.ceil(jnp.log2(jnp.maximum(top, SMALLEST)) * OCTAVE)
        whole = jnp.round(total * (jnp.exp2(scale * (-1.0 / OCTAVE)) * FULL))
        scales = jnp.broadcast_to(scale, (out_ref.shape[1] - rows, edge))
        out_ref[owner] = jnp.concatenate([whole, scales], axis=0).astype(jnp.int32).astype(jnp.int16)

    def body(step, carry):
        for k in range(unroll):
            one(step * unroll + k)
        return carry

    lax.fori_loop(0, peers // unroll, body, 0)


def add_slots(request_ref, x_ref, out_ref, sums):
    slots, rows, _ = out_ref.shape
    sums[...] = jnp.zeros_like(sums)

    def body(step, carry):
        for k in range(4):
            peer = step * 4 + k
            value = x_ref[peer].astype(jnp.int32).astype(jnp.float32)
            scale = jnp.exp2(value[rows:rows + 1] * (1.0 / OCTAVE)) * (1.0 / FULL)
            sums[request_ref[0, peer] % slots] += value[:rows] * scale
        return carry

    lax.fori_loop(0, x_ref.shape[0] // 4, body, 0)
    out_ref[...] = sums[...].astype(out_ref.dtype)


def on_device(lam_tiles, int_tiles, task_list, live_count, tile_mask, owner_map):
    tile_devs = lax.axis_size("tiles")
    reps = lax.axis_size("rep")
    rep_index = lax.axis_index("rep")
    lam_dev, edge, _ = lam_tiles.shape
    int_dev = int_tiles.shape[0]
    res_tile = owner_map.shape[0] // tile_devs
    rows = edge // reps

    request, code = pl.pallas_call(
        functools.partial(read_tasks, int_dev=int_dev, res_tile=res_tile),
        out_shape=(
            jax.ShapeDtypeStruct((tile_devs, 1, 128), jnp.int32),
            jax.ShapeDtypeStruct((1, tile_devs), jnp.int32),
        ),
        in_specs=[SMEM, SMEM, VMEM, VMEM],
        out_specs=(VMEM, VMEM),
        name="read_tasks",
    )(live_count, tile_mask, task_list.T, owner_map[None, :])
    request = lax.all_to_all(request, "tiles", split_axis=0, concat_axis=0, tiled=True)
    codes = [code] + [ring(code, k) for k in range(1, reps)]

    lam_all = pl.pallas_call(
        prepare_lambda,
        out_shape=jax.ShapeDtypeStruct((2 * lam_dev + 1, edge, edge), jnp.bfloat16),
        in_specs=[VMEM],
        out_specs=VMEM,
        name="prepare_lambda",
    )(lam_tiles)
    columns = pl.pallas_call(
        prepare_integrals,
        out_shape=jax.ShapeDtypeStruct((int_dev, rows, edge), jnp.bfloat16),
        in_specs=[SMEM, VMEM],
        out_specs=VMEM,
        scratch_shapes=[pltpu.VMEM((int_dev, edge, edge), jnp.bfloat16)],
        name="prepare_integrals",
    )((rep_index * rows).reshape(1), int_tiles)
    picked, asked = pl.pallas_call(
        functools.partial(pick, res_tile=res_tile),
        out_shape=(
            jax.ShapeDtypeStruct((tile_devs, rows, edge), jnp.bfloat16),
            jax.ShapeDtypeStruct((1, tile_devs), jnp.int32),
        ),
        in_specs=[VMEM, VMEM],
        out_specs=(VMEM, VMEM),
        scratch_shapes=[pltpu.SMEM((1, tile_devs), jnp.int32), pltpu.SemaphoreType.DMA],
        name="pick",
    )(request, columns)
    fetched = lax.all_to_all(picked, "tiles", split_axis=0, concat_axis=0, tiled=True)

    totals = pl.pallas_call(
        contract,
        out_shape=jax.ShapeDtypeStruct((tile_devs, rows + 8, edge), jnp.int16),
        in_specs=[SMEM] * reps + [VMEM, VMEM],
        out_specs=VMEM,
        name="contract",
    )(*codes, lam_all, fetched)
    partial_tiles = lax.all_to_all(totals, "tiles", split_axis=0, concat_axis=0, tiled=True)
    summed = pl.pallas_call(
        add_slots,
        out_shape=jax.ShapeDtypeStruct((res_tile, rows, edge), jnp.bfloat16),
        in_specs=[SMEM, VMEM],
        out_specs=VMEM,
        scratch_shapes=[pltpu.VMEM((res_tile, rows, edge), jnp.float32)],
        name="add_slots",
    )(asked, partial_tiles)
    mine = lax.all_to_all(summed, "rep", split_axis=0, concat_axis=0, tiled=True)
    return mine.reshape(edge, edge).T[None]


def solution(mesh):
    placed = (
        P("tiles", None, None),
        P("tiles", None, None),
        P(("tiles", "rep"), None),
        P(("tiles", "rep")),
        P("tiles"),
        P(),
    )
    return jax.shard_map(
        on_device,
        mesh=mesh,
        in_specs=placed,
        out_specs=P(("tiles", "rep"), None, None),
        check_vma=False,
    )
```

time: 160 us -> 138 us (0.86)
  blocking collectives: 68.4 us -> 51.7 us
  other arithmetic: 6.88 us -> 0 us
    all_to_all x1, blocking collectives: 60.1 us -> 43.4 us  [on_device(): lax.all_to_all(totals, 'tiles', split_axis=0, concat_axis=0, tiled=True)]
    all_to_all x1 -> x0, other arithmetic: 2.35 us -> none  [on_device(): lax.all_to_all(request.reshape(tile_devs, 1, 1), 'tiles', split_axis=0, c...]
    reduce_sum x3 -> x0, other arithmetic: 1.76 us -> none  [the longest x1 0.85 us: on_device(): places = jnp.sum(jnp.where(matches, owner_map[None, :], 0), axis=1)]
    broadcast_in_dim x2 -> x0, other arithmetic: 1.61 us -> none  [the longest x1 0.81 us: on_device(): jnp.where(hits_w, (task_list[:, 1] % int_dev)[:, None], 0)]
    pallas_call x2 -> x3, Pallas kernels: 11.7 us -> 12.2 us  [the longest x1 7.26 us: on_device(): pl.pallas_call(contract, out_shape=jax.ShapeDtypeStruct((tile_devs, rows...]
where the time goes in v2:
time: 138 us; the launch traced here: 136 us
  blocking collectives  51.7 us (37%)
  starting transfers between devices  33.5 us (24%)
  waiting for transfers between devices  28.3 us (21%)
  Pallas kernels  19.1 us (14%)
  local copies, waits for them, and re-layouts  2.34 us (2%)
    all_to_all x1, blocking collectives, on_device(): lax.all_to_all(totals, 'tiles', split_axis=0, concat_axis=0, tiled=True)  43.4 us
    all_to_all x1, starting transfers between devices, on_device(): lax.all_to_all(request, 'tiles', split_axis=0, concat_axis=0, tiled=True)  18.4 us
    all_to_all x1, waiting for transfers between devices, on_device(): lax.all_to_all(picked, 'tiles', split_axis=0, concat_axis=0, tiled=True)  17.8 us
    all_to_all x1, waiting for transfers between devices, on_device(): lax.all_to_all(request, 'tiles', split_axis=0, concat_axis=0, tiled=True)  9.51 us
    ppermute x3, starting transfers between devices, ring(): lax.ppermute(values, 'rep', [(i, (i + steps) % reps) for i in range(reps)])  9.33 us
    all_to_all x1, blocking collectives, on_device(): lax.all_to_all(summed, 'rep', split_axis=0, concat_axis=0, tiled=True)  8.25 us
    pallas_call x1, Pallas kernels, on_device(): pl.pallas_call(contract, out_shape=jax.ShapeDtypeStruct((tile_devs, rows...  7.26 us
    all_to_all x1, starting transfers between devices, on_device(): lax.all_to_all(picked, 'tiles', split_axis=0, concat_axis=0, tiled=True)  5.77 us
  transfers between devices with their start and end apart: 5, of which 3 were waited for; matrix products, arithmetic and copies ran while one was open for 0% of the time, Pallas kernels for 3%

profile of v2, /device:TPU:1, one launch (start us, length us, event | category | flops | bytes accessed | tf_op | source)
XLA Modules:
  0.0 135.7 jit_solution(531047231903327906)
XLA Ops:
  0.7 1.6 %read_tasks.1 = (s32[128,1,128]{2,1,0:T(1,128)}, s32[1,128]{1,0:T(1,128)}) custom-call(s32[1]{0:T(128)S(6)} %copy.8.live_ref, s32[16]{0:T(128)} %mask_ref.1, s32[4,128]{1,0:T(4,128)} %bitcast.8, s32[1,512]{1,0:T(1,128)} %bitcast.9), custom_call_target="tpu_custom_call" | custom-call | tf_op jit(solution)/shard_map/read_tasks/pallas_call | solution.py:149
  2.3 18.4 %all-to-all-start = ((s32[128,1,128]{2,1,0:T(1,128)}), s32[128,1,128]{2,1,0:T(1,128)S(1)}, u32[]{:S(2)}, u32[]{:S(2)}) async-start(s32[128,1,128]{2,1,0:T(1,128)} %get-tuple-element.9), calls=%async_computation | async-start | bytes 131072 | tf_op jit(solution)/shard_map/all_to_all | solution.py:159
  20.7 1.9 %prepare_integrals.1.tiles_ref = bf16[16,32,128]{2,1,0:T(8,128)(2,1)} custom-call(s32[1]{0:T(128)} %bitcast.2.start_ref, bf16[16,128,128]{2,1,0:T(8,128)(2,1)} %int_ref.1), custom_call_target="tpu_custom_call" | custom-call | tf_op jit(solution)/shard_map/prepare_integrals/pallas_call | solution.py:169
  22.6 0.0 copy-start.2
  22.6 9.5 %all-to-all-done.request_ref = s32[128,1,128]{2,1,0:T(1,128)S(1)} async-done(((s32[128,1,128]{2,1,0:T(1,128)}), s32[128,1,128]{2,1,0:T(1,128)S(1)}, u32[]{:S(2)}, u32[]{:S(2)}) %all-to-all-start) | async-done | bytes 65568 | tf_op jit(solution)/shard_map/all_to_all | solution.py:159
  32.1 0.0 copy-start.1
  32.1 0.6 copy-done.1
  32.8 3.3 %pick.1 = (bf16[128,32,128]{2,1,0:T(8,128)(2,1)}, s32[1,128]{1,0:T(1,128)}) custom-call(s32[128,1,128]{2,1,0:T(1,128)} %copy-done.1, bf16[16,32,128]{2,1,0:T(8,128)(2,1)} %prepare_integrals.1.tiles_ref), custom_call_target="tpu_custom_call" | custom-call | tf_op jit(solution)/shard_map/pick/pallas_call | solution.py:177
  36.0 5.8 %all-to-all-start.1 = ((bf16[128,32,128]{2,1,0:T(8,128)(2,1)}), bf16[128,32,128]{2,1,0:T(8,128)(2,1)S(1)}, u32[]{:S(2)}, u32[]{:S(2)}) async-start(bf16[128,32,128]{2,1,0:T(8,128)(2,1)} %get-tuple-element.12), calls=%async_computation.1 | async-start | bytes 2097152 | tf_op jit(solution)/shard_map/all_to_all | solution.py:188
  41.8 0.0 copy-done.2
  41.8 4.4 %collective-permute-start.2 = (s32[1,128]{1,0:T(1,128)S(1)}, s32[1,128]{1,0:T(1,128)S(1)}, u32[]{:S(2)}, u32[]{:S(2)}) collective-permute-start(s32[1,128]{1,0:T(1,128)S(1)} %copy-done.2), channel_id=1, source_target_pairs={{0,3},{1,0},{2,1},{3,2},{4,7},{5,4},{6,5},{7,6},{8,11},{9,8},{10,9... | collective-permute-start | bytes 1544 | tf_op jit(solution)/shard_map/ppermute | solution.py:19
  46.2 2.4 %collective-permute-start.1 = (s32[1,128]{1,0:T(1,128)S(1)}, s32[1,128]{1,0:T(1,128)S(1)}, u32[]{:S(2)}, u32[]{:S(2)}) collective-permute-start(s32[1,128]{1,0:T(1,128)S(1)} %copy-done.2), channel_id=1, source_target_pairs={{0,2},{1,3},{2,0},{3,1},{4,6},{5,7},{6,4},{7,5},{8,10},{9,11},{10,... | collective-permute-start | bytes 1544 | tf_op jit(solution)/shard_map/ppermute | solution.py:19
  48.7 2.5 %collective-permute-start = (s32[1,128]{1,0:T(1,128)S(1)}, s32[1,128]{1,0:T(1,128)S(1)}, u32[]{:S(2)}, u32[]{:S(2)}) collective-permute-start(s32[1,128]{1,0:T(1,128)S(1)} %copy-done.2), channel_id=1, source_target_pairs={{0,1},{1,2},{2,3},{3,0},{4,5},{5,6},{6,7},{7,4},{8,9},{9,10},{10,1... | collective-permute-start | bytes 1544 | tf_op jit(solution)/shard_map/ppermute | solution.py:19
  51.2 2.2 %prepare_lambda.1.refs_4_ = bf16[33,128,128]{2,1,0:T(8,128)(2,1)} custom-call(bf16[16,128,128]{2,1,0:T(8,128)(2,1)} %lam_ref.1), custom_call_target="tpu_custom_call" | custom-call | tf_op jit(solution)/shard_map/prepare_lambda/pallas_call | solution.py:162
  53.4 0.0 collective-permute-done.2.refs_3_
  53.4 0.0 copy-start.3
  53.4 0.0 collective-permute-done.1.refs_2_
  53.4 0.0 copy-start.4
  53.4 1.0 collective-permute-done.refs_1_
  54.4 0.0 copy-start.5
  54.5 17.8 %all-to-all-done.1.refs_5_ = bf16[128,32,128]{2,1,0:T(8,128)(2,1)S(1)} async-done(((bf16[128,32,128]{2,1,0:T(8,128)(2,1)}), bf16[128,32,128]{2,1,0:T(8,128)(2,1)S(1)}, u32[]{:S(2)}, u32[]{:S(2)}) %all-to-all-start.1) | async-done | bytes 1048608 | tf_op jit(solution)/shard_map/all_to_all | solution.py:188
  72.2 0.0 copy-done.3
  72.2 0.0 copy-done.4
  72.2 0.0 copy-done.5
  72.2 0.0 copy-start
  72.2 1.0 copy-done
  73.2 7.3 %contract.1 = s16[128,40,128]{2,1,0:T(8,128)(2,1)} custom-call(s32[1,128]{1,0:T(1,128)} %get-tuple-element.11.refs_0_, s32[1,128]{1,0:T(1,128)} %copy-done.5, s32[1,128]{1,0:T(1,128)} %copy-done.4, s32[1,128]{1,0:T(1,128)} %copy-done.3, bf16[33,128,128]{2,1,0:T(8,128)(2,1)} %prepare_lambda.1.refs_4_, bf16[128,32,128]{2,1,0:T(8,128)(2,1)} %copy-done), custom_call_target="tpu_custom_call" | custom-call | tf_op jit(solution)/shard_map/contract/pallas_call | solution.py:190
  80.5 43.4 %all_to_all.20.x_ref = s16[128,40,128]{2,1,0:T(8,128)(2,1)} all-to-all(s16[128,40,128]{2,1,0:T(8,128)(2,1)} %contract.1), channel_id=1, replica_groups=mesh['tiles'=128,'rep'=4] {'tiles'}, dimensions={0} | all-to-all | bytes 2621440 | tf_op jit(solution)/shard_map/all_to_all | solution.py:197
  123.9 2.8 %add_slots.1 = bf16[4,32,128]{2,1,0:T(8,128)(2,1)} custom-call(s32[1,128]{1,0:T(1,128)} %get-tuple-element.10.request_ref, s16[128,40,128]{2,1,0:T(8,128)(2,1)} %all_to_all.20.x_ref), custom_call_target="tpu_custom_call" | custom-call | tf_op jit(solution)/shard_map/add_slots/pallas_call | solution.py:198
  126.8 8.3 %all_to_all.21 = bf16[4,32,128]{2,1,0:T(8,128)(2,1)S(1)} all-to-all(bf16[4,32,128]{2,1,0:T(8,128)(2,1)} %add_slots.1), channel_id=1, replica_groups=mesh['tiles'=128,'rep'=4] {'rep'}, dimensions={0} | all-to-all | bytes 65536 | tf_op jit(solution)/shard_map/all_to_all | solution.py:206
  135.0 0.7 copy.7
Async XLA Ops:
  2.3 29.8 %all-to-all-start = ((s32[128,1,128]{2,1,0:T(1,128)}), s32[128,1,128]{2,1,0:T(1,128)S(1)}, u32[]{:S(2)}, u32[]{:S(2)}) async-start(s32[128,1,128]{2,1,0:T(1,128)} %get-tuple-element.9), calls=%async_computation | async-start | bytes 131072 | tf_op jit(solution)/shard_map/all_to_all | solution.py:159
  22.6 19.2 %copy-start.2 = (s32[1,128]{1,0:T(1,128)S(1)}, s32[1,128]{1,0:T(1,128)}, u32[]{:S(2)}) copy-start(s32[1,128]{1,0:T(1,128)} %get-tuple-element.11.refs_0_) | copy-start | bytes 1540
  32.1 0.6 copy-start.1
  36.0 36.2 %all-to-all-start.1 = ((bf16[128,32,128]{2,1,0:T(8,128)(2,1)}), bf16[128,32,128]{2,1,0:T(8,128)(2,1)S(1)}, u32[]{:S(2)}, u32[]{:S(2)}) async-start(bf16[128,32,128]{2,1,0:T(8,128)(2,1)} %get-tuple-element.12), calls=%async_computation.1 | async-start | bytes 2097152 | tf_op jit(solution)/shard_map/all_to_all | solution.py:188
  41.8 11.6 %collective-permute-start.2 = (s32[1,128]{1,0:T(1,128)S(1)}, s32[1,128]{1,0:T(1,128)S(1)}, u32[]{:S(2)}, u32[]{:S(2)}) collective-permute-start(s32[1,128]{1,0:T(1,128)S(1)} %copy-done.2), channel_id=1, source_target_pairs={{0,3},{1,0},{2,1},{3,2},{4,7},{5,4},{6,5},{7,6},{8,11},{9,8},{10,9... | collective-permute-start | bytes 1544 | tf_op jit(solution)/shard_map/ppermute | solution.py:19
  46.2 7.2 %collective-permute-start.1 = (s32[1,128]{1,0:T(1,128)S(1)}, s32[1,128]{1,0:T(1,128)S(1)}, u32[]{:S(2)}, u32[]{:S(2)}) collective-permute-start(s32[1,128]{1,0:T(1,128)S(1)} %copy-done.2), channel_id=1, source_target_pairs={{0,2},{1,3},{2,0},{3,1},{4,6},{5,7},{6,4},{7,5},{8,10},{9,11},{10,... | collective-permute-start | bytes 1544 | tf_op jit(solution)/shard_map/ppermute | solution.py:19
  48.7 5.8 %collective-permute-start = (s32[1,128]{1,0:T(1,128)S(1)}, s32[1,128]{1,0:T(1,128)S(1)}, u32[]{:S(2)}, u32[]{:S(2)}) collective-permute-start(s32[1,128]{1,0:T(1,128)S(1)} %copy-done.2), channel_id=1, source_target_pairs={{0,1},{1,2},{2,3},{3,0},{4,5},{5,6},{6,7},{7,4},{8,9},{9,10},{10,1... | collective-permute-start | bytes 1544 | tf_op jit(solution)/shard_map/ppermute | solution.py:19
  53.4 18.8 %copy-start.3 = (s32[1,128]{1,0:T(1,128)}, s32[1,128]{1,0:T(1,128)S(1)}, u32[]{:S(2)}) copy-start(s32[1,128]{1,0:T(1,128)S(1)} %collective-permute-done.2.refs_3_) | copy-start | bytes 1540
  53.4 18.8 %copy-start.4 = (s32[1,128]{1,0:T(1,128)}, s32[1,128]{1,0:T(1,128)S(1)}, u32[]{:S(2)}) copy-start(s32[1,128]{1,0:T(1,128)S(1)} %collective-permute-done.1.refs_2_) | copy-start | bytes 1540
  54.4 17.8 %copy-start.5 = (s32[1,128]{1,0:T(1,128)}, s32[1,128]{1,0:T(1,128)S(1)}, u32[]{:S(2)}) copy-start(s32[1,128]{1,0:T(1,128)S(1)} %collective-permute-done.refs_1_) | copy-start | bytes 1540
  72.2 1.0 copy-start

commit v3 on v2

--- a/solution.py
+++ b/solution.py
@@ -11,6 +11,7 @@
 OCTAVE = 256.0
 FULL = 32760.0
 SMALLEST = 2.0**-120
+ROOM = pltpu.CompilerParams(vmem_limit_bytes=8 * 2**20)
 SMEM = pl.BlockSpec(memory_space=pltpu.SMEM)
 
 
@@ -96,9 +97,11 @@
 def contract(*refs):
     *code_refs, lam_ref, w_ref, out_ref = refs
     peers, rows, edge = w_ref.shape
-    unroll = 32
-
-    def one(owner):
+    unroll = 64
+    words = rows // 2 + 1
+
+    def one(step, place):
+        owner = step * unroll + place
         codes = [ref[0, owner] for ref in code_refs]
         left = [w_ref[code % peers] for code in codes]
         right = [lam_ref[code // peers] for code in codes]
@@ -109,13 +112,14 @@
         )
         top = jnp.max(jnp.abs(total), axis=0, keepdims=True)
         scale = jnp.ceil(jnp.log2(jnp.maximum(top, SMALLEST)) * OCTAVE)
-        whole = jnp.round(total * (jnp.exp2(scale * (-1.0 / OCTAVE)) * FULL))
-        scales = jnp.broadcast_to(scale, (out_ref.shape[1] - rows, edge))
-        out_ref[owner] = jnp.concatenate([whole, scales], axis=0).astype(jnp.int32).astype(jnp.int16)
+        whole = jnp.round(total * (jnp.exp2(scale * (-1.0 / OCTAVE)) * FULL)).astype(jnp.int32)
+        first = pl.multiple_of(step * unroll * words, 8) + place * words
+        out_ref[pl.ds(first, rows // 2), :] = whole[: rows // 2] * 65536 + whole[rows // 2 :]
+        out_ref[pl.ds(first + rows // 2, 1), :] = scale.astype(jnp.int32)
 
     def body(step, carry):
         for k in range(unroll):
-            one(step * unroll + k)
+            one(step, k)
         return carry
 
     lax.fori_loop(0, peers // unroll, body, 0)
@@ -123,17 +127,23 @@
 
 def add_slots(request_ref, x_ref, out_ref, sums):
     slots, rows, _ = out_ref.shape
+    words = rows // 2 + 1
+    unroll = 8
     sums[...] = jnp.zeros_like(sums)
 
     def body(step, carry):
-        for k in range(4):
-            peer = step * 4 + k
-            value = x_ref[peer].astype(jnp.int32).astype(jnp.float32)
-            scale = jnp.exp2(value[rows:rows + 1] * (1.0 / OCTAVE)) * (1.0 / FULL)
-            sums[request_ref[0, peer] % slots] += value[:rows] * scale
+        for k in range(unroll):
+            first = pl.multiple_of(step * unroll * words, 8) + k * words
+            pairs = x_ref[pl.ds(first, rows // 2), :]
+            low = lax.shift_right_arithmetic(lax.shift_left(pairs, 16), 16)
+            high = lax.shift_right_arithmetic(pairs - low, 16)
+            scale = x_ref[pl.ds(first + rows // 2, 1), :].astype(jnp.float32)
+            scale = jnp.exp2(scale * (1.0 / OCTAVE)) * (1.0 / FULL)
+            value = jnp.concatenate([high, low], axis=0).astype(jnp.float32) * scale
+            sums[request_ref[0, step * unroll + k] % slots] += value
         return carry
 
-    lax.fori_loop(0, x_ref.shape[0] // 4, body, 0)
+    lax.fori_loop(0, request_ref.shape[1] // unroll, body, 0)
     out_ref[...] = sums[...].astype(out_ref.dtype)
 
 
@@ -145,6 +155,7 @@
     int_dev = int_tiles.shape[0]
     res_tile = owner_map.shape[0] // tile_devs
     rows = edge // reps
+    words = rows // 2 + 1
 
     request, code = pl.pallas_call(
         functools.partial(read_tasks, int_dev=int_dev, res_tile=res_tile),
@@ -164,6 +175,7 @@
         out_shape=jax.ShapeDtypeStruct((2 * lam_dev + 1, edge, edge), jnp.bfloat16),
         in_specs=[VMEM],
         out_specs=VMEM,
+        compiler_params=ROOM,
         name="prepare_lambda",
     )(lam_tiles)
     columns = pl.pallas_call(
@@ -172,6 +184,7 @@
         in_specs=[SMEM, VMEM],
         out_specs=VMEM,
         scratch_shapes=[pltpu.VMEM((int_dev, edge, edge), jnp.bfloat16)],
+        compiler_params=ROOM,
         name="prepare_integrals",
     )((rep_index * rows).reshape(1), int_tiles)
     picked, asked = pl.pallas_call(
@@ -183,24 +196,29 @@
         in_specs=[VMEM, VMEM],
         out_specs=(VMEM, VMEM),
         scratch_shapes=[pltpu.SMEM((1, tile_devs), jnp.int32), pltpu.SemaphoreType.DMA],
+        compiler_params=ROOM,
         name="pick",
     )(request, columns)
     fetched = lax.all_to_all(picked, "tiles", split_axis=0, concat_axis=0, tiled=True)
 
     totals = pl.pallas_call(
         contract,
-        out_shape=jax.ShapeDtypeStruct((tile_devs, rows + 8, edge), jnp.int16),
+        out_shape=jax.ShapeDtypeStruct((tile_devs * words, edge), jnp.int32),
         in_specs=[SMEM] * reps + [VMEM, VMEM],
         out_specs=VMEM,
+        compiler_params=ROOM,
         name="contract",
     )(*codes, lam_all, fetched)
+    totals = totals.reshape(tile_devs, words, 1, edge)
     partial_tiles = lax.all_to_all(totals, "tiles", split_axis=0, concat_axis=0, tiled=True)
+    partial_tiles = partial_tiles.reshape(tile_devs * words, edge)
     summed = pl.pallas_call(
         add_slots,
         out_shape=jax.ShapeDtypeStruct((res_tile, rows, edge), jnp.bfloat16),
         in_specs=[SMEM, VMEM],
         out_specs=VMEM,
         scratch_shapes=[pltpu.VMEM((res_tile, rows, edge), jnp.float32)],
+        compiler_params=ROOM,
         name="add_slots",
     )(asked, partial_tiles)
     mine = lax.all_to_all(summed, "rep", split_axis=0, concat_axis=0, tiled=True)

time: 138 us -> 127 us (0.920)
  Pallas kernels: 19.1 us -> 10.9 us
  blocking collectives: 51.7 us -> 46.6 us
  waiting for transfers between devices: 28.3 us -> 31.1 us
    all_to_all x1, blocking collectives: 43.4 us -> 38.5 us  [on_device(): lax.all_to_all(totals, 'tiles', split_axis=0, concat_axis=0, tiled=True)]
    pallas_call x1, Pallas kernels: 7.26 us -> 5.19 us  [on_device(): pl.pallas_call(contract, out_shape=jax.ShapeDtypeStruct((tile_devs * word...]
    pallas_call x1, Pallas kernels: 2.22 us -> 0.19 us  [on_device(): pl.pallas_call(prepare_lambda, out_shape=jax.ShapeDtypeStruct((2 * lam_de...]
    ppermute x3, waiting for transfers between devices: 1.03 us -> 3.05 us  [ring(): lax.ppermute(values, 'rep', [(i, (i + steps) % reps) for i in range(reps)])]
    pallas_call x1, Pallas kernels: 1.9 us -> 0.2 us  [on_device(): pl.pallas_call(prepare_integrals, out_shape=jax.ShapeDtypeStruct((int_dev...]
    pallas_call x1, Pallas kernels: 2.85 us -> 1.36 us  [on_device(): pl.pallas_call(add_slots, out_shape=jax.ShapeDtypeStruct((res_tile, rows,...]
  transfers between devices with their start and end apart: 5 -> 5, of which waited for: 3 -> 4; matrix products, arithmetic and copies ran while one was open for 0% -> 0% of each run, Pallas kernels for 3% -> 0%
where the time goes in v3:
time: 127 us; the launch traced here: 125 us
  blocking collectives  46.6 us (37%)
  starting transfers between devices  33.5 us (26%)
  waiting for transfers between devices  31.1 us (24%)
  Pallas kernels  10.9 us (9%)
  local copies, waits for them, and re-layouts  1.77 us (1%)
    all_to_all x1, blocking collectives, on_device(): lax.all_to_all(totals, 'tiles', split_axis=0, concat_axis=0, tiled=True)  38.5 us
    all_to_all x1, starting transfers between devices, on_device(): lax.all_to_all(request, 'tiles', split_axis=0, concat_axis=0, tiled=True)  18.4 us
    all_to_all x1, waiting for transfers between devices, on_device(): lax.all_to_all(picked, 'tiles', split_axis=0, concat_axis=0, tiled=True)  17.8 us
    all_to_all x1, waiting for transfers between devices, on_device(): lax.all_to_all(request, 'tiles', split_axis=0, concat_axis=0, tiled=True)  10.3 us
    ppermute x3, starting transfers between devices, ring(): lax.ppermute(values, 'rep', [(i, (i + steps) % reps) for i in range(reps)])  9.33 us
    all_to_all x1, blocking collectives, on_device(): lax.all_to_all(summed, 'rep', split_axis=0, concat_axis=0, tiled=True)  8.12 us
    all_to_all x1, starting transfers between devices, on_device(): lax.all_to_all(picked, 'tiles', split_axis=0, concat_axis=0, tiled=True)  5.73 us
    pallas_call x1, Pallas kernels, on_device(): pl.pallas_call(contract, out_shape=jax.ShapeDtypeStruct((tile_devs * word...  5.19 us
  transfers between devices with their start and end apart: 5, of which 4 were waited for; matrix products, arithmetic and copies ran while one was open for 0% of the time, Pallas kernels for 0%

profile of v3, /device:TPU:1, one launch (start us, length us, event | category | flops | bytes accessed | tf_op | source)
XLA Modules:
  0.0 124.7 jit_solution(5919868527957337277)
XLA Ops:
  0.7 1.6 %read_tasks.1 = (s32[128,1,128]{2,1,0:T(1,128)}, s32[1,128]{1,0:T(1,128)}) custom-call(s32[1]{0:T(128)S(6)} %copy.11.live_ref, s32[16]{0:T(128)} %mask_ref.1, s32[4,128]{1,0:T(4,128)} %bitcast.12, s32[1,512]{1,0:T(1,128)} %bitcast.13), custom_call_target="tpu_custom_call" | custom-call | tf_op jit(solution)/shard_map/read_tasks/pallas_call | solution.py:160
  2.3 18.4 %all-to-all-start = ((s32[128,1,128]{2,1,0:T(1,128)}), s32[128,1,128]{2,1,0:T(1,128)S(1)}, u32[]{:S(2)}, u32[]{:S(2)}) async-start(s32[128,1,128]{2,1,0:T(1,128)} %get-tuple-element.9), calls=%async_computation | async-start | bytes 131072 | tf_op jit(solution)/shard_map/all_to_all | solution.py:170
  20.7 0.0 copy-start.1
  20.7 1.0 copy-done.1
  21.8 0.2 prepare_integrals.1.tiles_ref
  22.0 0.0 copy-start.2
  22.0 0.0 copy-start
  22.0 10.3 %all-to-all-done.request_ref = s32[128,1,128]{2,1,0:T(1,128)S(1)} async-done(((s32[128,1,128]{2,1,0:T(1,128)}), s32[128,1,128]{2,1,0:T(1,128)S(1)}, u32[]{:S(2)}, u32[]{:S(2)}) %all-to-all-start) | async-done | bytes 65568 | tf_op jit(solution)/shard_map/all_to_all | solution.py:170
  32.3 2.4 %pick.1 = (bf16[128,32,128]{2,1,0:T(8,128)(2,1)}, s32[1,128]{1,0:T(1,128)S(1)}) custom-call(s32[128,1,128]{2,1,0:T(1,128)S(1)} %all-to-all-done.request_ref, bf16[16,32,128]{2,1,0:T(8,128)(2,1)S(1)} %prepare_integrals.1.tiles_ref), custom_call_target="tpu_custom_call" | custom-call | tf_op jit(solution)/shard_map/pick/pallas_call | solution.py:190
  34.6 5.7 %all-to-all-start.1 = ((bf16[128,32,128]{2,1,0:T(8,128)(2,1)}), bf16[128,32,128]{2,1,0:T(8,128)(2,1)S(1)}, u32[]{:S(2)}, u32[]{:S(2)}) async-start(bf16[128,32,128]{2,1,0:T(8,128)(2,1)} %get-tuple-element.12), calls=%async_computation.1 | async-start | bytes 2097152 | tf_op jit(solution)/shard_map/all_to_all | solution.py:202
  40.4 0.0 copy-done.2
  40.4 4.4 %collective-permute-start.2 = (s32[1,128]{1,0:T(1,128)S(1)}, s32[1,128]{1,0:T(1,128)S(1)}, u32[]{:S(2)}, u32[]{:S(2)}) collective-permute-start(s32[1,128]{1,0:T(1,128)S(1)} %copy-done.2), channel_id=1, source_target_pairs={{0,3},{1,0},{2,1},{3,2},{4,7},{5,4},{6,5},{7,6},{8,11},{9,8},{10,9... | collective-permute-start | bytes 1544 | tf_op jit(solution)/shard_map/ppermute | solution.py:20
  44.8 2.4 %collective-permute-start.1 = (s32[1,128]{1,0:T(1,128)S(1)}, s32[1,128]{1,0:T(1,128)S(1)}, u32[]{:S(2)}, u32[]{:S(2)}) collective-permute-start(s32[1,128]{1,0:T(1,128)S(1)} %copy-done.2), channel_id=1, source_target_pairs={{0,2},{1,3},{2,0},{3,1},{4,6},{5,7},{6,4},{7,5},{8,10},{9,11},{10,... | collective-permute-start | bytes 1544 | tf_op jit(solution)/shard_map/ppermute | solution.py:20
  47.2 2.5 %collective-permute-start = (s32[1,128]{1,0:T(1,128)S(1)}, s32[1,128]{1,0:T(1,128)S(1)}, u32[]{:S(2)}, u32[]{:S(2)}) collective-permute-start(s32[1,128]{1,0:T(1,128)S(1)} %copy-done.2), channel_id=1, source_target_pairs={{0,1},{1,2},{2,3},{3,0},{4,5},{5,6},{6,7},{7,4},{8,9},{9,10},{10,1... | collective-permute-start | bytes 1544 | tf_op jit(solution)/shard_map/ppermute | solution.py:20
  49.7 0.0 copy-done
  49.7 0.2 prepare_lambda.1.refs_4_
  49.9 0.0 collective-permute-done.2.refs_3_
  49.9 0.9 collective-permute-done.1.refs_2_
  50.8 2.1 %collective-permute-done.refs_1_ = s32[1,128]{1,0:T(1,128)S(1)} collective-permute-done((s32[1,128]{1,0:T(1,128)S(1)}, s32[1,128]{1,0:T(1,128)S(1)}, u32[]{:S(2)}, u32[]{:S(2)}) %collective-permute-start) | collective-permute-done | bytes 544 | tf_op jit(solution)/shard_map/ppermute | solution.py:20
  53.0 17.8 %all-to-all-done.1.refs_5_ = bf16[128,32,128]{2,1,0:T(8,128)(2,1)S(1)} async-done(((bf16[128,32,128]{2,1,0:T(8,128)(2,1)}), bf16[128,32,128]{2,1,0:T(8,128)(2,1)S(1)}, u32[]{:S(2)}, u32[]{:S(2)}) %all-to-all-start.1) | async-done | bytes 1048608 | tf_op jit(solution)/shard_map/all_to_all | solution.py:202
  70.8 5.2 %contract.1 = s32[2176,128]{1,0:T(8,128)S(1)} custom-call(s32[1,128]{1,0:T(1,128)S(1)} %copy-done.2, s32[1,128]{1,0:T(1,128)S(1)} %collective-permute-done.refs_1_, s32[1,128]{1,0:T(1,128)S(1)} %collective-permute-done.1.refs_2_, s32[1,128]{1,0:T(1,128)S(1)} %collective-permute-done.2.refs_3_, bf16[33,128,128]{2,1,0:T(8,128)(2,1)S(1)} %prepare_lambda.1.refs_4_, ...), custom_call_target="tpu_custom_call" | custom-call | tf_op jit(solution)/shard_map/contract/pallas_call | solution.py:204
  76.0 38.5 %all_to_all.20 = s32[128,17,1,128]{3,2,1,0:T(1,128)S(1)} all-to-all(s32[128,17,1,128]{3,2,1,0:T(1,128)S(1)} %bitcast.9), channel_id=1, replica_groups=mesh['tiles'=128,'rep'=4] {'tiles'}, dimensions={0} | all-to-all | bytes 2228224 | tf_op jit(solution)/shard_map/all_to_all | solution.py:213
  114.5 1.4 %add_slots.1 = bf16[4,32,128]{2,1,0:T(8,128)(2,1)S(1)} custom-call(s32[1,128]{1,0:T(1,128)S(1)} %get-tuple-element.10.request_ref, s32[2176,128]{1,0:T(8,128)S(1)} %bitcast.10), custom_call_target="tpu_custom_call" | custom-call | tf_op jit(solution)/shard_map/add_slots/pallas_call | solution.py:215
  115.8 8.1 %all_to_all.21 = bf16[4,32,128]{2,1,0:T(8,128)(2,1)S(1)} all-to-all(bf16[4,32,128]{2,1,0:T(8,128)(2,1)S(1)} %add_slots.1), channel_id=1, replica_groups=mesh['tiles'=128,'rep'=4] {'rep'}, dimensions={0} | all-to-all | bytes 65536 | tf_op jit(solution)/shard_map/all_to_all | solution.py:224
  123.9 0.7 copy.10
Async XLA Ops:
  2.3 30.0 %all-to-all-start = ((s32[128,1,128]{2,1,0:T(1,128)}), s32[128,1,128]{2,1,0:T(1,128)S(1)}, u32[]{:S(2)}, u32[]{:S(2)}) async-start(s32[128,1,128]{2,1,0:T(1,128)} %get-tuple-element.9), calls=%async_computation | async-start | bytes 131072 | tf_op jit(solution)/shard_map/all_to_all | solution.py:170
  20.7 1.0 copy-start.1
  22.0 18.4 %copy-start.2 = (s32[1,128]{1,0:T(1,128)S(1)}, s32[1,128]{1,0:T(1,128)}, u32[]{:S(2)}) copy-start(s32[1,128]{1,0:T(1,128)} %get-tuple-element.11.refs_0_) | copy-start | bytes 1540
  22.0 27.8 %copy-start = (bf16[16,128,128]{2,1,0:T(8,128)(2,1)S(1)}, bf16[16,128,128]{2,1,0:T(8,128)(2,1)}, u32[]{:S(2)}) copy-start(bf16[16,128,128]{2,1,0:T(8,128)(2,1)} %lam_ref.1) | copy-start | bytes 1572868
  34.6 36.1 %all-to-all-start.1 = ((bf16[128,32,128]{2,1,0:T(8,128)(2,1)}), bf16[128,32,128]{2,1,0:T(8,128)(2,1)S(1)}, u32[]{:S(2)}, u32[]{:S(2)}) async-start(bf16[128,32,128]{2,1,0:T(8,128)(2,1)} %get-tuple-element.12), calls=%async_computation.1 | async-start | bytes 2097152 | tf_op jit(solution)/shard_map/all_to_all | solution.py:202
  40.4 9.6 %collective-permute-start.2 = (s32[1,128]{1,0:T(1,128)S(1)}, s32[1,128]{1,0:T(1,128)S(1)}, u32[]{:S(2)}, u32[]{:S(2)}) collective-permute-start(s32[1,128]{1,0:T(1,128)S(1)} %copy-done.2), channel_id=1, source_target_pairs={{0,3},{1,0},{2,1},{3,2},{4,7},{5,4},{6,5},{7,6},{8,11},{9,8},{10,9... | collective-permute-start | bytes 1544 | tf_op jit(solution)/shard_map/ppermute | solution.py:20
  44.8 6.1 %collective-permute-start.1 = (s32[1,128]{1,0:T(1,128)S(1)}, s32[1,128]{1,0:T(1,128)S(1)}, u32[]{:S(2)}, u32[]{:S(2)}) collective-permute-start(s32[1,128]{1,0:T(1,128)S(1)} %copy-done.2), channel_id=1, source_target_pairs={{0,2},{1,3},{2,0},{3,1},{4,6},{5,7},{6,4},{7,5},{8,10},{9,11},{10,... | collective-permute-start | bytes 1544 | tf_op jit(solution)/shard_map/ppermute | solution.py:20
  47.2 5.8 %collective-permute-start = (s32[1,128]{1,0:T(1,128)S(1)}, s32[1,128]{1,0:T(1,128)S(1)}, u32[]{:S(2)}, u32[]{:S(2)}) collective-permute-start(s32[1,128]{1,0:T(1,128)S(1)} %copy-done.2), channel_id=1, source_target_pairs={{0,1},{1,2},{2,3},{3,0},{4,5},{5,6},{6,7},{7,4},{8,9},{9,10},{10,1... | collective-permute-start | bytes 1544 | tf_op jit(solution)/shard_map/ppermute | solution.py:20

commit v4 on v3

--- a/solution.py
+++ b/solution.py
@@ -13,6 +13,10 @@
 SMALLEST = 2.0**-120
 ROOM = pltpu.CompilerParams(vmem_limit_bytes=8 * 2**20)
 SMEM = pl.BlockSpec(memory_space=pltpu.SMEM)
+
+
+def power(size):
+    return size.bit_length() - 1
 
 
 def ring(values, steps):
@@ -86,12 +90,12 @@
     copy.wait()
 
     def body(step, carry):
-        for k in range(8):
-            peer = step * 8 + k
-            out_ref[peer] = tiles_ref[asked[0, peer] // res_tile]
+        for k in range(32):
+            peer = step * 32 + k
+            out_ref[peer] = tiles_ref[lax.shift_right_logical(asked[0, peer], power(res_tile))]
         return carry
 
-    lax.fori_loop(0, peers // 8, body, 0)
+    lax.fori_loop(0, peers // 32, body, 0)
 
 
 def contract(*refs):
@@ -103,8 +107,8 @@
     def one(step, place):
         owner = step * unroll + place
         codes = [ref[0, owner] for ref in code_refs]
-        left = [w_ref[code % peers] for code in codes]
-        right = [lam_ref[code // peers] for code in codes]
+        left = [w_ref[lax.bitwise_and(code, peers - 1)] for code in codes]
+        right = [lam_ref[lax.shift_right_logical(code, power(peers))] for code in codes]
         total = jnp.dot(
             jnp.concatenate(left, axis=1),
             jnp.concatenate(right, axis=0),
@@ -140,7 +144,8 @@
             scale = x_ref[pl.ds(first + rows // 2, 1), :].astype(jnp.float32)
             scale = jnp.exp2(scale * (1.0 / OCTAVE)) * (1.0 / FULL)
             value = jnp.concatenate([high, low], axis=0).astype(jnp.float32) * scale
-            sums[request_ref[0, step * unroll + k] % slots] += value
+            slot = lax.bitwise_and(request_ref[0, step * unroll + k], slots - 1)
+            sums[slot] += value
         return carry
 
     lax.fori_loop(0, request_ref.shape[1] // unroll, body, 0)

time: 127 us -> 124 us (0.976)
  Pallas kernels: 10.9 us -> 8.71 us
    pallas_call x1, Pallas kernels: 5.19 us -> 3.58 us  [on_device(): pl.pallas_call(contract, out_shape=jax.ShapeDtypeStruct((tile_devs * word...]
where the time goes in v4:
time: 124 us; the launch traced here: 122 us
  blocking collectives  46.6 us (38%)
  starting transfers between devices  33.5 us (27%)
  waiting for transfers between devices  31.1 us (25%)
  Pallas kernels  8.71 us (7%)
  local copies, waits for them, and re-layouts  1.77 us (1%)
    all_to_all x1, blocking collectives, on_device(): lax.all_to_all(totals, 'tiles', split_axis=0, concat_axis=0, tiled=True)  38.5 us
    all_to_all x1, starting transfers between devices, on_device(): lax.all_to_all(request, 'tiles', split_axis=0, concat_axis=0, tiled=True)  18.4 us
    all_to_all x1, waiting for transfers between devices, on_device(): lax.all_to_all(picked, 'tiles', split_axis=0, concat_axis=0, tiled=True)  17.8 us
    all_to_all x1, waiting for transfers between devices, on_device(): lax.all_to_all(request, 'tiles', split_axis=0, concat_axis=0, tiled=True)  10.3 us
    ppermute x3, starting transfers between devices, ring(): lax.ppermute(values, 'rep', [(i, (i + steps) % reps) for i in range(reps)])  9.33 us
    all_to_all x1, blocking collectives, on_device(): lax.all_to_all(summed, 'rep', split_axis=0, concat_axis=0, tiled=True)  8.12 us
    all_to_all x1, starting transfers between devices, on_device(): lax.all_to_all(picked, 'tiles', split_axis=0, concat_axis=0, tiled=True)  5.73 us
    pallas_call x1, Pallas kernels, on_device(): pl.pallas_call(contract, out_shape=jax.ShapeDtypeStruct((tile_devs * word...  3.58 us
  transfers between devices with their start and end apart: 5, of which 4 were waited for; matrix products, arithmetic and copies ran while one was open for 0% of the time, Pallas kernels for 0%

profile of v4, /device:TPU:1, one launch (start us, length us, event | category | flops | bytes accessed | tf_op | source)
XLA Modules:
  0.0 122.4 jit_solution(111340540107466049)
XLA Ops:
  0.7 1.6 %read_tasks.1 = (s32[128,1,128]{2,1,0:T(1,128)}, s32[1,128]{1,0:T(1,128)}) custom-call(s32[1]{0:T(128)S(6)} %copy.11.live_ref, s32[16]{0:T(128)} %mask_ref.1, s32[4,128]{1,0:T(4,128)} %bitcast.12, s32[1,512]{1,0:T(1,128)} %bitcast.13), custom_call_target="tpu_custom_call" | custom-call | tf_op jit(solution)/shard_map/read_tasks/pallas_call | solution.py:165
  2.3 18.4 %all-to-all-start = ((s32[128,1,128]{2,1,0:T(1,128)}), s32[128,1,128]{2,1,0:T(1,128)S(1)}, u32[]{:S(2)}, u32[]{:S(2)}) async-start(s32[128,1,128]{2,1,0:T(1,128)} %get-tuple-element.9), calls=%async_computation | async-start | bytes 131072 | tf_op jit(solution)/shard_map/all_to_all | solution.py:175
  20.7 0.0 copy-start.1
  20.7 1.0 copy-done.1
  21.8 0.2 prepare_integrals.1.tiles_ref
  22.0 0.0 copy-start.2
  22.0 0.0 copy-start
  22.0 10.3 %all-to-all-done.request_ref = s32[128,1,128]{2,1,0:T(1,128)S(1)} async-done(((s32[128,1,128]{2,1,0:T(1,128)}), s32[128,1,128]{2,1,0:T(1,128)S(1)}, u32[]{:S(2)}, u32[]{:S(2)}) %all-to-all-start) | async-done | bytes 65568 | tf_op jit(solution)/shard_map/all_to_all | solution.py:175
  32.3 1.8 %pick.1 = (bf16[128,32,128]{2,1,0:T(8,128)(2,1)}, s32[1,128]{1,0:T(1,128)S(1)}) custom-call(s32[128,1,128]{2,1,0:T(1,128)S(1)} %all-to-all-done.request_ref, bf16[16,32,128]{2,1,0:T(8,128)(2,1)S(1)} %prepare_integrals.1.tiles_ref), custom_call_target="tpu_custom_call" | custom-call | tf_op jit(solution)/shard_map/pick/pallas_call | solution.py:195
  34.1 5.7 %all-to-all-start.1 = ((bf16[128,32,128]{2,1,0:T(8,128)(2,1)}), bf16[128,32,128]{2,1,0:T(8,128)(2,1)S(1)}, u32[]{:S(2)}, u32[]{:S(2)}) async-start(bf16[128,32,128]{2,1,0:T(8,128)(2,1)} %get-tuple-element.12), calls=%async_computation.1 | async-start | bytes 2097152 | tf_op jit(solution)/shard_map/all_to_all | solution.py:207
  39.8 0.0 copy-done.2
  39.8 4.4 %collective-permute-start.2 = (s32[1,128]{1,0:T(1,128)S(1)}, s32[1,128]{1,0:T(1,128)S(1)}, u32[]{:S(2)}, u32[]{:S(2)}) collective-permute-start(s32[1,128]{1,0:T(1,128)S(1)} %copy-done.2), channel_id=1, source_target_pairs={{0,3},{1,0},{2,1},{3,2},{4,7},{5,4},{6,5},{7,6},{8,11},{9,8},{10,9... | collective-permute-start | bytes 1544 | tf_op jit(solution)/shard_map/ppermute | solution.py:24
  44.2 2.4 %collective-permute-start.1 = (s32[1,128]{1,0:T(1,128)S(1)}, s32[1,128]{1,0:T(1,128)S(1)}, u32[]{:S(2)}, u32[]{:S(2)}) collective-permute-start(s32[1,128]{1,0:T(1,128)S(1)} %copy-done.2), channel_id=1, source_target_pairs={{0,2},{1,3},{2,0},{3,1},{4,6},{5,7},{6,4},{7,5},{8,10},{9,11},{10,... | collective-permute-start | bytes 1544 | tf_op jit(solution)/shard_map/ppermute | solution.py:24
  46.6 2.5 %collective-permute-start = (s32[1,128]{1,0:T(1,128)S(1)}, s32[1,128]{1,0:T(1,128)S(1)}, u32[]{:S(2)}, u32[]{:S(2)}) collective-permute-start(s32[1,128]{1,0:T(1,128)S(1)} %copy-done.2), channel_id=1, source_target_pairs={{0,1},{1,2},{2,3},{3,0},{4,5},{5,6},{6,7},{7,4},{8,9},{9,10},{10,1... | collective-permute-start | bytes 1544 | tf_op jit(solution)/shard_map/ppermute | solution.py:24
  49.2 0.0 copy-done
  49.2 0.2 prepare_lambda.1.refs_4_
  49.4 0.0 collective-permute-done.2.refs_3_
  49.4 0.9 collective-permute-done.1.refs_2_
  50.3 2.1 %collective-permute-done.refs_1_ = s32[1,128]{1,0:T(1,128)S(1)} collective-permute-done((s32[1,128]{1,0:T(1,128)S(1)}, s32[1,128]{1,0:T(1,128)S(1)}, u32[]{:S(2)}, u32[]{:S(2)}) %collective-permute-start) | collective-permute-done | bytes 544 | tf_op jit(solution)/shard_map/ppermute | solution.py:24
  52.4 17.8 %all-to-all-done.1.refs_5_ = bf16[128,32,128]{2,1,0:T(8,128)(2,1)S(1)} async-done(((bf16[128,32,128]{2,1,0:T(8,128)(2,1)}), bf16[128,32,128]{2,1,0:T(8,128)(2,1)S(1)}, u32[]{:S(2)}, u32[]{:S(2)}) %all-to-all-start.1) | async-done | bytes 1048608 | tf_op jit(solution)/shard_map/all_to_all | solution.py:207
  70.2 3.6 %contract.1 = s32[2176,128]{1,0:T(8,128)S(1)} custom-call(s32[1,128]{1,0:T(1,128)S(1)} %copy-done.2, s32[1,128]{1,0:T(1,128)S(1)} %collective-permute-done.refs_1_, s32[1,128]{1,0:T(1,128)S(1)} %collective-permute-done.1.refs_2_, s32[1,128]{1,0:T(1,128)S(1)} %collective-permute-done.2.refs_3_, bf16[33,128,128]{2,1,0:T(8,128)(2,1)S(1)} %prepare_lambda.1.refs_4_, ...), custom_call_target="tpu_custom_call" | custom-call | tf_op jit(solution)/shard_map/contract/pallas_call | solution.py:209
  73.8 38.5 %all_to_all.20 = s32[128,17,1,128]{3,2,1,0:T(1,128)S(1)} all-to-all(s32[128,17,1,128]{3,2,1,0:T(1,128)S(1)} %bitcast.9), channel_id=1, replica_groups=mesh['tiles'=128,'rep'=4] {'tiles'}, dimensions={0} | all-to-all | bytes 2228224 | tf_op jit(solution)/shard_map/all_to_all | solution.py:218
  112.3 1.3 %add_slots.1 = bf16[4,32,128]{2,1,0:T(8,128)(2,1)S(1)} custom-call(s32[1,128]{1,0:T(1,128)S(1)} %get-tuple-element.10.request_ref, s32[2176,128]{1,0:T(8,128)S(1)} %bitcast.10), custom_call_target="tpu_custom_call" | custom-call | tf_op jit(solution)/shard_map/add_slots/pallas_call | solution.py:220
  113.6 8.1 %all_to_all.21 = bf16[4,32,128]{2,1,0:T(8,128)(2,1)S(1)} all-to-all(bf16[4,32,128]{2,1,0:T(8,128)(2,1)S(1)} %add_slots.1), channel_id=1, replica_groups=mesh['tiles'=128,'rep'=4] {'rep'}, dimensions={0} | all-to-all | bytes 65536 | tf_op jit(solution)/shard_map/all_to_all | solution.py:229
  121.7 0.7 copy.10
Async XLA Ops:
  2.3 30.0 %all-to-all-start = ((s32[128,1,128]{2,1,0:T(1,128)}), s32[128,1,128]{2,1,0:T(1,128)S(1)}, u32[]{:S(2)}, u32[]{:S(2)}) async-start(s32[128,1,128]{2,1,0:T(1,128)} %get-tuple-element.9), calls=%async_computation | async-start | bytes 131072 | tf_op jit(solution)/shard_map/all_to_all | solution.py:175
  20.7 1.0 copy-start.1
  22.0 17.8 %copy-start.2 = (s32[1,128]{1,0:T(1,128)S(1)}, s32[1,128]{1,0:T(1,128)}, u32[]{:S(2)}) copy-start(s32[1,128]{1,0:T(1,128)} %get-tuple-element.11.refs_0_) | copy-start | bytes 1540
  22.0 27.2 %copy-start = (bf16[16,128,128]{2,1,0:T(8,128)(2,1)S(1)}, bf16[16,128,128]{2,1,0:T(8,128)(2,1)}, u32[]{:S(2)}) copy-start(bf16[16,128,128]{2,1,0:T(8,128)(2,1)} %lam_ref.1) | copy-start | bytes 1572868
  34.1 36.1 %all-to-all-start.1 = ((bf16[128,32,128]{2,1,0:T(8,128)(2,1)}), bf16[128,32,128]{2,1,0:T(8,128)(2,1)S(1)}, u32[]{:S(2)}, u32[]{:S(2)}) async-start(bf16[128,32,128]{2,1,0:T(8,128)(2,1)} %get-tuple-element.12), calls=%async_computation.1 | async-start | bytes 2097152 | tf_op jit(solution)/shard_map/all_to_all | solution.py:207
  39.8 9.6 %collective-permute-start.2 = (s32[1,128]{1,0:T(1,128)S(1)}, s32[1,128]{1,0:T(1,128)S(1)}, u32[]{:S(2)}, u32[]{:S(2)}) collective-permute-start(s32[1,128]{1,0:T(1,128)S(1)} %copy-done.2), channel_id=1, source_target_pairs={{0,3},{1,0},{2,1},{3,2},{4,7},{5,4},{6,5},{7,6},{8,11},{9,8},{10,9... | collective-permute-start | bytes 1544 | tf_op jit(solution)/shard_map/ppermute | solution.py:24
  44.2 6.1 %collective-permute-start.1 = (s32[1,128]{1,0:T(1,128)S(1)}, s32[1,128]{1,0:T(1,128)S(1)}, u32[]{:S(2)}, u32[]{:S(2)}) collective-permute-start(s32[1,128]{1,0:T(1,128)S(1)} %copy-done.2), channel_id=1, source_target_pairs={{0,2},{1,3},{2,0},{3,1},{4,6},{5,7},{6,4},{7,5},{8,10},{9,11},{10,... | collective-permute-start | bytes 1544 | tf_op jit(solution)/shard_map/ppermute | solution.py:24
  46.6 5.8 %collective-permute-start = (s32[1,128]{1,0:T(1,128)S(1)}, s32[1,128]{1,0:T(1,128)S(1)}, u32[]{:S(2)}, u32[]{:S(2)}) collective-permute-start(s32[1,128]{1,0:T(1,128)S(1)} %copy-done.2), channel_id=1, source_target_pairs={{0,1},{1,2},{2,3},{3,0},{4,5},{5,6},{6,7},{7,4},{8,9},{9,10},{10,1... | collective-permute-start | bytes 1544 | tf_op jit(solution)/shard_map/ppermute | solution.py:24

commit v5 on v4

v5 whole, which is shorter than its diff:
```python
import functools

import jax
import jax.numpy as jnp
from jax import lax
from jax.experimental import pallas as pl
from jax.experimental.pallas import tpu as pltpu
from jax.sharding import PartitionSpec as P

VMEM = pl.BlockSpec(memory_space=pltpu.VMEM)
OCTAVE = 256.0
FULL = 32760.0
SMALLEST = 2.0**-110
ROOM = pltpu.CompilerParams(vmem_limit_bytes=8 * 2**20)
SMEM = pl.BlockSpec(memory_space=pltpu.SMEM)


def power(size):
    return size.bit_length() - 1


def ring(values, steps):
    reps = lax.axis_size("rep")
    return lax.ppermute(values, "rep", [(i, (i + steps) % reps) for i in range(reps)])


def prepare_lambda(lam_ref, out_ref):
    count = lam_ref.shape[0]
    for tile in range(count):
        out_ref[tile] = lam_ref[tile].T
        out_ref[count + tile] = lam_ref[tile]
    out_ref[2 * count] = jnp.zeros_like(out_ref[2 * count])


def prepare_integrals(start_ref, int_ref, out_ref, turned):
    count, rows, _ = out_ref.shape
    start = pl.multiple_of(start_ref[0], rows)
    for tile in range(count):
        turned[tile] = int_ref[tile].T
        out_ref[tile] = turned[tile, pl.ds(start, rows), :]


def ask(tasks, request_ref, int_dev):
    peers, task_dev = request_ref.shape[0], tasks.shape[1]
    w_ids = tasks[1:2, :]
    peer = lax.broadcasted_iota(jnp.int32, (peers, task_dev), 0)
    wanted = jnp.where(peer == lax.shift_right_logical(w_ids, power(int_dev)), w_ids, 0)
    wanted = jnp.sum(lax.bitwise_and(wanted, int_dev - 1), axis=1, keepdims=True)
    request_ref[...] = jnp.broadcast_to(wanted, (peers, task_dev))


def read_tasks(live_ref, mask_ref, task_ref, map_ref, code_ref, int_dev, res_tile):
    lam_dev = mask_ref.shape[0]
    task_dev = task_ref.shape[1]
    peers = code_ref.shape[1]
    res_total = map_ref.shape[1]
    placed = map_ref[...]
    parts = jnp.concatenate(
        [placed // res_tile, placed % res_tile, jnp.zeros((6, res_total), jnp.int32)], axis=0
    )
    named = lax.broadcasted_iota(jnp.int32, (res_total, task_dev), 0) == task_ref[2:3, :]
    looked_up = jnp.dot(
        parts.astype(jnp.float32).astype(jnp.bfloat16),
        jnp.where(named, 1.0, 0.0).astype(jnp.bfloat16),
        preferred_element_type=jnp.float32,
    ).astype(jnp.int32)
    o_owner, slot = looked_up[0:1, :], looked_up[1:2, :]
    w_owner = task_ref[1:2, :] // int_dev
    lam_local = task_ref[0:1, :] % lam_dev
    hits_o = lax.broadcasted_iota(jnp.int32, (peers, task_dev), 0) == o_owner
    kept = jnp.zeros((1, task_dev), jnp.int32)
    for tile in range(lam_dev):
        kept = jnp.where(lam_local == tile, mask_ref[tile], kept)
    live = lax.broadcasted_iota(jnp.int32, (1, task_dev), 1) < live_ref[0]
    variant = jnp.where((kept == 1) & live, lam_local + lam_dev * task_ref[3:4, :], 2 * lam_dev)
    rows = jnp.concatenate([variant, w_owner, slot, jnp.zeros((5, task_dev), jnp.int32)], axis=0)
    by_owner = lax.dot_general(
        rows.astype(jnp.float32).astype(jnp.bfloat16),
        jnp.where(hits_o, 1.0, 0.0).astype(jnp.bfloat16),
        (((1,), (1,)), ((), ())),
        preferred_element_type=jnp.float32,
    ).astype(jnp.int32)
    code_ref[...] = (by_owner[0:1, :] * peers + by_owner[1:2, :]) * res_tile + by_owner[2:3, :]


def pick(request_ref, tiles_ref, out_ref, row, asked, sem):
    peers = out_ref.shape[0]
    got = request_ref[...]
    diagonal = lax.broadcasted_iota(jnp.int32, got.shape, 0) == lax.broadcasted_iota(jnp.int32, got.shape, 1)
    row[...] = jnp.sum(jnp.where(diagonal, got, 0), axis=0, keepdims=True)
    copy = pltpu.make_async_copy(row, asked, sem)
    copy.start()
    copy.wait()

    def body(step, carry):
        for k in range(32):
            peer = step * 32 + k
            out_ref[peer] = tiles_ref[asked[0, peer]]
        return carry

    lax.fori_loop(0, peers // 32, body, 0)


def contract(*refs, slots):
    *code_refs, lam_ref, w_ref, out_ref = refs
    peers, rows, edge = w_ref.shape
    unroll = 64
    words = rows // 2 + 1

    def one(step, place):
        owner = step * unroll + place
        codes = [ref[0, owner] for ref in code_refs]
        slot = lax.bitwise_and(codes[0], slots - 1)
        codes = [lax.shift_right_logical(code, power(slots)) for code in codes]
        left = [w_ref[lax.bitwise_and(code, peers - 1)] for code in codes]
        right = [lam_ref[lax.shift_right_logical(code, power(peers))] for code in codes]
        total = jnp.dot(
            jnp.concatenate(left, axis=1),
            jnp.concatenate(right, axis=0),
            preferred_element_type=jnp.float32,
        )
        top = jnp.max(jnp.abs(total), axis=0, keepdims=True)
        scale = jnp.ceil(jnp.log2(jnp.maximum(top, SMALLEST)) * OCTAVE)
        whole = jnp.round(total * (jnp.exp2(scale * (-1.0 / OCTAVE)) * FULL)).astype(jnp.int32)
        first = pl.multiple_of(step * unroll * words, 8) + place * words
        out_ref[pl.ds(first, rows // 2), :] = whole[: rows // 2] * 65536 + whole[rows // 2 :]
        out_ref[pl.ds(first + rows // 2, 1), :] = scale.astype(jnp.int32) * slots + slot

    def body(step, carry):
        for k in range(unroll):
            one(step, k)
        return carry

    lax.fori_loop(0, peers // unroll, body, 0)


def add_slots(x_ref, out_ref):
    slots, rows, edge = out_ref.shape
    words = rows // 2 + 1
    unroll = 16

    def body(step, sums):
        for k in range(unroll):
            first = pl.multiple_of(step * unroll * words, 8) + k * words
            pairs = x_ref[pl.ds(first, rows // 2), :]
            low = lax.shift_right_arithmetic(lax.shift_left(pairs, 16), 16)
            high = lax.shift_right_arithmetic(pairs - low, 16)
            last = x_ref[pl.ds(first + rows // 2, 1), :]
            slot = lax.bitwise_and(last, slots - 1)
            scale = lax.shift_right_arithmetic(last, power(slots)).astype(jnp.float32)
            scale = jnp.exp2(scale * (1.0 / OCTAVE)) * (1.0 / FULL)
            value = jnp.concatenate([high, low], axis=0).astype(jnp.float32) * scale
            mine = [jnp.broadcast_to(slot, (rows, edge)) == s for s in range(slots)]
            sums = tuple(jnp.where(m, total + value, total) for m, total in zip(mine, sums))
        return sums

    zero = jnp.zeros((rows, edge), jnp.float32)
    sums = lax.fori_loop(0, x_ref.shape[0] // (words * unroll), body, (zero,) * slots)
    for s in range(slots):
        out_ref[s] = sums[s].astype(out_ref.dtype)


def on_device(lam_tiles, int_tiles, task_list, live_count, tile_mask, owner_map):
    tile_devs = lax.axis_size("tiles")
    reps = lax.axis_size("rep")
    rep_index = lax.axis_index("rep")
    lam_dev, edge, _ = lam_tiles.shape
    int_dev = int_tiles.shape[0]
    res_tile = owner_map.shape[0] // tile_devs
    rows = edge // reps
    words = rows // 2 + 1

    tasks = task_list.T
    request = pl.pallas_call(
        functools.partial(ask, int_dev=int_dev),
        out_shape=jax.ShapeDtypeStruct((tile_devs, 128), jnp.int32),
        in_specs=[VMEM],
        out_specs=VMEM,
        compiler_params=ROOM,
        name="ask",
    )(tasks)
    request = lax.all_to_all(
        request.reshape(tile_devs, 1, 128), "tiles", split_axis=0, concat_axis=0, tiled=True
    ).reshape(tile_devs, 128)
    code = pl.pallas_call(
        functools.partial(read_tasks, int_dev=int_dev, res_tile=res_tile),
        out_shape=jax.ShapeDtypeStruct((1, tile_devs), jnp.int32),
        in_specs=[SMEM, SMEM, VMEM, VMEM],
        out_specs=VMEM,
        name="read_tasks",
    )(live_count, tile_mask, tasks, owner_map[None, :])
    codes = [code] + [ring(code, k) for k in range(1, reps)]

    lam_all = pl.pallas_call(
        prepare_lambda,
        out_shape=jax.ShapeDtypeStruct((2 * lam_dev + 1, edge, edge), jnp.bfloat16),
        in_specs=[VMEM],
        out_specs=VMEM,
        compiler_params=ROOM,
        name="prepare_lambda",
    )(lam_tiles)
    columns = pl.pallas_call(
        prepare_integrals,
        out_shape=jax.ShapeDtypeStruct((int_dev, rows, edge), jnp.bfloat16),
        in_specs=[SMEM, VMEM],
        out_specs=VMEM,
        scratch_shapes=[pltpu.VMEM((int_dev, edge, edge), jnp.bfloat16)],
        compiler_params=ROOM,
        name="prepare_integrals",
    )((rep_index * rows).reshape(1), int_tiles)
    picked = pl.pallas_call(
        pick,
        out_shape=jax.ShapeDtypeStruct((tile_devs, rows, edge), jnp.bfloat16),
        in_specs=[VMEM, VMEM],
        out_specs=VMEM,
        scratch_shapes=[
            pltpu.VMEM((1, tile_devs), jnp.int32),
            pltpu.SMEM((1, tile_devs), jnp.int32),
            pltpu.SemaphoreType.DMA,
        ],
        compiler_params=ROOM,
        name="pick",
    )(request, columns)
    fetched = lax.all_to_all(picked, "tiles", split_axis=0, concat_axis=0, tiled=True)

    totals = pl.pallas_call(
        functools.partial(contract, slots=res_tile),
        out_shape=jax.ShapeDtypeStruct((tile_devs * words, edge), jnp.int32),
        in_specs=[SMEM] * reps + [VMEM, VMEM],
        out_specs=VMEM,
        compiler_params=ROOM,
        name="contract",
    )(*codes, lam_all, fetched)
    totals = totals.reshape(tile_devs, words, 1, edge)
    partial_tiles = lax.all_to_all(totals, "tiles", split_axis=0, concat_axis=0, tiled=True)
    partial_tiles = partial_tiles.reshape(tile_devs * words, edge)
    summed = pl.pallas_call(
        add_slots,
        out_shape=jax.ShapeDtypeStruct((res_tile, rows, edge), jnp.bfloat16),
        in_specs=[VMEM],
        out_specs=VMEM,
        compiler_params=ROOM,
        name="add_slots",
    )(partial_tiles)
    mine = lax.all_to_all(summed, "rep", split_axis=0, concat_axis=0, tiled=True)
    return mine.reshape(edge, edge).T[None]


def solution(mesh):
    placed = (
        P("tiles", None, None),
        P("tiles", None, None),
        P(("tiles", "rep"), None),
        P(("tiles", "rep")),
        P("tiles"),
        P(),
    )
    return jax.shard_map(
        on_device,
        mesh=mesh,
        in_specs=placed,
        out_specs=P(("tiles", "rep"), None, None),
        check_vma=False,
    )
```

time: 124 us -> 123 us (level)
  waiting for transfers between devices: 31.1 us -> 28.7 us
    all_to_all x1, waiting for transfers between devices: 17.8 us -> 15.3 us  [on_device(): lax.all_to_all(picked, 'tiles', split_axis=0, concat_axis=0, tiled=True)]
    pallas_call x2 -> x3, Pallas kernels: 5.37 us -> 5.8 us  [the longest x1 3.37 us: on_device(): pl.pallas_call(functools.partial(contract, slots=res_tile), out_shape=jax...]
  transfers between devices with their start and end apart: 5 -> 5, of which waited for: 4 -> 4; matrix products, arithmetic and copies ran while one was open for 0% -> 0% of each run, Pallas kernels for 0% -> 2%
where the time goes in v5:
time: 123 us; the launch traced here: 121 us
  blocking collectives  46.6 us (38%)
  starting transfers between devices  33.8 us (27%)
  waiting for transfers between devices  28.7 us (23%)
  Pallas kernels  8.77 us (7%)
  local copies, waits for them, and re-layouts  2.45 us (2%)
    all_to_all x1, blocking collectives, on_device(): lax.all_to_all(totals, 'tiles', split_axis=0, concat_axis=0, tiled=True)  38.5 us
    all_to_all x1, starting transfers between devices, on_device(): lax.all_to_all(request.reshape(tile_devs, 1, 128), 'tiles', split_axis=0,...  18.4 us
    all_to_all x1, waiting for transfers between devices, on_device(): lax.all_to_all(picked, 'tiles', split_axis=0, concat_axis=0, tiled=True)  15.3 us
    all_to_all x1, waiting for transfers between devices, on_device(): lax.all_to_all(request.reshape(tile_devs, 1, 128), 'tiles', split_axis=0,...  10.2 us
    ppermute x3, starting transfers between devices, ring(): lax.ppermute(values, 'rep', [(i, (i + steps) % reps) for i in range(reps)])  9.45 us
    all_to_all x1, blocking collectives, on_device(): lax.all_to_all(summed, 'rep', split_axis=0, concat_axis=0, tiled=True)  8.11 us
    all_to_all x1, starting transfers between devices, on_device(): lax.all_to_all(picked, 'tiles', split_axis=0, concat_axis=0, tiled=True)  5.9 us
    pallas_call x1, Pallas kernels, on_device(): pl.pallas_call(functools.partial(contract, slots=res_tile), out_shape=jax...  3.37 us
  transfers between devices with their start and end apart: 5, of which 4 were waited for; matrix products, arithmetic and copies ran while one was open for 0% of the time, Pallas kernels for 2%

profile of v5, /device:TPU:1, one launch (start us, length us, event | category | flops | bytes accessed | tf_op | source)
XLA Modules:
  0.0 121.1 jit_solution(1468239126870308474)
XLA Ops:
  0.0 0.0 copy-start.2
  0.0 0.7 copy-done.2
  0.7 0.7 ask.1
  1.4 18.4 %all-to-all-start = ((s32[128,1,128]{2,1,0:T(1,128)}), s32[128,1,128]{2,1,0:T(1,128)S(1)}, u32[]{:S(2)}, u32[]{:S(2)}) async-start(s32[128,1,128]{2,1,0:T(1,128)} %bitcast.3), calls=%async_computation | async-start | bytes 131072 | tf_op jit(solution)/shard_map/all_to_all | solution.py:182
  19.9 0.0 copy-start.1
  19.9 1.0 copy-done.1
  20.9 0.2 prepare_integrals.1.tiles_ref
  21.1 10.2 %all-to-all-done = s32[128,1,128]{2,1,0:T(1,128)S(1)} async-done(((s32[128,1,128]{2,1,0:T(1,128)}), s32[128,1,128]{2,1,0:T(1,128)S(1)}, u32[]{:S(2)}, u32[]{:S(2)}) %all-to-all-start) | async-done | bytes 65568 | tf_op jit(solution)/shard_map/all_to_all | solution.py:182
  31.3 1.7 %pick.1 = bf16[128,32,128]{2,1,0:T(8,128)(2,1)} custom-call(s32[128,128]{1,0:T(8,128)S(1)} %bitcast.15, bf16[16,32,128]{2,1,0:T(8,128)(2,1)S(1)} %prepare_integrals.1.tiles_ref), custom_call_target="tpu_custom_call" | custom-call | tf_op jit(solution)/shard_map/pick/pallas_call | solution.py:211
  33.0 0.0 copy-start
  33.0 5.9 %all-to-all-start.1 = ((bf16[128,32,128]{2,1,0:T(8,128)(2,1)}), bf16[128,32,128]{2,1,0:T(8,128)(2,1)S(1)}, u32[]{:S(2)}, u32[]{:S(2)}) async-start(bf16[128,32,128]{2,1,0:T(8,128)(2,1)} %pick.1), calls=%async_computation.1 | async-start | bytes 2097152 | tf_op jit(solution)/shard_map/all_to_all | solution.py:224
  39.6 1.5 %read_tasks.1.refs_0_ = s32[1,128]{1,0:T(1,128)} custom-call(s32[1]{0:T(128)S(6)} %copy.12.live_ref, s32[16]{0:T(128)} %mask_ref.1, s32[4,128]{1,0:T(4,128)} %bitcast.16, s32[1,512]{1,0:T(1,128)} %bitcast.19), custom_call_target="tpu_custom_call" | custom-call | tf_op jit(solution)/shard_map/read_tasks/pallas_call | solution.py:185
  41.1 0.0 copy-start.3
  41.1 4.5 %collective-permute-start.2 = (s32[1,128]{1,0:T(1,128)}, s32[1,128]{1,0:T(1,128)S(1)}, u32[]{:S(2)}, u32[]{:S(2)}) collective-permute-start(s32[1,128]{1,0:T(1,128)} %read_tasks.1.refs_0_), channel_id=1, source_target_pairs={{0,3},{1,0},{2,1},{3,2},{4,7},{5,4},{6,5},{7,6},{8,11},{9,8},{10,9... | collective-permute-start | bytes 1544 | tf_op jit(solution)/shard_map/ppermute | solution.py:24
  45.6 2.4 %collective-permute-start.1 = (s32[1,128]{1,0:T(1,128)}, s32[1,128]{1,0:T(1,128)S(1)}, u32[]{:S(2)}, u32[]{:S(2)}) collective-permute-start(s32[1,128]{1,0:T(1,128)} %read_tasks.1.refs_0_), channel_id=1, source_target_pairs={{0,2},{1,3},{2,0},{3,1},{4,6},{5,7},{6,4},{7,5},{8,10},{9,11},{10,... | collective-permute-start | bytes 1544 | tf_op jit(solution)/shard_map/ppermute | solution.py:24
  48.0 2.5 %collective-permute-start = (s32[1,128]{1,0:T(1,128)}, s32[1,128]{1,0:T(1,128)S(1)}, u32[]{:S(2)}, u32[]{:S(2)}) collective-permute-start(s32[1,128]{1,0:T(1,128)} %read_tasks.1.refs_0_), channel_id=1, source_target_pairs={{0,1},{1,2},{2,3},{3,0},{4,5},{5,6},{6,7},{7,4},{8,9},{9,10},{10,1... | collective-permute-start | bytes 1544 | tf_op jit(solution)/shard_map/ppermute | solution.py:24
  50.6 0.0 copy-done
  50.6 0.2 prepare_lambda.1.refs_4_
  50.8 0.0 collective-permute-done.2.refs_3_
  50.8 1.0 collective-permute-done.1.refs_2_
  51.8 2.1 %collective-permute-done.refs_1_ = s32[1,128]{1,0:T(1,128)S(1)} collective-permute-done((s32[1,128]{1,0:T(1,128)}, s32[1,128]{1,0:T(1,128)S(1)}, u32[]{:S(2)}, u32[]{:S(2)}) %collective-permute-start) | collective-permute-done | bytes 544 | tf_op jit(solution)/shard_map/ppermute | solution.py:24
  54.0 15.3 %all-to-all-done.1.refs_5_ = bf16[128,32,128]{2,1,0:T(8,128)(2,1)S(1)} async-done(((bf16[128,32,128]{2,1,0:T(8,128)(2,1)}), bf16[128,32,128]{2,1,0:T(8,128)(2,1)S(1)}, u32[]{:S(2)}, u32[]{:S(2)}) %all-to-all-start.1) | async-done | bytes 1048608 | tf_op jit(solution)/shard_map/all_to_all | solution.py:224
  69.3 0.0 copy-done.3
  69.3 3.4 %contract.1 = s32[2176,128]{1,0:T(8,128)S(1)} custom-call(s32[1,128]{1,0:T(1,128)S(1)} %copy-done.3, s32[1,128]{1,0:T(1,128)S(1)} %collective-permute-done.refs_1_, s32[1,128]{1,0:T(1,128)S(1)} %collective-permute-done.1.refs_2_, s32[1,128]{1,0:T(1,128)S(1)} %collective-permute-done.2.refs_3_, bf16[33,128,128]{2,1,0:T(8,128)(2,1)S(1)} %prepare_lambda.1.refs_4_, ...), custom_call_target="tpu_custom_call" | custom-call | tf_op jit(solution)/shard_map/contract/pallas_call | solution.py:226
  72.7 38.5 %all_to_all.20 = s32[128,17,1,128]{3,2,1,0:T(1,128)S(1)} all-to-all(s32[128,17,1,128]{3,2,1,0:T(1,128)S(1)} %bitcast.13), channel_id=1, replica_groups=mesh['tiles'=128,'rep'=4] {'tiles'}, dimensions={0} | all-to-all | bytes 2228224 | tf_op jit(solution)/shard_map/all_to_all | solution.py:235
  111.2 1.0 add_slots.1
  112.3 8.1 %all_to_all.21 = bf16[4,32,128]{2,1,0:T(8,128)(2,1)S(1)} all-to-all(bf16[4,32,128]{2,1,0:T(8,128)(2,1)S(1)} %add_slots.1), channel_id=1, replica_groups=mesh['tiles'=128,'rep'=4] {'rep'}, dimensions={0} | all-to-all | bytes 65536 | tf_op jit(solution)/shard_map/all_to_all | solution.py:245
  120.4 0.7 copy.11
Async XLA Ops:
  0.0 0.7 copy-start.2
  1.4 29.9 %all-to-all-start = ((s32[128,1,128]{2,1,0:T(1,128)}), s32[128,1,128]{2,1,0:T(1,128)S(1)}, u32[]{:S(2)}, u32[]{:S(2)}) async-start(s32[128,1,128]{2,1,0:T(1,128)} %bitcast.3), calls=%async_computation | async-start | bytes 131072 | tf_op jit(solution)/shard_map/all_to_all | solution.py:182
  19.9 1.0 copy-start.1
  33.0 17.6 %copy-start = (bf16[16,128,128]{2,1,0:T(8,128)(2,1)S(1)}, bf16[16,128,128]{2,1,0:T(8,128)(2,1)}, u32[]{:S(2)}) copy-start(bf16[16,128,128]{2,1,0:T(8,128)(2,1)} %lam_ref.1) | copy-start | bytes 1572868
  33.0 36.3 %all-to-all-start.1 = ((bf16[128,32,128]{2,1,0:T(8,128)(2,1)}), bf16[128,32,128]{2,1,0:T(8,128)(2,1)S(1)}, u32[]{:S(2)}, u32[]{:S(2)}) async-start(bf16[128,32,128]{2,1,0:T(8,128)(2,1)} %pick.1), calls=%async_computation.1 | async-start | bytes 2097152 | tf_op jit(solution)/shard_map/all_to_all | solution.py:224
  41.1 28.2 %copy-start.3 = (s32[1,128]{1,0:T(1,128)S(1)}, s32[1,128]{1,0:T(1,128)}, u32[]{:S(2)}) copy-start(s32[1,128]{1,0:T(1,128)} %read_tasks.1.refs_0_) | copy-start | bytes 1540
  41.1 9.7 %collective-permute-start.2 = (s32[1,128]{1,0:T(1,128)}, s32[1,128]{1,0:T(1,128)S(1)}, u32[]{:S(2)}, u32[]{:S(2)}) collective-permute-start(s32[1,128]{1,0:T(1,128)} %read_tasks.1.refs_0_), channel_id=1, source_target_pairs={{0,3},{1,0},{2,1},{3,2},{4,7},{5,4},{6,5},{7,6},{8,11},{9,8},{10,9... | collective-permute-start | bytes 1544 | tf_op jit(solution)/shard_map/ppermute | solution.py:24
  45.6 6.2 %collective-permute-start.1 = (s32[1,128]{1,0:T(1,128)}, s32[1,128]{1,0:T(1,128)S(1)}, u32[]{:S(2)}, u32[]{:S(2)}) collective-permute-start(s32[1,128]{1,0:T(1,128)} %read_tasks.1.refs_0_), channel_id=1, source_target_pairs={{0,2},{1,3},{2,0},{3,1},{4,6},{5,7},{6,4},{7,5},{8,10},{9,11},{10,... | collective-permute-start | bytes 1544 | tf_op jit(solution)/shard_map/ppermute | solution.py:24
  48.0 5.9 %collective-permute-start = (s32[1,128]{1,0:T(1,128)}, s32[1,128]{1,0:T(1,128)S(1)}, u32[]{:S(2)}, u32[]{:S(2)}) collective-permute-start(s32[1,128]{1,0:T(1,128)} %read_tasks.1.refs_0_), channel_id=1, source_target_pairs={{0,1},{1,2},{2,3},{3,0},{4,5},{5,6},{6,7},{7,4},{8,9},{9,10},{10,1... | collective-permute-start | bytes 1544 | tf_op jit(solution)/shard_map/ppermute | solution.py:24

commit v6 on v5

--- a/solution.py
+++ b/solution.py
@@ -32,20 +32,25 @@
     out_ref[2 * count] = jnp.zeros_like(out_ref[2 * count])
 
 
-def prepare_integrals(start_ref, int_ref, out_ref, turned):
-    count, rows, _ = out_ref.shape
-    start = pl.multiple_of(start_ref[0], rows)
-    for tile in range(count):
-        turned[tile] = int_ref[tile].T
-        out_ref[tile] = turned[tile, pl.ds(start, rows), :]
-
-
-def ask(tasks, request_ref, int_dev):
-    peers, task_dev = request_ref.shape[0], tasks.shape[1]
-    w_ids = tasks[1:2, :]
+def prepare_integrals(place_ref, own_ref, other_ref, out_ref, turned):
+    _, count, rows, _ = out_ref.shape
+    core = place_ref[0]
+    start = pl.multiple_of(place_ref[1], rows)
+    for place, tiles in ((core, own_ref), (1 - core, other_ref)):
+        for tile in range(count):
+            turned[tile] = tiles[tile].T
+            out_ref[place, tile] = turned[tile, pl.ds(start, rows), :]
+
+
+def ask(task_ref, request_ref, int_dev):
+    peers, task_dev = request_ref.shape[0], task_ref.shape[1]
+    w_ids = task_ref[1:2, :]
+    w_owner = lax.shift_right_logical(w_ids, power(int_dev))
+    place = lax.bitwise_and(w_owner, 1) * power(int_dev)
+    named = lax.shift_left(lax.bitwise_and(w_ids, int_dev - 1), place)
     peer = lax.broadcasted_iota(jnp.int32, (peers, task_dev), 0)
-    wanted = jnp.where(peer == lax.shift_right_logical(w_ids, power(int_dev)), w_ids, 0)
-    wanted = jnp.sum(lax.bitwise_and(wanted, int_dev - 1), axis=1, keepdims=True)
+    wanted = jnp.where(peer == lax.shift_right_logical(w_owner, 1), named, 0)
+    wanted = jnp.sum(wanted, axis=1, keepdims=True)
     request_ref[...] = jnp.broadcast_to(wanted, (peers, task_dev))
 
 
@@ -84,7 +89,8 @@
 
 
 def pick(request_ref, tiles_ref, out_ref, row, asked, sem):
-    peers = out_ref.shape[0]
+    peers, both, edge = out_ref.shape
+    _, int_dev, rows, _ = tiles_ref.shape
     got = request_ref[...]
     diagonal = lax.broadcasted_iota(jnp.int32, got.shape, 0) == lax.broadcasted_iota(jnp.int32, got.shape, 1)
     row[...] = jnp.sum(jnp.where(diagonal, got, 0), axis=0, keepdims=True)
@@ -93,12 +99,14 @@
     copy.wait()
 
     def body(step, carry):
-        for k in range(32):
-            peer = step * 32 + k
-            out_ref[peer] = tiles_ref[asked[0, peer]]
+        for k in range(16):
+            peer = step * 16 + k
+            word = asked[0, peer]
+            out_ref[peer, :rows] = tiles_ref[0, lax.bitwise_and(word, int_dev - 1)]
+            out_ref[peer, rows:] = tiles_ref[1, lax.shift_right_logical(word, power(int_dev))]
         return carry
 
-    lax.fori_loop(0, peers // 32, body, 0)
+    lax.fori_loop(0, peers // 16, body, 0)
 
 
 def contract(*refs, slots):
@@ -135,29 +143,36 @@
 
 
 def add_slots(x_ref, out_ref):
-    slots, rows, edge = out_ref.shape
+    owners, slots, rows, edge = out_ref.shape
     words = rows // 2 + 1
     unroll = 16
-
-    def body(step, sums):
-        for k in range(unroll):
-            first = pl.multiple_of(step * unroll * words, 8) + k * words
-            pairs = x_ref[pl.ds(first, rows // 2), :]
-            low = lax.shift_right_arithmetic(lax.shift_left(pairs, 16), 16)
-            high = lax.shift_right_arithmetic(pairs - low, 16)
-            last = x_ref[pl.ds(first + rows // 2, 1), :]
-            slot = lax.bitwise_and(last, slots - 1)
-            scale = lax.shift_right_arithmetic(last, power(slots)).astype(jnp.float32)
-            scale = jnp.exp2(scale * (1.0 / OCTAVE)) * (1.0 / FULL)
-            value = jnp.concatenate([high, low], axis=0).astype(jnp.float32) * scale
-            mine = [jnp.broadcast_to(slot, (rows, edge)) == s for s in range(slots)]
-            sums = tuple(jnp.where(m, total + value, total) for m, total in zip(mine, sums))
-        return sums
-
     zero = jnp.zeros((rows, edge), jnp.float32)
-    sums = lax.fori_loop(0, x_ref.shape[0] // (words * unroll), body, (zero,) * slots)
-    for s in range(slots):
-        out_ref[s] = sums[s].astype(out_ref.dtype)
+    for owner in range(owners):
+
+        def body(step, sums):
+            for k in range(unroll):
+                first = pl.multiple_of(step * unroll * owners * words, 8) + (k * owners + owner) * words
+                pairs = x_ref[pl.ds(first, rows // 2), :]
+                low = lax.shift_right_arithmetic(lax.shift_left(pairs, 16), 16)
+                high = lax.shift_right_arithmetic(pairs - low, 16)
+                last = x_ref[pl.ds(first + rows // 2, 1), :]
+                slot = lax.bitwise_and(last, slots - 1)
+                scale = lax.shift_right_arithmetic(last, power(slots)).astype(jnp.float32)
+                scale = jnp.exp2(scale * (1.0 / OCTAVE)) * (1.0 / FULL)
+                value = jnp.concatenate([high, low], axis=0).astype(jnp.float32) * scale
+                mine = [jnp.broadcast_to(slot, (rows, edge)) == s for s in range(slots)]
+                sums = tuple(jnp.where(m, total + value, total) for m, total in zip(mine, sums))
+            return sums
+
+        sums = lax.fori_loop(0, x_ref.shape[0] // (words * owners * unroll), body, (zero,) * slots)
+        for s in range(slots):
+            out_ref[owner, s] = sums[s]
+
+
+def finish(x_ref, out_ref):
+    parts, rows, edge = x_ref.shape
+    total = x_ref[: parts // 2] + x_ref[parts // 2 :]
+    out_ref[...] = total.reshape(edge, edge).T.astype(out_ref.dtype)
 
 
 def on_device(lam_tiles, int_tiles, task_list, live_count, tile_mask, owner_map):
@@ -171,17 +186,19 @@
     words = rows // 2 + 1
 
     tasks = task_list.T
+    chips = tile_devs // 2
+    same_core = [[2 * chip + core for chip in range(chips)] for core in range(2)]
     request = pl.pallas_call(
         functools.partial(ask, int_dev=int_dev),
-        out_shape=jax.ShapeDtypeStruct((tile_devs, 128), jnp.int32),
+        out_shape=jax.ShapeDtypeStruct((chips, 128), jnp.int32),
         in_specs=[VMEM],
         out_specs=VMEM,
         compiler_params=ROOM,
         name="ask",
     )(tasks)
     request = lax.all_to_all(
-        request.reshape(tile_devs, 1, 128), "tiles", split_axis=0, concat_axis=0, tiled=True
-    ).reshape(tile_devs, 128)
+        request.reshape(chips, 1, 128), "tiles", split_axis=0, concat_axis=0, tiled=True, axis_index_groups=same_core
+    ).reshape(chips, 128)
     code = pl.pallas_call(
         functools.partial(read_tasks, int_dev=int_dev, res_tile=res_tile),
         out_shape=jax.ShapeDtypeStruct((1, tile_devs), jnp.int32),
@@ -199,29 +216,32 @@
         compiler_params=ROOM,
         name="prepare_lambda",
     )(lam_tiles)
+    other = lax.ppermute(int_tiles, "tiles", [(i, i ^ 1) for i in range(tile_devs)])
     columns = pl.pallas_call(
         prepare_integrals,
-        out_shape=jax.ShapeDtypeStruct((int_dev, rows, edge), jnp.bfloat16),
-        in_specs=[SMEM, VMEM],
+        out_shape=jax.ShapeDtypeStruct((2, int_dev, rows, edge), jnp.bfloat16),
+        in_specs=[SMEM, VMEM, VMEM],
         out_specs=VMEM,
         scratch_shapes=[pltpu.VMEM((int_dev, edge, edge), jnp.bfloat16)],
         compiler_params=ROOM,
         name="prepare_integrals",
-    )((rep_index * rows).reshape(1), int_tiles)
+    )(jnp.stack([lax.axis_index("tiles") % 2, rep_index * rows]), int_tiles, other)
     picked = pl.pallas_call(
         pick,
-        out_shape=jax.ShapeDtypeStruct((tile_devs, rows, edge), jnp.bfloat16),
+        out_shape=jax.ShapeDtypeStruct((chips, 2 * rows, edge), jnp.bfloat16),
         in_specs=[VMEM, VMEM],
         out_specs=VMEM,
         scratch_shapes=[
-            pltpu.VMEM((1, tile_devs), jnp.int32),
-            pltpu.SMEM((1, tile_devs), jnp.int32),
+            pltpu.VMEM((1, 128), jnp.int32),
+            pltpu.SMEM((1, 128), jnp.int32),
             pltpu.SemaphoreType.DMA,
         ],
         compiler_params=ROOM,
         name="pick",
     )(request, columns)
-    fetched = lax.all_to_all(picked, "tiles", split_axis=0, concat_axis=0, tiled=True)
+    fetched = lax.all_to_all(
+        picked, "tiles", split_axis=0, concat_axis=0, tiled=True, axis_index_groups=same_core
+    ).reshape(tile_devs, rows, edge)
 
     totals = pl.pallas_call(
         functools.partial(contract, slots=res_tile),
@@ -231,19 +251,36 @@
         compiler_params=ROOM,
         name="contract",
     )(*codes, lam_all, fetched)
-    totals = totals.reshape(tile_devs, words, 1, edge)
-    partial_tiles = lax.all_to_all(totals, "tiles", split_axis=0, concat_axis=0, tiled=True)
-    partial_tiles = partial_tiles.reshape(tile_devs * words, edge)
+    totals = totals.reshape(chips, 2 * words, 1, edge)
+    partial_tiles = lax.all_to_all(
+        totals, "tiles", split_axis=0, concat_axis=0, tiled=True, axis_index_groups=same_core
+    ).reshape(tile_devs * words, edge)
     summed = pl.pallas_call(
         add_slots,
-        out_shape=jax.ShapeDtypeStruct((res_tile, rows, edge), jnp.bfloat16),
+        out_shape=jax.ShapeDtypeStruct((2, res_tile, rows, edge), jnp.float32),
         in_specs=[VMEM],
         out_specs=VMEM,
         compiler_params=ROOM,
         name="add_slots",
     )(partial_tiles)
-    mine = lax.all_to_all(summed, "rep", split_axis=0, concat_axis=0, tiled=True)
-    return mine.reshape(edge, edge).T[None]
+    same_chip = [[2 * reps * chip + i for i in range(2 * reps)] for chip in range(chips)]
+    mine = lax.all_to_all(
+        summed.reshape(2 * res_tile, rows, edge),
+        ("tiles", "rep"),
+        split_axis=0,
+        concat_axis=0,
+        tiled=True,
+        axis_index_groups=same_chip,
+    )
+    mine = pl.pallas_call(
+        finish,
+        out_shape=jax.ShapeDtypeStruct((edge, edge), jnp.bfloat16),
+        in_specs=[VMEM],
+        out_specs=VMEM,
+        compiler_params=ROOM,
+        name="finish",
+    )(mine)
+    return mine[None]
 
 
 def solution(mesh):

time: 123 us -> 121 us (0.984); the launches traced: 121 us -> 120 us
  waiting for transfers between devices: 28.7 us -> 23.4 us
  blocking collectives: 46.6 us -> 50.4 us
  Pallas kernels: 8.77 us -> 10.1 us
    ppermute x0 -> x1, starting transfers between devices: none -> 8.78 us  [on_device(): lax.ppermute(int_tiles, 'tiles', [(i, i ^ 1) for i in range(tile_devs)])]
    all_to_all x2, starting transfers between devices: 24.3 us -> 15.7 us  [the longest x1 10.9 us: on_device(): lax.all_to_all(request.reshape(chips, 1, 128), 'tiles', split_axis=0, con...]
    all_to_all x2, waiting for transfers between devices: 25.5 us -> 20.2 us  [the longest x1 11.5 us: on_device(): lax.all_to_all(picked, 'tiles', split_axis=0, concat_axis=0, tiled=True,...]
    all_to_all x2, blocking collectives: 46.6 us -> 50.4 us  [the longest x1 37.2 us: on_device(): lax.all_to_all(totals, 'tiles', split_axis=0, concat_axis=0, tiled=True,...]
    pallas_call x3 -> x4, Pallas kernels: 2.94 us -> 4.34 us  [the longest x1 1.69 us: on_device(): pl.pallas_call(pick, out_shape=jax.ShapeDtypeStruct((chips, 2 * rows, edg...]
  transfers between devices with their start and end apart: 5 -> 6, of which waited for: 4 -> 4; matrix products, arithmetic and copies ran while one was open for 0% -> 0% of each run, Pallas kernels for 2% -> 3%
where the time goes in v6:
time: 121 us; the launch traced here: 120 us
  blocking collectives  50.4 us (42%)
  starting transfers between devices  34 us (28%)
  waiting for transfers between devices  23.4 us (19%)
  Pallas kernels  10.1 us (8%)
  local copies, waits for them, and re-layouts  1.73 us (1%)
    all_to_all x1, blocking collectives, on_device(): lax.all_to_all(totals, 'tiles', split_axis=0, concat_axis=0, tiled=True,...  37.2 us
    all_to_all x1, blocking collectives, on_device(): lax.all_to_all(summed.reshape(2 * res_tile, rows, edge), ('tiles', 'rep')...  13.2 us
    all_to_all x1, waiting for transfers between devices, on_device(): lax.all_to_all(picked, 'tiles', split_axis=0, concat_axis=0, tiled=True,...  11.5 us
    all_to_all x1, starting transfers between devices, on_device(): lax.all_to_all(request.reshape(chips, 1, 128), 'tiles', split_axis=0, con...  10.9 us
    ppermute x3, starting transfers between devices, ring(): lax.ppermute(values, 'rep', [(i, (i + steps) % reps) for i in range(reps)])  9.45 us
    ppermute x1, starting transfers between devices, on_device(): lax.ppermute(int_tiles, 'tiles', [(i, i ^ 1) for i in range(tile_devs)])  8.78 us
    all_to_all x1, waiting for transfers between devices, on_device(): lax.all_to_all(request.reshape(chips, 1, 128), 'tiles', split_axis=0, con...  8.75 us
    all_to_all x1, starting transfers between devices, on_device(): lax.all_to_all(picked, 'tiles', split_axis=0, concat_axis=0, tiled=True,...  4.8 us
  transfers between devices with their start and end apart: 6, of which 4 were waited for; matrix products, arithmetic and copies ran while one was open for 0% of the time, Pallas kernels for 3%

profile of v6, /device:TPU:1, one launch (start us, length us, event | category | flops | bytes accessed | tf_op | source)
XLA Modules:
  0.0 120.4 jit_solution(6406567748949483711)
XLA Ops:
  0.0 8.8 %collective-permute-start.3 = (bf16[16,128,128]{2,1,0:T(8,128)(2,1)}, bf16[16,128,128]{2,1,0:T(8,128)(2,1)S(1)}, u32[]{:S(2)}, u32[]{:S(2)}) collective-permute-start(bf16[16,128,128]{2,1,0:T(8,128)(2,1)} %own_ref.1), channel_id=1, source_target_pairs={{0,4},{4,0},{8,12},{12,8},{16,20},{20,16},{24,28},{28,24},{32,36},... | collective-permute-start | bytes 1572872 | tf_op jit(solution)/shard_map/ppermute | solution.py:219
  8.8 0.0 copy-start.2
  8.8 0.7 copy-done.2
  9.5 0.7 ask.1
  10.2 10.9 %all-to-all-start = ((s32[64,1,128]{2,1,0:T(1,128)}), s32[64,1,128]{2,1,0:T(1,128)S(1)}, u32[]{:S(2)}, u32[]{:S(2)}) async-start(s32[64,1,128]{2,1,0:T(1,128)} %bitcast.3), calls=%async_computation | async-start | bytes 65536 | tf_op jit(solution)/shard_map/all_to_all | solution.py:199
  21.1 0.1 pad_add_fusion.place_ref
  21.2 0.0 collective-permute-done.3.other_ref
  21.2 0.0 copy-start
  21.2 1.0 copy-done
  22.3 0.9 prepare_integrals.1.tiles_ref
  23.1 8.7 %all-to-all-done = s32[64,1,128]{2,1,0:T(1,128)S(1)} async-done(((s32[64,1,128]{2,1,0:T(1,128)}), s32[64,1,128]{2,1,0:T(1,128)S(1)}, u32[]{:S(2)}, u32[]{:S(2)}) %all-to-all-start) | async-done | bytes 32800 | tf_op jit(solution)/shard_map/all_to_all | solution.py:199
  31.9 1.7 %pick.1 = bf16[64,64,128]{2,1,0:T(8,128)(2,1)} custom-call(s32[64,128]{1,0:T(8,128)S(1)} %bitcast.17, bf16[2,16,32,128]{3,2,1,0:T(8,128)(2,1)S(1)} %prepare_integrals.1.tiles_ref), custom_call_target="tpu_custom_call" | custom-call | tf_op jit(solution)/shard_map/pick/pallas_call | solution.py:229
  33.6 0.0 copy-start.1
  33.6 4.8 %all-to-all-start.1 = ((bf16[64,64,128]{2,1,0:T(8,128)(2,1)}), bf16[64,64,128]{2,1,0:T(8,128)(2,1)S(1)}, u32[]{:S(2)}, u32[]{:S(2)}) async-start(bf16[64,64,128]{2,1,0:T(8,128)(2,1)} %pick.1), calls=%async_computation.1 | async-start | bytes 2097152 | tf_op jit(solution)/shard_map/all_to_all | solution.py:242
  39.1 1.5 %read_tasks.1.refs_0_ = s32[1,128]{1,0:T(1,128)} custom-call(s32[1]{0:T(128)S(6)} %copy.9.live_ref, s32[16]{0:T(128)} %mask_ref.1, s32[4,128]{1,0:T(4,128)} %bitcast.18, s32[1,512]{1,0:T(1,128)} %bitcast.20), custom_call_target="tpu_custom_call" | custom-call | tf_op jit(solution)/shard_map/read_tasks/pallas_call | solution.py:202
  40.6 0.0 copy-start.3
  40.6 4.5 %collective-permute-start.2 = (s32[1,128]{1,0:T(1,128)}, s32[1,128]{1,0:T(1,128)S(1)}, u32[]{:S(2)}, u32[]{:S(2)}) collective-permute-start(s32[1,128]{1,0:T(1,128)} %read_tasks.1.refs_0_), channel_id=1, source_target_pairs={{0,3},{1,0},{2,1},{3,2},{4,7},{5,4},{6,5},{7,6},{8,11},{9,8},{10,9... | collective-permute-start | bytes 1544 | tf_op jit(solution)/shard_map/ppermute | solution.py:24
  45.1 2.4 %collective-permute-start.1 = (s32[1,128]{1,0:T(1,128)}, s32[1,128]{1,0:T(1,128)S(1)}, u32[]{:S(2)}, u32[]{:S(2)}) collective-permute-start(s32[1,128]{1,0:T(1,128)} %read_tasks.1.refs_0_), channel_id=1, source_target_pairs={{0,2},{1,3},{2,0},{3,1},{4,6},{5,7},{6,4},{7,5},{8,10},{9,11},{10,... | collective-permute-start | bytes 1544 | tf_op jit(solution)/shard_map/ppermute | solution.py:24
  47.5 2.5 %collective-permute-start = (s32[1,128]{1,0:T(1,128)}, s32[1,128]{1,0:T(1,128)S(1)}, u32[]{:S(2)}, u32[]{:S(2)}) collective-permute-start(s32[1,128]{1,0:T(1,128)} %read_tasks.1.refs_0_), channel_id=1, source_target_pairs={{0,1},{1,2},{2,3},{3,0},{4,5},{5,6},{6,7},{7,4},{8,9},{9,10},{10,1... | collective-permute-start | bytes 1544 | tf_op jit(solution)/shard_map/ppermute | solution.py:24
  50.1 0.0 copy-done.1
  50.1 0.2 prepare_lambda.1.refs_4_
  50.3 0.0 collective-permute-done.2.refs_3_
  50.3 1.0 collective-permute-done.1.refs_2_
  51.3 2.1 %collective-permute-done.refs_1_ = s32[1,128]{1,0:T(1,128)S(1)} collective-permute-done((s32[1,128]{1,0:T(1,128)}, s32[1,128]{1,0:T(1,128)S(1)}, u32[]{:S(2)}, u32[]{:S(2)}) %collective-permute-start) | collective-permute-done | bytes 544 | tf_op jit(solution)/shard_map/ppermute | solution.py:24
  53.5 11.5 %all-to-all-done.1 = bf16[64,64,128]{2,1,0:T(8,128)(2,1)S(1)} async-done(((bf16[64,64,128]{2,1,0:T(8,128)(2,1)}), bf16[64,64,128]{2,1,0:T(8,128)(2,1)S(1)}, u32[]{:S(2)}, u32[]{:S(2)}) %all-to-all-start.1) | async-done | bytes 1048608 | tf_op jit(solution)/shard_map/all_to_all | solution.py:242
  64.9 0.0 copy-done.3
  64.9 3.4 %contract.1 = s32[2176,128]{1,0:T(8,128)S(1)} custom-call(s32[1,128]{1,0:T(1,128)S(1)} %copy-done.3, s32[1,128]{1,0:T(1,128)S(1)} %collective-permute-done.refs_1_, s32[1,128]{1,0:T(1,128)S(1)} %collective-permute-done.1.refs_2_, s32[1,128]{1,0:T(1,128)S(1)} %collective-permute-done.2.refs_3_, bf16[33,128,128]{2,1,0:T(8,128)(2,1)S(1)} %prepare_lambda.1.refs_4_, ...), custom_call_target="tpu_custom_call" | custom-call | tf_op jit(solution)/shard_map/contract/pallas_call | solution.py:246
  68.3 37.2 %all_to_all.20 = s32[64,34,1,128]{3,2,1,0:T(1,128)S(1)} all-to-all(s32[64,34,1,128]{3,2,1,0:T(1,128)S(1)} %bitcast.13), channel_id=1, replica_groups={{0,8,16,24,32,40,48,56,64,72,80,88,96,104,112,120,128,136,144,152,160,1..., dimensions={0} | all-to-all | bytes 2228224 | tf_op jit(solution)/shard_map/all_to_all | solution.py:255
  105.5 1.0 add_slots.1
  106.5 13.2 %all_to_all.21.x_ref = f32[8,32,128]{2,1,0:T(8,128)S(1)} all-to-all(f32[8,32,128]{2,1,0:T(8,128)S(1)} %bitcast.16), channel_id=1, replica_groups={{0,1,2,3,4,5,6,7},{8,9,10,11,12,13,14,15},{16,17,18,19,20,21,22,23},{24..., dimensions={0} | all-to-all | bytes 262144 | tf_op jit(solution)/shard_map/all_to_all | solution.py:267
  119.7 0.7 finish.1
Async XLA Ops:
  0.0 21.2 %collective-permute-start.3 = (bf16[16,128,128]{2,1,0:T(8,128)(2,1)}, bf16[16,128,128]{2,1,0:T(8,128)(2,1)S(1)}, u32[]{:S(2)}, u32[]{:S(2)}) collective-permute-start(bf16[16,128,128]{2,1,0:T(8,128)(2,1)} %own_ref.1), channel_id=1, source_target_pairs={{0,4},{4,0},{8,12},{12,8},{16,20},{20,16},{24,28},{28,24},{32,36},... | collective-permute-start | bytes 1572872 | tf_op jit(solution)/shard_map/ppermute | solution.py:219
  8.8 0.7 copy-start.2
  10.2 21.7 %all-to-all-start = ((s32[64,1,128]{2,1,0:T(1,128)}), s32[64,1,128]{2,1,0:T(1,128)S(1)}, u32[]{:S(2)}, u32[]{:S(2)}) async-start(s32[64,1,128]{2,1,0:T(1,128)} %bitcast.3), calls=%async_computation | async-start | bytes 65536 | tf_op jit(solution)/shard_map/all_to_all | solution.py:199
  21.2 1.0 copy-start
  33.6 16.5 %copy-start.1 = (bf16[16,128,128]{2,1,0:T(8,128)(2,1)S(1)}, bf16[16,128,128]{2,1,0:T(8,128)(2,1)}, u32[]{:S(2)}) copy-start(bf16[16,128,128]{2,1,0:T(8,128)(2,1)} %lam_ref.1) | copy-start | bytes 1572868
  33.6 31.3 %all-to-all-start.1 = ((bf16[64,64,128]{2,1,0:T(8,128)(2,1)}), bf16[64,64,128]{2,1,0:T(8,128)(2,1)S(1)}, u32[]{:S(2)}, u32[]{:S(2)}) async-start(bf16[64,64,128]{2,1,0:T(8,128)(2,1)} %pick.1), calls=%async_computation.1 | async-start | bytes 2097152 | tf_op jit(solution)/shard_map/all_to_all | solution.py:242
  40.6 24.4 %copy-start.3 = (s32[1,128]{1,0:T(1,128)S(1)}, s32[1,128]{1,0:T(1,128)}, u32[]{:S(2)}) copy-start(s32[1,128]{1,0:T(1,128)} %read_tasks.1.refs_0_) | copy-start | bytes 1540
  40.6 9.7 %collective-permute-start.2 = (s32[1,128]{1,0:T(1,128)}, s32[1,128]{1,0:T(1,128)S(1)}, u32[]{:S(2)}, u32[]{:S(2)}) collective-permute-start(s32[1,128]{1,0:T(1,128)} %read_tasks.1.refs_0_), channel_id=1, source_target_pairs={{0,3},{1,0},{2,1},{3,2},{4,7},{5,4},{6,5},{7,6},{8,11},{9,8},{10,9... | collective-permute-start | bytes 1544 | tf_op jit(solution)/shard_map/ppermute | solution.py:24
  45.1 6.2 %collective-permute-start.1 = (s32[1,128]{1,0:T(1,128)}, s32[1,128]{1,0:T(1,128)S(1)}, u32[]{:S(2)}, u32[]{:S(2)}) collective-permute-start(s32[1,128]{1,0:T(1,128)} %read_tasks.1.refs_0_), channel_id=1, source_target_pairs={{0,2},{1,3},{2,0},{3,1},{4,6},{5,7},{6,4},{7,5},{8,10},{9,11},{10,... | collective-permute-start | bytes 1544 | tf_op jit(solution)/shard_map/ppermute | solution.py:24
  47.5 5.9 %collective-permute-start = (s32[1,128]{1,0:T(1,128)}, s32[1,128]{1,0:T(1,128)S(1)}, u32[]{:S(2)}, u32[]{:S(2)}) collective-permute-start(s32[1,128]{1,0:T(1,128)} %read_tasks.1.refs_0_), channel_id=1, source_target_pairs={{0,1},{1,2},{2,3},{3,0},{4,5},{5,6},{6,7},{7,4},{8,9},{9,10},{10,1... | collective-permute-start | bytes 1544 | tf_op jit(solution)/shard_map/ppermute | solution.py:24

commit v7 on v6

--- a/solution.py
+++ b/solution.py
@@ -8,7 +8,7 @@
 from jax.sharding import PartitionSpec as P
 
 VMEM = pl.BlockSpec(memory_space=pltpu.VMEM)
-OCTAVE = 256.0
+OCTAVE = 64.0
 FULL = 32760.0
 SMALLEST = 2.0**-110
 ROOM = pltpu.CompilerParams(vmem_limit_bytes=8 * 2**20)
@@ -112,11 +112,11 @@
 def contract(*refs, slots):
     *code_refs, lam_ref, w_ref, out_ref = refs
     peers, rows, edge = w_ref.shape
-    unroll = 64
-    words = rows // 2 + 1
-
-    def one(step, place):
-        owner = step * unroll + place
+    unroll = 32
+    half = rows // 2
+    words = rows + 1
+
+    def one(owner):
         codes = [ref[0, owner] for ref in code_refs]
         slot = lax.bitwise_and(codes[0], slots - 1)
         codes = [lax.shift_right_logical(code, power(slots)) for code in codes]
@@ -130,41 +130,48 @@
         top = jnp.max(jnp.abs(total), axis=0, keepdims=True)
         scale = jnp.ceil(jnp.log2(jnp.maximum(top, SMALLEST)) * OCTAVE)
         whole = jnp.round(total * (jnp.exp2(scale * (-1.0 / OCTAVE)) * FULL)).astype(jnp.int32)
-        first = pl.multiple_of(step * unroll * words, 8) + place * words
-        out_ref[pl.ds(first, rows // 2), :] = whole[: rows // 2] * 65536 + whole[rows // 2 :]
-        out_ref[pl.ds(first + rows // 2, 1), :] = scale.astype(jnp.int32) * slots + slot
+        return whole[:half] * 65536 + whole[half:], scale.astype(jnp.int32) * slots + slot
 
     def body(step, carry):
-        for k in range(unroll):
-            one(step, k)
+        for place in range(unroll):
+            first = pl.multiple_of(step * unroll * words, 8) + place * words
+            pairs, last = one((step * unroll + place) * 2)
+            out_ref[pl.ds(first, half), :] = pairs
+            pairs, other = one((step * unroll + place) * 2 + 1)
+            out_ref[pl.ds(first + half, half), :] = pairs
+            out_ref[pl.ds(first + rows, 1), :] = last * 65536 + other
         return carry
 
-    lax.fori_loop(0, peers // unroll, body, 0)
+    lax.fori_loop(0, peers // 2 // unroll, body, 0)
+
+
+def halves(pairs):
+    low = lax.shift_right_arithmetic(lax.shift_left(pairs, 16), 16)
+    return lax.shift_right_arithmetic(pairs - low, 16), low
 
 
 def add_slots(x_ref, out_ref):
     owners, slots, rows, edge = out_ref.shape
-    words = rows // 2 + 1
+    half = rows // 2
+    words = rows + 1
     unroll = 16
     zero = jnp.zeros((rows, edge), jnp.float32)
     for owner in range(owners):
 
         def body(step, sums):
             for k in range(unroll):
-                first = pl.multiple_of(step * unroll * owners * words, 8) + (k * owners + owner) * words
-                pairs = x_ref[pl.ds(first, rows // 2), :]
-                low = lax.shift_right_arithmetic(lax.shift_left(pairs, 16), 16)
-                high = lax.shift_right_arithmetic(pairs - low, 16)
-                last = x_ref[pl.ds(first + rows // 2, 1), :]
+                first = pl.multiple_of(step * unroll * words, 8) + k * words
+                value = jnp.concatenate(halves(x_ref[pl.ds(first + owner * half, half), :]), axis=0)
+                last = halves(x_ref[pl.ds(first + rows, 1), :])[owner]
                 slot = lax.bitwise_and(last, slots - 1)
                 scale = lax.shift_right_arithmetic(last, power(slots)).astype(jnp.float32)
                 scale = jnp.exp2(scale * (1.0 / OCTAVE)) * (1.0 / FULL)
-                value = jnp.concatenate([high, low], axis=0).astype(jnp.float32) * scale
+                value = value.astype(jnp.float32) * scale
                 mine = [jnp.broadcast_to(slot, (rows, edge)) == s for s in range(slots)]
                 sums = tuple(jnp.where(m, total + value, total) for m, total in zip(mine, sums))
             return sums
 
-        sums = lax.fori_loop(0, x_ref.shape[0] // (words * owners * unroll), body, (zero,) * slots)
+        sums = lax.fori_loop(0, x_ref.shape[0] // (words * unroll), body, (zero,) * slots)
         for s in range(slots):
             out_ref[owner, s] = sums[s]
 
@@ -183,7 +190,7 @@
     int_dev = int_tiles.shape[0]
     res_tile = owner_map.shape[0] // tile_devs
     rows = edge // reps
-    words = rows // 2 + 1
+    words = rows + 1
 
     tasks = task_list.T
     chips = tile_devs // 2
@@ -245,16 +252,16 @@
 
     totals = pl.pallas_call(
         functools.partial(contract, slots=res_tile),
-        out_shape=jax.ShapeDtypeStruct((tile_devs * words, edge), jnp.int32),
+        out_shape=jax.ShapeDtypeStruct((chips * words, edge), jnp.int32),
         in_specs=[SMEM] * reps + [VMEM, VMEM],
         out_specs=VMEM,
         compiler_params=ROOM,
         name="contract",
     )(*codes, lam_all, fetched)
-    totals = totals.reshape(chips, 2 * words, 1, edge)
+    totals = totals.reshape(chips, words, 1, edge)
     partial_tiles = lax.all_to_all(
         totals, "tiles", split_axis=0, concat_axis=0, tiled=True, axis_index_groups=same_core
-    ).reshape(tile_devs * words, edge)
+    ).reshape(chips * words, edge)
     summed = pl.pallas_call(
         add_slots,
         out_shape=jax.ShapeDtypeStruct((2, res_tile, rows, edge), jnp.float32),

time: 121 us -> 120 us (level)
  no operation moved by 1% of the time
where the time goes in v7:
time: 120 us
  blocking collectives  49.7 us (41%)
  starting transfers between devices  34 us (28%)
  waiting for transfers between devices  23.4 us (20%)
  Pallas kernels  10.2 us (8%)
  local copies, waits for them, and re-layouts  1.73 us (1%)
    all_to_all x1, blocking collectives, on_device(): lax.all_to_all(totals, 'tiles', split_axis=0, concat_axis=0, tiled=True,...  36.5 us
    all_to_all x1, blocking collectives, on_device(): lax.all_to_all(summed.reshape(2 * res_tile, rows, edge), ('tiles', 'rep')...  13.2 us
    all_to_all x1, waiting for transfers between devices, on_device(): lax.all_to_all(picked, 'tiles', split_axis=0, concat_axis=0, tiled=True,...  11.5 us
    all_to_all x1, starting transfers between devices, on_device(): lax.all_to_all(request.reshape(chips, 1, 128), 'tiles', split_axis=0, con...  10.9 us
    ppermute x3, starting transfers between devices, ring(): lax.ppermute(values, 'rep', [(i, (i + steps) % reps) for i in range(reps)])  9.45 us
    ppermute x1, starting transfers between devices, on_device(): lax.ppermute(int_tiles, 'tiles', [(i, i ^ 1) for i in range(tile_devs)])  8.78 us
    all_to_all x1, waiting for transfers between devices, on_device(): lax.all_to_all(request.reshape(chips, 1, 128), 'tiles', split_axis=0, con...  8.75 us
    all_to_all x1, starting transfers between devices, on_device(): lax.all_to_all(picked, 'tiles', split_axis=0, concat_axis=0, tiled=True,...  4.8 us
  transfers between devices with their start and end apart: 6, of which 4 were waited for; matrix products, arithmetic and copies ran while one was open for 0% of the time, Pallas kernels for 3%

profile of v7, /device:TPU:1, one launch (start us, length us, event | category | flops | bytes accessed | tf_op | source)
XLA Modules:
  0.0 119.8 jit_solution(4857509558639169036)
XLA Ops:
  0.0 8.8 %collective-permute-start.3 = (bf16[16,128,128]{2,1,0:T(8,128)(2,1)}, bf16[16,128,128]{2,1,0:T(8,128)(2,1)S(1)}, u32[]{:S(2)}, u32[]{:S(2)}) collective-permute-start(bf16[16,128,128]{2,1,0:T(8,128)(2,1)} %own_ref.1), channel_id=1, source_target_pairs={{0,4},{4,0},{8,12},{12,8},{16,20},{20,16},{24,28},{28,24},{32,36},... | collective-permute-start | bytes 1572872 | tf_op jit(solution)/shard_map/ppermute | solution.py:226
  8.8 0.0 copy-start.2
  8.8 0.7 copy-done.2
  9.5 0.7 ask.1
  10.2 10.9 %all-to-all-start = ((s32[64,1,128]{2,1,0:T(1,128)}), s32[64,1,128]{2,1,0:T(1,128)S(1)}, u32[]{:S(2)}, u32[]{:S(2)}) async-start(s32[64,1,128]{2,1,0:T(1,128)} %bitcast.3), calls=%async_computation | async-start | bytes 65536 | tf_op jit(solution)/shard_map/all_to_all | solution.py:206
  21.1 0.1 pad_add_fusion.place_ref
  21.2 0.0 collective-permute-done.3.other_ref
  21.2 0.0 copy-start
  21.2 1.0 copy-done
  22.3 0.9 prepare_integrals.1.tiles_ref
  23.1 8.7 %all-to-all-done = s32[64,1,128]{2,1,0:T(1,128)S(1)} async-done(((s32[64,1,128]{2,1,0:T(1,128)}), s32[64,1,128]{2,1,0:T(1,128)S(1)}, u32[]{:S(2)}, u32[]{:S(2)}) %all-to-all-start) | async-done | bytes 32800 | tf_op jit(solution)/shard_map/all_to_all | solution.py:206
  31.9 1.7 %pick.1 = bf16[64,64,128]{2,1,0:T(8,128)(2,1)} custom-call(s32[64,128]{1,0:T(8,128)S(1)} %bitcast.17, bf16[2,16,32,128]{3,2,1,0:T(8,128)(2,1)S(1)} %prepare_integrals.1.tiles_ref), custom_call_target="tpu_custom_call" | custom-call | tf_op jit(solution)/shard_map/pick/pallas_call | solution.py:236
  33.6 0.0 copy-start.1
  33.6 4.8 %all-to-all-start.1 = ((bf16[64,64,128]{2,1,0:T(8,128)(2,1)}), bf16[64,64,128]{2,1,0:T(8,128)(2,1)S(1)}, u32[]{:S(2)}, u32[]{:S(2)}) async-start(bf16[64,64,128]{2,1,0:T(8,128)(2,1)} %pick.1), calls=%async_computation.1 | async-start | bytes 2097152 | tf_op jit(solution)/shard_map/all_to_all | solution.py:249
  39.1 1.5 %read_tasks.1.refs_0_ = s32[1,128]{1,0:T(1,128)} custom-call(s32[1]{0:T(128)S(6)} %copy.9.live_ref, s32[16]{0:T(128)} %mask_ref.1, s32[4,128]{1,0:T(4,128)} %bitcast.18, s32[1,512]{1,0:T(1,128)} %bitcast.20), custom_call_target="tpu_custom_call" | custom-call | tf_op jit(solution)/shard_map/read_tasks/pallas_call | solution.py:209
  40.6 0.0 copy-start.3
  40.6 4.5 %collective-permute-start.2 = (s32[1,128]{1,0:T(1,128)}, s32[1,128]{1,0:T(1,128)S(1)}, u32[]{:S(2)}, u32[]{:S(2)}) collective-permute-start(s32[1,128]{1,0:T(1,128)} %read_tasks.1.refs_0_), channel_id=1, source_target_pairs={{0,3},{1,0},{2,1},{3,2},{4,7},{5,4},{6,5},{7,6},{8,11},{9,8},{10,9... | collective-permute-start | bytes 1544 | tf_op jit(solution)/shard_map/ppermute | solution.py:24
  45.1 2.4 %collective-permute-start.1 = (s32[1,128]{1,0:T(1,128)}, s32[1,128]{1,0:T(1,128)S(1)}, u32[]{:S(2)}, u32[]{:S(2)}) collective-permute-start(s32[1,128]{1,0:T(1,128)} %read_tasks.1.refs_0_), channel_id=1, source_target_pairs={{0,2},{1,3},{2,0},{3,1},{4,6},{5,7},{6,4},{7,5},{8,10},{9,11},{10,... | collective-permute-start | bytes 1544 | tf_op jit(solution)/shard_map/ppermute | solution.py:24
  47.5 2.5 %collective-permute-start = (s32[1,128]{1,0:T(1,128)}, s32[1,128]{1,0:T(1,128)S(1)}, u32[]{:S(2)}, u32[]{:S(2)}) collective-permute-start(s32[1,128]{1,0:T(1,128)} %read_tasks.1.refs_0_), channel_id=1, source_target_pairs={{0,1},{1,2},{2,3},{3,0},{4,5},{5,6},{6,7},{7,4},{8,9},{9,10},{10,1... | collective-permute-start | bytes 1544 | tf_op jit(solution)/shard_map/ppermute | solution.py:24
  50.1 0.0 copy-done.1
  50.1 0.2 prepare_lambda.1.refs_4_
  50.3 0.0 collective-permute-done.2.refs_3_
  50.3 1.0 collective-permute-done.1.refs_2_
  51.3 2.1 %collective-permute-done.refs_1_ = s32[1,128]{1,0:T(1,128)S(1)} collective-permute-done((s32[1,128]{1,0:T(1,128)}, s32[1,128]{1,0:T(1,128)S(1)}, u32[]{:S(2)}, u32[]{:S(2)}) %collective-permute-start) | collective-permute-done | bytes 544 | tf_op jit(solution)/shard_map/ppermute | solution.py:24
  53.5 11.5 %all-to-all-done.1 = bf16[64,64,128]{2,1,0:T(8,128)(2,1)S(1)} async-done(((bf16[64,64,128]{2,1,0:T(8,128)(2,1)}), bf16[64,64,128]{2,1,0:T(8,128)(2,1)S(1)}, u32[]{:S(2)}, u32[]{:S(2)}) %all-to-all-start.1) | async-done | bytes 1048608 | tf_op jit(solution)/shard_map/all_to_all | solution.py:249
  64.9 0.0 copy-done.3
  64.9 3.4 %contract.1 = s32[2112,128]{1,0:T(8,128)S(1)} custom-call(s32[1,128]{1,0:T(1,128)S(1)} %copy-done.3, s32[1,128]{1,0:T(1,128)S(1)} %collective-permute-done.refs_1_, s32[1,128]{1,0:T(1,128)S(1)} %collective-permute-done.1.refs_2_, s32[1,128]{1,0:T(1,128)S(1)} %collective-permute-done.2.refs_3_, bf16[33,128,128]{2,1,0:T(8,128)(2,1)S(1)} %prepare_lambda.1.refs_4_, ...), custom_call_target="tpu_custom_call" | custom-call | tf_op jit(solution)/shard_map/contract/pallas_call | solution.py:253
  68.3 36.5 %all_to_all.20 = s32[64,33,1,128]{3,2,1,0:T(1,128)S(1)} all-to-all(s32[64,33,1,128]{3,2,1,0:T(1,128)S(1)} %bitcast.14), channel_id=1, replica_groups={{0,8,16,24,32,40,48,56,64,72,80,88,96,104,112,120,128,136,144,152,160,1..., dimensions={0} | all-to-all | bytes 2162688 | tf_op jit(solution)/shard_map/all_to_all | solution.py:262
  104.8 1.1 add_slots.1
  105.9 13.2 %all_to_all.21.x_ref = f32[8,32,128]{2,1,0:T(8,128)S(1)} all-to-all(f32[8,32,128]{2,1,0:T(8,128)S(1)} %bitcast.16), channel_id=1, replica_groups={{0,1,2,3,4,5,6,7},{8,9,10,11,12,13,14,15},{16,17,18,19,20,21,22,23},{24..., dimensions={0} | all-to-all | bytes 262144 | tf_op jit(solution)/shard_map/all_to_all | solution.py:274
  119.1 0.7 finish.1
Async XLA Ops:
  0.0 21.2 %collective-permute-start.3 = (bf16[16,128,128]{2,1,0:T(8,128)(2,1)}, bf16[16,128,128]{2,1,0:T(8,128)(2,1)S(1)}, u32[]{:S(2)}, u32[]{:S(2)}) collective-permute-start(bf16[16,128,128]{2,1,0:T(8,128)(2,1)} %own_ref.1), channel_id=1, source_target_pairs={{0,4},{4,0},{8,12},{12,8},{16,20},{20,16},{24,28},{28,24},{32,36},... | collective-permute-start | bytes 1572872 | tf_op jit(solution)/shard_map/ppermute | solution.py:226
  8.8 0.7 copy-start.2
  10.2 21.7 %all-to-all-start = ((s32[64,1,128]{2,1,0:T(1,128)}), s32[64,1,128]{2,1,0:T(1,128)S(1)}, u32[]{:S(2)}, u32[]{:S(2)}) async-start(s32[64,1,128]{2,1,0:T(1,128)} %bitcast.3), calls=%async_computation | async-start | bytes 65536 | tf_op jit(solution)/shard_map/all_to_all | solution.py:206
  21.2 1.0 copy-start
  33.6 16.5 %copy-start.1 = (bf16[16,128,128]{2,1,0:T(8,128)(2,1)S(1)}, bf16[16,128,128]{2,1,0:T(8,128)(2,1)}, u32[]{:S(2)}) copy-start(bf16[16,128,128]{2,1,0:T(8,128)(2,1)} %lam_ref.1) | copy-start | bytes 1572868
  33.6 31.3 %all-to-all-start.1 = ((bf16[64,64,128]{2,1,0:T(8,128)(2,1)}), bf16[64,64,128]{2,1,0:T(8,128)(2,1)S(1)}, u32[]{:S(2)}, u32[]{:S(2)}) async-start(bf16[64,64,128]{2,1,0:T(8,128)(2,1)} %pick.1), calls=%async_computation.1 | async-start | bytes 2097152 | tf_op jit(solution)/shard_map/all_to_all | solution.py:249
  40.6 24.4 %copy-start.3 = (s32[1,128]{1,0:T(1,128)S(1)}, s32[1,128]{1,0:T(1,128)}, u32[]{:S(2)}) copy-start(s32[1,128]{1,0:T(1,128)} %read_tasks.1.refs_0_) | copy-start | bytes 1540
  40.6 9.7 %collective-permute-start.2 = (s32[1,128]{1,0:T(1,128)}, s32[1,128]{1,0:T(1,128)S(1)}, u32[]{:S(2)}, u32[]{:S(2)}) collective-permute-start(s32[1,128]{1,0:T(1,128)} %read_tasks.1.refs_0_), channel_id=1, source_target_pairs={{0,3},{1,0},{2,1},{3,2},{4,7},{5,4},{6,5},{7,6},{8,11},{9,8},{10,9... | collective-permute-start | bytes 1544 | tf_op jit(solution)/shard_map/ppermute | solution.py:24
  45.1 6.2 %collective-permute-start.1 = (s32[1,128]{1,0:T(1,128)}, s32[1,128]{1,0:T(1,128)S(1)}, u32[]{:S(2)}, u32[]{:S(2)}) collective-permute-start(s32[1,128]{1,0:T(1,128)} %read_tasks.1.refs_0_), channel_id=1, source_target_pairs={{0,2},{1,3},{2,0},{3,1},{4,6},{5,7},{6,4},{7,5},{8,10},{9,11},{10,... | collective-permute-start | bytes 1544 | tf_op jit(solution)/shard_map/ppermute | solution.py:24
  47.5 5.9 %collective-permute-start = (s32[1,128]{1,0:T(1,128)}, s32[1,128]{1,0:T(1,128)S(1)}, u32[]{:S(2)}, u32[]{:S(2)}) collective-permute-start(s32[1,128]{1,0:T(1,128)} %read_tasks.1.refs_0_), channel_id=1, source_target_pairs={{0,1},{1,2},{2,3},{3,0},{4,5},{5,6},{6,7},{7,4},{8,9},{9,10},{10,1... | collective-permute-start | bytes 1544 | tf_op jit(solution)/shard_map/ppermute | solution.py:24

commit v8 on v7

--- a/solution.py
+++ b/solution.py
@@ -88,31 +88,34 @@
     code_ref[...] = (by_owner[0:1, :] * peers + by_owner[1:2, :]) * res_tile + by_owner[2:3, :]
 
 
-def pick(request_ref, tiles_ref, out_ref, row, asked, sem):
-    peers, both, edge = out_ref.shape
+def pick(request_ref, tiles_ref, out_ref, filled, row, asked, sem, sent):
+    peers, both, edge = filled.shape
     _, int_dev, rows, _ = tiles_ref.shape
+    parts = sent.shape[0]
+    share = peers // parts
     got = request_ref[...]
     diagonal = lax.broadcasted_iota(jnp.int32, got.shape, 0) == lax.broadcasted_iota(jnp.int32, got.shape, 1)
     row[...] = jnp.sum(jnp.where(diagonal, got, 0), axis=0, keepdims=True)
     copy = pltpu.make_async_copy(row, asked, sem)
     copy.start()
     copy.wait()
-
-    def body(step, carry):
-        for k in range(16):
-            peer = step * 16 + k
+    copies = []
+    for part in range(parts):
+        for peer in range(part * share, (part + 1) * share):
             word = asked[0, peer]
-            out_ref[peer, :rows] = tiles_ref[0, lax.bitwise_and(word, int_dev - 1)]
-            out_ref[peer, rows:] = tiles_ref[1, lax.shift_right_logical(word, power(int_dev))]
-        return carry
-
-    lax.fori_loop(0, peers // 16, body, 0)
+            filled[peer, :rows] = tiles_ref[0, lax.bitwise_and(word, int_dev - 1)]
+            filled[peer, rows:] = tiles_ref[1, lax.shift_right_logical(word, power(int_dev))]
+        piece = pl.ds(part * share, share)
+        copies.append(pltpu.make_async_copy(filled.at[piece], out_ref.at[piece], sent.at[part]))
+        copies[-1].start()
+    for copy in copies:
+        copy.wait()
 
 
 def contract(*refs, slots):
     *code_refs, lam_ref, w_ref, out_ref = refs
     peers, rows, edge = w_ref.shape
-    unroll = 32
+    unroll = 64
     half = rows // 2
     words = rows + 1
 
@@ -211,6 +214,7 @@
         out_shape=jax.ShapeDtypeStruct((1, tile_devs), jnp.int32),
         in_specs=[SMEM, SMEM, VMEM, VMEM],
         out_specs=VMEM,
+        compiler_params=ROOM,
         name="read_tasks",
     )(live_count, tile_mask, tasks, owner_map[None, :])
     codes = [code] + [ring(code, k) for k in range(1, reps)]
@@ -237,11 +241,13 @@
         pick,
         out_shape=jax.ShapeDtypeStruct((chips, 2 * rows, edge), jnp.bfloat16),
         in_specs=[VMEM, VMEM],
-        out_specs=VMEM,
+        out_specs=pl.BlockSpec(memory_space=pltpu.HBM),
         scratch_shapes=[
+            pltpu.VMEM((chips, 2 * rows, edge), jnp.bfloat16),
             pltpu.VMEM((1, 128), jnp.int32),
             pltpu.SMEM((1, 128), jnp.int32),
             pltpu.SemaphoreType.DMA,
+            pltpu.SemaphoreType.DMA((4,)),
         ],
         compiler_params=ROOM,
         name="pick",

time: 120 us -> 120 us (level)
  transfers between devices with their start and end apart: 6 -> 6, of which waited for: 4 -> 4; matrix products, arithmetic and copies ran while one was open for 0% -> 0% of each run, Pallas kernels for 3% -> 2%
where the time goes in v8:
time: 120 us
  blocking collectives  49.7 us (41%)
  starting transfers between devices  33.8 us (28%)
  waiting for transfers between devices  24.2 us (20%)
  Pallas kernels  9.55 us (8%)
  local copies, waits for them, and re-layouts  1.74 us (1%)
    all_to_all x1, blocking collectives, on_device(): lax.all_to_all(totals, 'tiles', split_axis=0, concat_axis=0, tiled=True,...  36.5 us
    all_to_all x1, blocking collectives, on_device(): lax.all_to_all(summed.reshape(2 * res_tile, rows, edge), ('tiles', 'rep')...  13.2 us
    all_to_all x1, waiting for transfers between devices, on_device(): lax.all_to_all(picked, 'tiles', split_axis=0, concat_axis=0, tiled=True,...  12.4 us
    all_to_all x1, starting transfers between devices, on_device(): lax.all_to_all(request.reshape(chips, 1, 128), 'tiles', split_axis=0, con...  10.9 us
    ppermute x3, starting transfers between devices, ring(): lax.ppermute(values, 'rep', [(i, (i + steps) % reps) for i in range(reps)])  9.34 us
    ppermute x1, starting transfers between devices, on_device(): lax.ppermute(int_tiles, 'tiles', [(i, i ^ 1) for i in range(tile_devs)])  8.78 us
    all_to_all x1, waiting for transfers between devices, on_device(): lax.all_to_all(request.reshape(chips, 1, 128), 'tiles', split_axis=0, con...  8.75 us
    all_to_all x1, starting transfers between devices, on_device(): lax.all_to_all(picked, 'tiles', split_axis=0, concat_axis=0, tiled=True,...  4.8 us
  transfers between devices with their start and end apart: 6, of which 4 were waited for; matrix products, arithmetic and copies ran while one was open for 0% of the time, Pallas kernels for 2%

profile of v8, /device:TPU:1, one launch (start us, length us, event | category | flops | bytes accessed | tf_op | source)
XLA Modules:
  0.0 119.9 jit_solution(17252651217437280789)
XLA Ops:
  0.0 8.8 %collective-permute-start.3 = (bf16[16,128,128]{2,1,0:T(8,128)(2,1)}, bf16[16,128,128]{2,1,0:T(8,128)(2,1)S(1)}, u32[]{:S(2)}, u32[]{:S(2)}) collective-permute-start(bf16[16,128,128]{2,1,0:T(8,128)(2,1)} %own_ref.1), channel_id=1, source_target_pairs={{0,4},{4,0},{8,12},{12,8},{16,20},{20,16},{24,28},{28,24},{32,36},... | collective-permute-start | bytes 1572872 | tf_op jit(solution)/shard_map/ppermute | solution.py:230
  8.8 0.0 copy-start.2
  8.8 0.7 copy-done.2
  9.5 0.7 ask.1
  10.2 10.9 %all-to-all-start = ((s32[64,1,128]{2,1,0:T(1,128)}), s32[64,1,128]{2,1,0:T(1,128)S(1)}, u32[]{:S(2)}, u32[]{:S(2)}) async-start(s32[64,1,128]{2,1,0:T(1,128)} %bitcast.3), calls=%async_computation | async-start | bytes 65536 | tf_op jit(solution)/shard_map/all_to_all | solution.py:209
  21.1 0.1 pad_add_fusion.place_ref
  21.2 0.0 collective-permute-done.3.other_ref
  21.2 0.0 copy-start
  21.2 1.0 copy-done
  22.3 0.9 prepare_integrals.1.tiles_ref
  23.1 8.7 %all-to-all-done = s32[64,1,128]{2,1,0:T(1,128)S(1)} async-done(((s32[64,1,128]{2,1,0:T(1,128)}), s32[64,1,128]{2,1,0:T(1,128)S(1)}, u32[]{:S(2)}, u32[]{:S(2)}) %all-to-all-start) | async-done | bytes 32800 | tf_op jit(solution)/shard_map/all_to_all | solution.py:209
  31.9 1.6 %pick.1 = bf16[64,64,128]{2,1,0:T(8,128)(2,1)} custom-call(s32[64,128]{1,0:T(8,128)S(1)} %bitcast.17, bf16[2,16,32,128]{3,2,1,0:T(8,128)(2,1)S(1)} %prepare_integrals.1.tiles_ref), custom_call_target="tpu_custom_call" | custom-call | tf_op jit(solution)/shard_map/pick/pallas_call | solution.py:240
  33.5 0.0 copy-start.3
  33.5 0.0 copy-start.4
  33.5 0.0 copy-start.5
  33.5 0.0 copy-start.1
  33.6 4.8 %all-to-all-start.1 = ((bf16[64,64,128]{2,1,0:T(8,128)(2,1)}), bf16[64,64,128]{2,1,0:T(8,128)(2,1)S(1)}, u32[]{:S(2)}, u32[]{:S(2)}) async-start(bf16[64,64,128]{2,1,0:T(8,128)(2,1)} %pick.1), calls=%async_computation.1 | async-start | bytes 2097152 | tf_op jit(solution)/shard_map/all_to_all | solution.py:255
  39.0 0.0 copy-done.3
  39.0 0.0 copy-done.4
  39.0 0.0 copy-done.5
  39.0 0.8 read_tasks.1.refs_0_
  39.9 4.4 %collective-permute-start.2 = (s32[1,128]{1,0:T(1,128)S(1)}, s32[1,128]{1,0:T(1,128)S(1)}, u32[]{:S(2)}, u32[]{:S(2)}) collective-permute-start(s32[1,128]{1,0:T(1,128)S(1)} %read_tasks.1.refs_0_), channel_id=1, source_target_pairs={{0,3},{1,0},{2,1},{3,2},{4,7},{5,4},{6,5},{7,6},{8,11},{9,8},{10,9... | collective-permute-start | bytes 1544 | tf_op jit(solution)/shard_map/ppermute | solution.py:24
  44.3 2.4 %collective-permute-start.1 = (s32[1,128]{1,0:T(1,128)S(1)}, s32[1,128]{1,0:T(1,128)S(1)}, u32[]{:S(2)}, u32[]{:S(2)}) collective-permute-start(s32[1,128]{1,0:T(1,128)S(1)} %read_tasks.1.refs_0_), channel_id=1, source_target_pairs={{0,2},{1,3},{2,0},{3,1},{4,6},{5,7},{6,4},{7,5},{8,10},{9,11},{10,... | collective-permute-start | bytes 1544 | tf_op jit(solution)/shard_map/ppermute | solution.py:24
  46.7 2.5 %collective-permute-start = (s32[1,128]{1,0:T(1,128)S(1)}, s32[1,128]{1,0:T(1,128)S(1)}, u32[]{:S(2)}, u32[]{:S(2)}) collective-permute-start(s32[1,128]{1,0:T(1,128)S(1)} %read_tasks.1.refs_0_), channel_id=1, source_target_pairs={{0,1},{1,2},{2,3},{3,0},{4,5},{5,6},{6,7},{7,4},{8,9},{9,10},{10,1... | collective-permute-start | bytes 1544 | tf_op jit(solution)/shard_map/ppermute | solution.py:24
  49.2 0.0 copy-done.1
  49.2 0.2 prepare_lambda.1.refs_4_
  49.4 0.0 collective-permute-done.2.refs_3_
  49.4 0.9 collective-permute-done.1.refs_2_
  50.4 2.1 %collective-permute-done.refs_1_ = s32[1,128]{1,0:T(1,128)S(1)} collective-permute-done((s32[1,128]{1,0:T(1,128)S(1)}, s32[1,128]{1,0:T(1,128)S(1)}, u32[]{:S(2)}, u32[]{:S(2)}) %collective-permute-start) | collective-permute-done | bytes 544 | tf_op jit(solution)/shard_map/ppermute | solution.py:24
  52.5 12.4 %all-to-all-done.1 = bf16[64,64,128]{2,1,0:T(8,128)(2,1)S(1)} async-done(((bf16[64,64,128]{2,1,0:T(8,128)(2,1)}), bf16[64,64,128]{2,1,0:T(8,128)(2,1)S(1)}, u32[]{:S(2)}, u32[]{:S(2)}) %all-to-all-start.1) | async-done | bytes 1048608 | tf_op jit(solution)/shard_map/all_to_all | solution.py:255
  64.9 3.5 %contract.1 = s32[2112,128]{1,0:T(8,128)S(1)} custom-call(s32[1,128]{1,0:T(1,128)S(1)} %read_tasks.1.refs_0_, s32[1,128]{1,0:T(1,128)S(1)} %collective-permute-done.refs_1_, s32[1,128]{1,0:T(1,128)S(1)} %collective-permute-done.1.refs_2_, s32[1,128]{1,0:T(1,128)S(1)} %collective-permute-done.2.refs_3_, bf16[33,128,128]{2,1,0:T(8,128)(2,1)S(1)} %prepare_lambda.1.refs_4_, ...), custom_call_target="tpu_custom_call" | custom-call | tf_op jit(solution)/shard_map/contract/pallas_call | solution.py:259
  68.4 36.5 %all_to_all.20 = s32[64,33,1,128]{3,2,1,0:T(1,128)S(1)} all-to-all(s32[64,33,1,128]{3,2,1,0:T(1,128)S(1)} %bitcast.14), channel_id=1, replica_groups={{0,8,16,24,32,40,48,56,64,72,80,88,96,104,112,120,128,136,144,152,160,1..., dimensions={0} | all-to-all | bytes 2162688 | tf_op jit(solution)/shard_map/all_to_all | solution.py:268
  104.9 1.1 add_slots.1
  106.0 13.2 %all_to_all.21.x_ref = f32[8,32,128]{2,1,0:T(8,128)S(1)} all-to-all(f32[8,32,128]{2,1,0:T(8,128)S(1)} %bitcast.16), channel_id=1, replica_groups={{0,1,2,3,4,5,6,7},{8,9,10,11,12,13,14,15},{16,17,18,19,20,21,22,23},{24..., dimensions={0} | all-to-all | bytes 262144 | tf_op jit(solution)/shard_map/all_to_all | solution.py:280
  119.2 0.7 finish.1
Async XLA Ops:
  0.0 21.2 %collective-permute-start.3 = (bf16[16,128,128]{2,1,0:T(8,128)(2,1)}, bf16[16,128,128]{2,1,0:T(8,128)(2,1)S(1)}, u32[]{:S(2)}, u32[]{:S(2)}) collective-permute-start(bf16[16,128,128]{2,1,0:T(8,128)(2,1)} %own_ref.1), channel_id=1, source_target_pairs={{0,4},{4,0},{8,12},{12,8},{16,20},{20,16},{24,28},{28,24},{32,36},... | collective-permute-start | bytes 1572872 | tf_op jit(solution)/shard_map/ppermute | solution.py:230
  8.8 0.7 copy-start.2
  10.2 21.7 %all-to-all-start = ((s32[64,1,128]{2,1,0:T(1,128)}), s32[64,1,128]{2,1,0:T(1,128)S(1)}, u32[]{:S(2)}, u32[]{:S(2)}) async-start(s32[64,1,128]{2,1,0:T(1,128)} %bitcast.3), calls=%async_computation | async-start | bytes 65536 | tf_op jit(solution)/shard_map/all_to_all | solution.py:209
  21.2 1.0 copy-start
  33.5 5.5 %copy-start.3 = (s32[128,4]{0,1:T(4,128)S(1)}, s32[128,4]{0,1:T(4,128)}, u32[]{:S(2)}) copy-start(s32[128,4]{0,1:T(4,128)} %param.8) | copy-start | bytes 6148
  33.5 5.5 %copy-start.4 = (s32[512]{0:T(512)S(1)}, s32[512]{0:T(512)}, u32[]{:S(2)}) copy-start(s32[512]{0:T(512)} %param.11) | copy-start | bytes 6148
  33.5 5.5 %copy-start.5 = (s32[16]{0:T(128)S(1)}, s32[16]{0:T(128)}, u32[]{:S(2)}) copy-start(s32[16]{0:T(128)} %mask_ref.1) | copy-start | bytes 196
  33.5 15.7 %copy-start.1 = (bf16[16,128,128]{2,1,0:T(8,128)(2,1)S(1)}, bf16[16,128,128]{2,1,0:T(8,128)(2,1)}, u32[]{:S(2)}) copy-start(bf16[16,128,128]{2,1,0:T(8,128)(2,1)} %lam_ref.1) | copy-start | bytes 1572868
  33.6 31.3 %all-to-all-start.1 = ((bf16[64,64,128]{2,1,0:T(8,128)(2,1)}), bf16[64,64,128]{2,1,0:T(8,128)(2,1)S(1)}, u32[]{:S(2)}, u32[]{:S(2)}) async-start(bf16[64,64,128]{2,1,0:T(8,128)(2,1)} %pick.1), calls=%async_computation.1 | async-start | bytes 2097152 | tf_op jit(solution)/shard_map/all_to_all | solution.py:255
  39.9 9.6 %collective-permute-start.2 = (s32[1,128]{1,0:T(1,128)S(1)}, s32[1,128]{1,0:T(1,128)S(1)}, u32[]{:S(2)}, u32[]{:S(2)}) collective-permute-start(s32[1,128]{1,0:T(1,128)S(1)} %read_tasks.1.refs_0_), channel_id=1, source_target_pairs={{0,3},{1,0},{2,1},{3,2},{4,7},{5,4},{6,5},{7,6},{8,11},{9,8},{10,9... | collective-permute-start | bytes 1544 | tf_op jit(solution)/shard_map/ppermute | solution.py:24
  44.3 6.1 %collective-permute-start.1 = (s32[1,128]{1,0:T(1,128)S(1)}, s32[1,128]{1,0:T(1,128)S(1)}, u32[]{:S(2)}, u32[]{:S(2)}) collective-permute-start(s32[1,128]{1,0:T(1,128)S(1)} %read_tasks.1.refs_0_), channel_id=1, source_target_pairs={{0,2},{1,3},{2,0},{3,1},{4,6},{5,7},{6,4},{7,5},{8,10},{9,11},{10,... | collective-permute-start | bytes 1544 | tf_op jit(solution)/shard_map/ppermute | solution.py:24
  46.7 5.8 %collective-permute-start = (s32[1,128]{1,0:T(1,128)S(1)}, s32[1,128]{1,0:T(1,128)S(1)}, u32[]{:S(2)}, u32[]{:S(2)}) collective-permute-start(s32[1,128]{1,0:T(1,128)S(1)} %read_tasks.1.refs_0_), channel_id=1, source_target_pairs={{0,1},{1,2},{2,3},{3,0},{4,5},{5,6},{6,7},{7,4},{8,9},{9,10},{10,1... | collective-permute-start | bytes 1544 | tf_op jit(solution)/shard_map/ppermute | solution.py:24

commit v9 on v7

--- a/solution.py
+++ b/solution.py
@@ -154,7 +154,7 @@
     owners, slots, rows, edge = out_ref.shape
     half = rows // 2
     words = rows + 1
-    unroll = 16
+    unroll = 32
     zero = jnp.zeros((rows, edge), jnp.float32)
     for owner in range(owners):
 
@@ -211,6 +211,7 @@
         out_shape=jax.ShapeDtypeStruct((1, tile_devs), jnp.int32),
         in_specs=[SMEM, SMEM, VMEM, VMEM],
         out_specs=VMEM,
+        compiler_params=ROOM,
         name="read_tasks",
     )(live_count, tile_mask, tasks, owner_map[None, :])
     codes = [code] + [ring(code, k) for k in range(1, reps)]

time: 120 us -> 120 us (level)
  transfers between devices with their start and end apart: 6 -> 6, of which waited for: 4 -> 4; matrix products, arithmetic and copies ran while one was open for 0% -> 0% of each run, Pallas kernels for 3% -> 2%
where the time goes in v9:
time: 120 us
  blocking collectives  49.7 us (41%)
  starting transfers between devices  33.8 us (28%)
  waiting for transfers between devices  24.2 us (20%)
  Pallas kernels  9.49 us (8%)
  local copies, waits for them, and re-layouts  1.74 us (1%)
    all_to_all x1, blocking collectives, on_device(): lax.all_to_all(totals, 'tiles', split_axis=0, concat_axis=0, tiled=True,...  36.5 us
    all_to_all x1, blocking collectives, on_device(): lax.all_to_all(summed.reshape(2 * res_tile, rows, edge), ('tiles', 'rep')...  13.2 us
    all_to_all x1, waiting for transfers between devices, on_device(): lax.all_to_all(picked, 'tiles', split_axis=0, concat_axis=0, tiled=True,...  12.4 us
    all_to_all x1, starting transfers between devices, on_device(): lax.all_to_all(request.reshape(chips, 1, 128), 'tiles', split_axis=0, con...  10.9 us
    ppermute x3, starting transfers between devices, ring(): lax.ppermute(values, 'rep', [(i, (i + steps) % reps) for i in range(reps)])  9.34 us
    ppermute x1, starting transfers between devices, on_device(): lax.ppermute(int_tiles, 'tiles', [(i, i ^ 1) for i in range(tile_devs)])  8.78 us
    all_to_all x1, waiting for transfers between devices, on_device(): lax.all_to_all(request.reshape(chips, 1, 128), 'tiles', split_axis=0, con...  8.75 us
    all_to_all x1, starting transfers between devices, on_device(): lax.all_to_all(picked, 'tiles', split_axis=0, concat_axis=0, tiled=True,...  4.8 us
  transfers between devices with their start and end apart: 6, of which 4 were waited for; matrix products, arithmetic and copies ran while one was open for 0% of the time, Pallas kernels for 2%

profile of v9, /device:TPU:1, one launch (start us, length us, event | category | flops | bytes accessed | tf_op | source)
XLA Modules:
  0.0 119.8 jit_solution(14446486653513646156)
XLA Ops:
  0.0 8.8 %collective-permute-start.3 = (bf16[16,128,128]{2,1,0:T(8,128)(2,1)}, bf16[16,128,128]{2,1,0:T(8,128)(2,1)S(1)}, u32[]{:S(2)}, u32[]{:S(2)}) collective-permute-start(bf16[16,128,128]{2,1,0:T(8,128)(2,1)} %own_ref.1), channel_id=1, source_target_pairs={{0,4},{4,0},{8,12},{12,8},{16,20},{20,16},{24,28},{28,24},{32,36},... | collective-permute-start | bytes 1572872 | tf_op jit(solution)/shard_map/ppermute | solution.py:227
  8.8 0.0 copy-start.2
  8.8 0.7 copy-done.2
  9.5 0.7 ask.1
  10.2 10.9 %all-to-all-start = ((s32[64,1,128]{2,1,0:T(1,128)}), s32[64,1,128]{2,1,0:T(1,128)S(1)}, u32[]{:S(2)}, u32[]{:S(2)}) async-start(s32[64,1,128]{2,1,0:T(1,128)} %bitcast.3), calls=%async_computation | async-start | bytes 65536 | tf_op jit(solution)/shard_map/all_to_all | solution.py:206
  21.1 0.1 pad_add_fusion.place_ref
  21.2 0.0 collective-permute-done.3.other_ref
  21.2 0.0 copy-start
  21.2 1.0 copy-done
  22.3 0.9 prepare_integrals.1.tiles_ref
  23.1 8.7 %all-to-all-done = s32[64,1,128]{2,1,0:T(1,128)S(1)} async-done(((s32[64,1,128]{2,1,0:T(1,128)}), s32[64,1,128]{2,1,0:T(1,128)S(1)}, u32[]{:S(2)}, u32[]{:S(2)}) %all-to-all-start) | async-done | bytes 32800 | tf_op jit(solution)/shard_map/all_to_all | solution.py:206
  31.9 1.7 %pick.1 = bf16[64,64,128]{2,1,0:T(8,128)(2,1)} custom-call(s32[64,128]{1,0:T(8,128)S(1)} %bitcast.17, bf16[2,16,32,128]{3,2,1,0:T(8,128)(2,1)S(1)} %prepare_integrals.1.tiles_ref), custom_call_target="tpu_custom_call" | custom-call | tf_op jit(solution)/shard_map/pick/pallas_call | solution.py:237
  33.6 0.0 copy-start.3
  33.6 0.0 copy-start.4
  33.6 0.0 copy-start.5
  33.6 0.0 copy-start.1
  33.6 4.8 %all-to-all-start.1 = ((bf16[64,64,128]{2,1,0:T(8,128)(2,1)}), bf16[64,64,128]{2,1,0:T(8,128)(2,1)S(1)}, u32[]{:S(2)}, u32[]{:S(2)}) async-start(bf16[64,64,128]{2,1,0:T(8,128)(2,1)} %pick.1), calls=%async_computation.1 | async-start | bytes 2097152 | tf_op jit(solution)/shard_map/all_to_all | solution.py:250
  39.1 0.0 copy-done.3
  39.1 0.0 copy-done.4
  39.1 0.0 copy-done.5
  39.1 0.8 read_tasks.1.refs_0_
  40.0 4.4 %collective-permute-start.2 = (s32[1,128]{1,0:T(1,128)S(1)}, s32[1,128]{1,0:T(1,128)S(1)}, u32[]{:S(2)}, u32[]{:S(2)}) collective-permute-start(s32[1,128]{1,0:T(1,128)S(1)} %read_tasks.1.refs_0_), channel_id=1, source_target_pairs={{0,3},{1,0},{2,1},{3,2},{4,7},{5,4},{6,5},{7,6},{8,11},{9,8},{10,9... | collective-permute-start | bytes 1544 | tf_op jit(solution)/shard_map/ppermute | solution.py:24
  44.4 2.4 %collective-permute-start.1 = (s32[1,128]{1,0:T(1,128)S(1)}, s32[1,128]{1,0:T(1,128)S(1)}, u32[]{:S(2)}, u32[]{:S(2)}) collective-permute-start(s32[1,128]{1,0:T(1,128)S(1)} %read_tasks.1.refs_0_), channel_id=1, source_target_pairs={{0,2},{1,3},{2,0},{3,1},{4,6},{5,7},{6,4},{7,5},{8,10},{9,11},{10,... | collective-permute-start | bytes 1544 | tf_op jit(solution)/shard_map/ppermute | solution.py:24
  46.8 2.5 %collective-permute-start = (s32[1,128]{1,0:T(1,128)S(1)}, s32[1,128]{1,0:T(1,128)S(1)}, u32[]{:S(2)}, u32[]{:S(2)}) collective-permute-start(s32[1,128]{1,0:T(1,128)S(1)} %read_tasks.1.refs_0_), channel_id=1, source_target_pairs={{0,1},{1,2},{2,3},{3,0},{4,5},{5,6},{6,7},{7,4},{8,9},{9,10},{10,1... | collective-permute-start | bytes 1544 | tf_op jit(solution)/shard_map/ppermute | solution.py:24
  49.3 0.0 copy-done.1
  49.3 0.2 prepare_lambda.1.refs_4_
  49.5 0.0 collective-permute-done.2.refs_3_
  49.5 0.9 collective-permute-done.1.refs_2_
  50.4 2.1 %collective-permute-done.refs_1_ = s32[1,128]{1,0:T(1,128)S(1)} collective-permute-done((s32[1,128]{1,0:T(1,128)S(1)}, s32[1,128]{1,0:T(1,128)S(1)}, u32[]{:S(2)}, u32[]{:S(2)}) %collective-permute-start) | collective-permute-done | bytes 544 | tf_op jit(solution)/shard_map/ppermute | solution.py:24
  52.6 12.4 %all-to-all-done.1 = bf16[64,64,128]{2,1,0:T(8,128)(2,1)S(1)} async-done(((bf16[64,64,128]{2,1,0:T(8,128)(2,1)}), bf16[64,64,128]{2,1,0:T(8,128)(2,1)S(1)}, u32[]{:S(2)}, u32[]{:S(2)}) %all-to-all-start.1) | async-done | bytes 1048608 | tf_op jit(solution)/shard_map/all_to_all | solution.py:250
  65.0 3.4 %contract.1 = s32[2112,128]{1,0:T(8,128)S(1)} custom-call(s32[1,128]{1,0:T(1,128)S(1)} %read_tasks.1.refs_0_, s32[1,128]{1,0:T(1,128)S(1)} %collective-permute-done.refs_1_, s32[1,128]{1,0:T(1,128)S(1)} %collective-permute-done.1.refs_2_, s32[1,128]{1,0:T(1,128)S(1)} %collective-permute-done.2.refs_3_, bf16[33,128,128]{2,1,0:T(8,128)(2,1)S(1)} %prepare_lambda.1.refs_4_, ...), custom_call_target="tpu_custom_call" | custom-call | tf_op jit(solution)/shard_map/contract/pallas_call | solution.py:254
  68.4 36.5 %all_to_all.20 = s32[64,33,1,128]{3,2,1,0:T(1,128)S(1)} all-to-all(s32[64,33,1,128]{3,2,1,0:T(1,128)S(1)} %bitcast.14), channel_id=1, replica_groups={{0,8,16,24,32,40,48,56,64,72,80,88,96,104,112,120,128,136,144,152,160,1..., dimensions={0} | all-to-all | bytes 2162688 | tf_op jit(solution)/shard_map/all_to_all | solution.py:263
  104.9 1.1 add_slots.1
  105.9 13.2 %all_to_all.21.x_ref = f32[8,32,128]{2,1,0:T(8,128)S(1)} all-to-all(f32[8,32,128]{2,1,0:T(8,128)S(1)} %bitcast.16), channel_id=1, replica_groups={{0,1,2,3,4,5,6,7},{8,9,10,11,12,13,14,15},{16,17,18,19,20,21,22,23},{24..., dimensions={0} | all-to-all | bytes 262144 | tf_op jit(solution)/shard_map/all_to_all | solution.py:275
  119.1 0.7 finish.1
Async XLA Ops:
  0.0 21.2 %collective-permute-start.3 = (bf16[16,128,128]{2,1,0:T(8,128)(2,1)}, bf16[16,128,128]{2,1,0:T(8,128)(2,1)S(1)}, u32[]{:S(2)}, u32[]{:S(2)}) collective-permute-start(bf16[16,128,128]{2,1,0:T(8,128)(2,1)} %own_ref.1), channel_id=1, source_target_pairs={{0,4},{4,0},{8,12},{12,8},{16,20},{20,16},{24,28},{28,24},{32,36},... | collective-permute-start | bytes 1572872 | tf_op jit(solution)/shard_map/ppermute | solution.py:227
  8.8 0.7 copy-start.2
  10.2 21.7 %all-to-all-start = ((s32[64,1,128]{2,1,0:T(1,128)}), s32[64,1,128]{2,1,0:T(1,128)S(1)}, u32[]{:S(2)}, u32[]{:S(2)}) async-start(s32[64,1,128]{2,1,0:T(1,128)} %bitcast.3), calls=%async_computation | async-start | bytes 65536 | tf_op jit(solution)/shard_map/all_to_all | solution.py:206
  21.2 1.0 copy-start
  33.6 5.5 %copy-start.3 = (s32[128,4]{0,1:T(4,128)S(1)}, s32[128,4]{0,1:T(4,128)}, u32[]{:S(2)}) copy-start(s32[128,4]{0,1:T(4,128)} %param.8) | copy-start | bytes 6148
  33.6 5.5 %copy-start.4 = (s32[512]{0:T(512)S(1)}, s32[512]{0:T(512)}, u32[]{:S(2)}) copy-start(s32[512]{0:T(512)} %param.11) | copy-start | bytes 6148
  33.6 5.5 %copy-start.5 = (s32[16]{0:T(128)S(1)}, s32[16]{0:T(128)}, u32[]{:S(2)}) copy-start(s32[16]{0:T(128)} %mask_ref.1) | copy-start | bytes 196
  33.6 15.7 %copy-start.1 = (bf16[16,128,128]{2,1,0:T(8,128)(2,1)S(1)}, bf16[16,128,128]{2,1,0:T(8,128)(2,1)}, u32[]{:S(2)}) copy-start(bf16[16,128,128]{2,1,0:T(8,128)(2,1)} %lam_ref.1) | copy-start | bytes 1572868
  33.6 31.3 %all-to-all-start.1 = ((bf16[64,64,128]{2,1,0:T(8,128)(2,1)}), bf16[64,64,128]{2,1,0:T(8,128)(2,1)S(1)}, u32[]{:S(2)}, u32[]{:S(2)}) async-start(bf16[64,64,128]{2,1,0:T(8,128)(2,1)} %pick.1), calls=%async_computation.1 | async-start | bytes 2097152 | tf_op jit(solution)/shard_map/all_to_all | solution.py:250
  40.0 9.6 %collective-permute-start.2 = (s32[1,128]{1,0:T(1,128)S(1)}, s32[1,128]{1,0:T(1,128)S(1)}, u32[]{:S(2)}, u32[]{:S(2)}) collective-permute-start(s32[1,128]{1,0:T(1,128)S(1)} %read_tasks.1.refs_0_), channel_id=1, source_target_pairs={{0,3},{1,0},{2,1},{3,2},{4,7},{5,4},{6,5},{7,6},{8,11},{9,8},{10,9... | collective-permute-start | bytes 1544 | tf_op jit(solution)/shard_map/ppermute | solution.py:24
  44.4 6.1 %collective-permute-start.1 = (s32[1,128]{1,0:T(1,128)S(1)}, s32[1,128]{1,0:T(1,128)S(1)}, u32[]{:S(2)}, u32[]{:S(2)}) collective-permute-start(s32[1,128]{1,0:T(1,128)S(1)} %read_tasks.1.refs_0_), channel_id=1, source_target_pairs={{0,2},{1,3},{2,0},{3,1},{4,6},{5,7},{6,4},{7,5},{8,10},{9,11},{10,... | collective-permute-start | bytes 1544 | tf_op jit(solution)/shard_map/ppermute | solution.py:24
  46.8 5.8 %collective-permute-start = (s32[1,128]{1,0:T(1,128)S(1)}, s32[1,128]{1,0:T(1,128)S(1)}, u32[]{:S(2)}, u32[]{:S(2)}) collective-permute-start(s32[1,128]{1,0:T(1,128)S(1)} %read_tasks.1.refs_0_), channel_id=1, source_target_pairs={{0,1},{1,2},{2,3},{3,0},{4,5},{5,6},{6,7},{7,4},{8,9},{9,10},{10,1... | collective-permute-start | bytes 1544 | tf_op jit(solution)/shard_map/ppermute | solution.py:24

commit v10 on v9

--- a/solution.py
+++ b/solution.py
@@ -203,6 +203,7 @@
         compiler_params=ROOM,
         name="ask",
     )(tasks)
+    request, swapped = lax.optimization_barrier((request, int_tiles))
     request = lax.all_to_all(
         request.reshape(chips, 1, 128), "tiles", split_axis=0, concat_axis=0, tiled=True, axis_index_groups=same_core
     ).reshape(chips, 128)
@@ -224,7 +225,7 @@
         compiler_params=ROOM,
         name="prepare_lambda",
     )(lam_tiles)
-    other = lax.ppermute(int_tiles, "tiles", [(i, i ^ 1) for i in range(tile_devs)])
+    other = lax.ppermute(swapped, "tiles", [(i, i ^ 1) for i in range(tile_devs)])
     columns = pl.pallas_call(
         prepare_integrals,
         out_shape=jax.ShapeDtypeStruct((2, int_dev, rows, edge), jnp.bfloat16),

time: 120 us -> 120 us (level)
  no operation moved by 1% of the time
where the time goes in v10:
time: 120 us
  blocking collectives  49.7 us (41%)
  starting transfers between devices  33.9 us (28%)
  waiting for transfers between devices  24.2 us (20%)
  Pallas kernels  9.5 us (8%)
  local copies, waits for them, and re-layouts  1.75 us (1%)
    all_to_all x1, blocking collectives, on_device(): lax.all_to_all(totals, 'tiles', split_axis=0, concat_axis=0, tiled=True,...  36.5 us
    all_to_all x1, blocking collectives, on_device(): lax.all_to_all(summed.reshape(2 * res_tile, rows, edge), ('tiles', 'rep')...  13.2 us
    all_to_all x1, waiting for transfers between devices, on_device(): lax.all_to_all(picked, 'tiles', split_axis=0, concat_axis=0, tiled=True,...  12.4 us
    all_to_all x1, starting transfers between devices, on_device(): lax.all_to_all(request.reshape(chips, 1, 128), 'tiles', split_axis=0, con...  10.9 us
    ppermute x3, starting transfers between devices, ring(): lax.ppermute(values, 'rep', [(i, (i + steps) % reps) for i in range(reps)])  9.34 us
    ppermute x1, starting transfers between devices, on_device(): lax.ppermute(swapped, 'tiles', [(i, i ^ 1) for i in range(tile_devs)])  8.78 us
    all_to_all x1, waiting for transfers between devices, on_device(): lax.all_to_all(request.reshape(chips, 1, 128), 'tiles', split_axis=0, con...  8.75 us
    all_to_all x1, starting transfers between devices, on_device(): lax.all_to_all(picked, 'tiles', split_axis=0, concat_axis=0, tiled=True,...  4.8 us
  transfers between devices with their start and end apart: 6, of which 4 were waited for; matrix products, arithmetic and copies ran while one was open for 0% of the time, Pallas kernels for 2%

profile of v10, /device:TPU:1, one launch (start us, length us, event | category | flops | bytes accessed | tf_op | source)
XLA Modules:
  0.0 119.9 jit_solution(1042783166074492389)
XLA Ops:
  0.0 0.0 copy-start.2
  0.0 0.7 copy-done.2
  0.7 0.7 ask.1
  1.4 8.8 %collective-permute-start.3 = (bf16[16,128,128]{2,1,0:T(8,128)(2,1)}, bf16[16,128,128]{2,1,0:T(8,128)(2,1)S(1)}, u32[]{:S(2)}, u32[]{:S(2)}) collective-permute-start(bf16[16,128,128]{2,1,0:T(8,128)(2,1)} %own_ref.1), channel_id=1, source_target_pairs={{0,4},{4,0},{8,12},{12,8},{16,20},{20,16},{24,28},{28,24},{32,36},... | collective-permute-start | bytes 1572872 | tf_op jit(solution)/shard_map/ppermute | solution.py:228
  10.2 10.9 %all-to-all-start = ((s32[64,1,128]{2,1,0:T(1,128)}), s32[64,1,128]{2,1,0:T(1,128)S(1)}, u32[]{:S(2)}, u32[]{:S(2)}) async-start(s32[64,1,128]{2,1,0:T(1,128)} %bitcast.3), calls=%async_computation | async-start | bytes 65536 | tf_op jit(solution)/shard_map/all_to_all | solution.py:207
  21.1 0.1 pad_add_fusion.place_ref
  21.2 0.0 collective-permute-done.3.other_ref
  21.2 0.0 copy-start
  21.2 1.0 copy-done
  22.3 0.9 prepare_integrals.1.tiles_ref
  23.2 8.7 %all-to-all-done = s32[64,1,128]{2,1,0:T(1,128)S(1)} async-done(((s32[64,1,128]{2,1,0:T(1,128)}), s32[64,1,128]{2,1,0:T(1,128)S(1)}, u32[]{:S(2)}, u32[]{:S(2)}) %all-to-all-start) | async-done | bytes 32800 | tf_op jit(solution)/shard_map/all_to_all | solution.py:207
  31.9 1.7 %pick.1 = bf16[64,64,128]{2,1,0:T(8,128)(2,1)} custom-call(s32[64,128]{1,0:T(8,128)S(1)} %bitcast.17, bf16[2,16,32,128]{3,2,1,0:T(8,128)(2,1)S(1)} %prepare_integrals.1.tiles_ref), custom_call_target="tpu_custom_call" | custom-call | tf_op jit(solution)/shard_map/pick/pallas_call | solution.py:238
  33.6 0.0 copy-start.3
  33.6 0.0 copy-start.4
  33.6 0.0 copy-start.5
  33.6 0.0 copy-start.1
  33.6 4.8 %all-to-all-start.1 = ((bf16[64,64,128]{2,1,0:T(8,128)(2,1)}), bf16[64,64,128]{2,1,0:T(8,128)(2,1)S(1)}, u32[]{:S(2)}, u32[]{:S(2)}) async-start(bf16[64,64,128]{2,1,0:T(8,128)(2,1)} %pick.1), calls=%async_computation.1 | async-start | bytes 2097152 | tf_op jit(solution)/shard_map/all_to_all | solution.py:251
  39.1 0.0 copy-done.3
  39.1 0.0 copy-done.4
  39.1 0.0 copy-done.5
  39.1 0.8 read_tasks.1.refs_0_
  40.0 4.4 %collective-permute-start.2 = (s32[1,128]{1,0:T(1,128)S(1)}, s32[1,128]{1,0:T(1,128)S(1)}, u32[]{:S(2)}, u32[]{:S(2)}) collective-permute-start(s32[1,128]{1,0:T(1,128)S(1)} %read_tasks.1.refs_0_), channel_id=1, source_target_pairs={{0,3},{1,0},{2,1},{3,2},{4,7},{5,4},{6,5},{7,6},{8,11},{9,8},{10,9... | collective-permute-start | bytes 1544 | tf_op jit(solution)/shard_map/ppermute | solution.py:24
  44.4 2.4 %collective-permute-start.1 = (s32[1,128]{1,0:T(1,128)S(1)}, s32[1,128]{1,0:T(1,128)S(1)}, u32[]{:S(2)}, u32[]{:S(2)}) collective-permute-start(s32[1,128]{1,0:T(1,128)S(1)} %read_tasks.1.refs_0_), channel_id=1, source_target_pairs={{0,2},{1,3},{2,0},{3,1},{4,6},{5,7},{6,4},{7,5},{8,10},{9,11},{10,... | collective-permute-start | bytes 1544 | tf_op jit(solution)/shard_map/ppermute | solution.py:24
  46.8 2.5 %collective-permute-start = (s32[1,128]{1,0:T(1,128)S(1)}, s32[1,128]{1,0:T(1,128)S(1)}, u32[]{:S(2)}, u32[]{:S(2)}) collective-permute-start(s32[1,128]{1,0:T(1,128)S(1)} %read_tasks.1.refs_0_), channel_id=1, source_target_pairs={{0,1},{1,2},{2,3},{3,0},{4,5},{5,6},{6,7},{7,4},{8,9},{9,10},{10,1... | collective-permute-start | bytes 1544 | tf_op jit(solution)/shard_map/ppermute | solution.py:24
  49.3 0.0 copy-done.1
  49.3 0.2 prepare_lambda.1.refs_4_
  49.5 0.0 collective-permute-done.2.refs_3_
  49.5 0.9 collective-permute-done.1.refs_2_
  50.4 2.1 %collective-permute-done.refs_1_ = s32[1,128]{1,0:T(1,128)S(1)} collective-permute-done((s32[1,128]{1,0:T(1,128)S(1)}, s32[1,128]{1,0:T(1,128)S(1)}, u32[]{:S(2)}, u32[]{:S(2)}) %collective-permute-start) | collective-permute-done | bytes 544 | tf_op jit(solution)/shard_map/ppermute | solution.py:24
  52.6 12.4 %all-to-all-done.1 = bf16[64,64,128]{2,1,0:T(8,128)(2,1)S(1)} async-done(((bf16[64,64,128]{2,1,0:T(8,128)(2,1)}), bf16[64,64,128]{2,1,0:T(8,128)(2,1)S(1)}, u32[]{:S(2)}, u32[]{:S(2)}) %all-to-all-start.1) | async-done | bytes 1048608 | tf_op jit(solution)/shard_map/all_to_all | solution.py:251
  65.0 3.4 %contract.1 = s32[2112,128]{1,0:T(8,128)S(1)} custom-call(s32[1,128]{1,0:T(1,128)S(1)} %read_tasks.1.refs_0_, s32[1,128]{1,0:T(1,128)S(1)} %collective-permute-done.refs_1_, s32[1,128]{1,0:T(1,128)S(1)} %collective-permute-done.1.refs_2_, s32[1,128]{1,0:T(1,128)S(1)} %collective-permute-done.2.refs_3_, bf16[33,128,128]{2,1,0:T(8,128)(2,1)S(1)} %prepare_lambda.1.refs_4_, ...), custom_call_target="tpu_custom_call" | custom-call | tf_op jit(solution)/shard_map/contract/pallas_call | solution.py:255
  68.4 36.5 %all_to_all.20 = s32[64,33,1,128]{3,2,1,0:T(1,128)S(1)} all-to-all(s32[64,33,1,128]{3,2,1,0:T(1,128)S(1)} %bitcast.14), channel_id=1, replica_groups={{0,8,16,24,32,40,48,56,64,72,80,88,96,104,112,120,128,136,144,152,160,1..., dimensions={0} | all-to-all | bytes 2162688 | tf_op jit(solution)/shard_map/all_to_all | solution.py:264
  104.8 1.1 add_slots.1
  105.9 13.2 %all_to_all.21.x_ref = f32[8,32,128]{2,1,0:T(8,128)S(1)} all-to-all(f32[8,32,128]{2,1,0:T(8,128)S(1)} %bitcast.16), channel_id=1, replica_groups={{0,1,2,3,4,5,6,7},{8,9,10,11,12,13,14,15},{16,17,18,19,20,21,22,23},{24..., dimensions={0} | all-to-all | bytes 262144 | tf_op jit(solution)/shard_map/all_to_all | solution.py:276
  119.1 0.7 finish.1
Async XLA Ops:
  0.0 0.7 copy-start.2
  1.4 19.8 %collective-permute-start.3 = (bf16[16,128,128]{2,1,0:T(8,128)(2,1)}, bf16[16,128,128]{2,1,0:T(8,128)(2,1)S(1)}, u32[]{:S(2)}, u32[]{:S(2)}) collective-permute-start(bf16[16,128,128]{2,1,0:T(8,128)(2,1)} %own_ref.1), channel_id=1, source_target_pairs={{0,4},{4,0},{8,12},{12,8},{16,20},{20,16},{24,28},{28,24},{32,36},... | collective-permute-start | bytes 1572872 | tf_op jit(solution)/shard_map/ppermute | solution.py:228
  10.2 21.7 %all-to-all-start = ((s32[64,1,128]{2,1,0:T(1,128)}), s32[64,1,128]{2,1,0:T(1,128)S(1)}, u32[]{:S(2)}, u32[]{:S(2)}) async-start(s32[64,1,128]{2,1,0:T(1,128)} %bitcast.3), calls=%async_computation | async-start | bytes 65536 | tf_op jit(solution)/shard_map/all_to_all | solution.py:207
  21.2 1.0 copy-start
  33.6 5.5 %copy-start.3 = (s32[128,4]{0,1:T(4,128)S(1)}, s32[128,4]{0,1:T(4,128)}, u32[]{:S(2)}) copy-start(s32[128,4]{0,1:T(4,128)} %param.8) | copy-start | bytes 6148
  33.6 5.5 %copy-start.4 = (s32[512]{0:T(512)S(1)}, s32[512]{0:T(512)}, u32[]{:S(2)}) copy-start(s32[512]{0:T(512)} %param.11) | copy-start | bytes 6148
  33.6 5.5 %copy-start.5 = (s32[16]{0:T(128)S(1)}, s32[16]{0:T(128)}, u32[]{:S(2)}) copy-start(s32[16]{0:T(128)} %mask_ref.1) | copy-start | bytes 196
  33.6 15.7 %copy-start.1 = (bf16[16,128,128]{2,1,0:T(8,128)(2,1)S(1)}, bf16[16,128,128]{2,1,0:T(8,128)(2,1)}, u32[]{:S(2)}) copy-start(bf16[16,128,128]{2,1,0:T(8,128)(2,1)} %lam_ref.1) | copy-start | bytes 1572868
  33.6 31.3 %all-to-all-start.1 = ((bf16[64,64,128]{2,1,0:T(8,128)(2,1)}), bf16[64,64,128]{2,1,0:T(8,128)(2,1)S(1)}, u32[]{:S(2)}, u32[]{:S(2)}) async-start(bf16[64,64,128]{2,1,0:T(8,128)(2,1)} %pick.1), calls=%async_computation.1 | async-start | bytes 2097152 | tf_op jit(solution)/shard_map/all_to_all | solution.py:251
  40.0 9.6 %collective-permute-start.2 = (s32[1,128]{1,0:T(1,128)S(1)}, s32[1,128]{1,0:T(1,128)S(1)}, u32[]{:S(2)}, u32[]{:S(2)}) collective-permute-start(s32[1,128]{1,0:T(1,128)S(1)} %read_tasks.1.refs_0_), channel_id=1, source_target_pairs={{0,3},{1,0},{2,1},{3,2},{4,7},{5,4},{6,5},{7,6},{8,11},{9,8},{10,9... | collective-permute-start | bytes 1544 | tf_op jit(solution)/shard_map/ppermute | solution.py:24
  44.4 6.1 %collective-permute-start.1 = (s32[1,128]{1,0:T(1,128)S(1)}, s32[1,128]{1,0:T(1,128)S(1)}, u32[]{:S(2)}, u32[]{:S(2)}) collective-permute-start(s32[1,128]{1,0:T(1,128)S(1)} %read_tasks.1.refs_0_), channel_id=1, source_target_pairs={{0,2},{1,3},{2,0},{3,1},{4,6},{5,7},{6,4},{7,5},{8,10},{9,11},{10,... | collective-permute-start | bytes 1544 | tf_op jit(solution)/shard_map/ppermute | solution.py:24
  46.8 5.8 %collective-permute-start = (s32[1,128]{1,0:T(1,128)S(1)}, s32[1,128]{1,0:T(1,128)S(1)}, u32[]{:S(2)}, u32[]{:S(2)}) collective-permute-start(s32[1,128]{1,0:T(1,128)S(1)} %read_tasks.1.refs_0_), channel_id=1, source_target_pairs={{0,1},{1,2},{2,3},{3,0},{4,5},{5,6},{6,7},{7,4},{8,9},{9,10},{10,1... | collective-permute-start | bytes 1544 | tf_op jit(solution)/shard_map/ppermute | solution.py:24

commit v11 on v9

--- a/solution.py
+++ b/solution.py
@@ -112,7 +112,7 @@
 def contract(*refs, slots):
     *code_refs, lam_ref, w_ref, out_ref = refs
     peers, rows, edge = w_ref.shape
-    unroll = 32
+    unroll = 64
     half = rows // 2
     words = rows + 1
 

time: 120 us -> 120 us (level)
  no operation moved by 1% of the time
where the time goes in v11:
time: 120 us
  blocking collectives  49.7 us (41%)
  starting transfers between devices  33.8 us (28%)
  waiting for transfers between devices  24.2 us (20%)
  Pallas kernels  9.62 us (8%)
  local copies, waits for them, and re-layouts  1.74 us (1%)
    all_to_all x1, blocking collectives, on_device(): lax.all_to_all(totals, 'tiles', split_axis=0, concat_axis=0, tiled=True,...  36.5 us
    all_to_all x1, blocking collectives, on_device(): lax.all_to_all(summed.reshape(2 * res_tile, rows, edge), ('tiles', 'rep')...  13.2 us
    all_to_all x1, waiting for transfers between devices, on_device(): lax.all_to_all(picked, 'tiles', split_axis=0, concat_axis=0, tiled=True,...  12.4 us
    all_to_all x1, starting transfers between devices, on_device(): lax.all_to_all(request.reshape(chips, 1, 128), 'tiles', split_axis=0, con...  10.9 us
    ppermute x3, starting transfers between devices, ring(): lax.ppermute(values, 'rep', [(i, (i + steps) % reps) for i in range(reps)])  9.34 us
    ppermute x1, starting transfers between devices, on_device(): lax.ppermute(int_tiles, 'tiles', [(i, i ^ 1) for i in range(tile_devs)])  8.78 us
    all_to_all x1, waiting for transfers between devices, on_device(): lax.all_to_all(request.reshape(chips, 1, 128), 'tiles', split_axis=0, con...  8.75 us
    all_to_all x1, starting transfers between devices, on_device(): lax.all_to_all(picked, 'tiles', split_axis=0, concat_axis=0, tiled=True,...  4.8 us
  transfers between devices with their start and end apart: 6, of which 4 were waited for; matrix products, arithmetic and copies ran while one was open for 0% of the time, Pallas kernels for 2%

profile of v11, /device:TPU:1, one launch (start us, length us, event | category | flops | bytes accessed | tf_op | source)
XLA Modules:
  0.0 120.0 jit_solution(5749317267863833868)
XLA Ops:
  0.0 8.8 %collective-permute-start.3 = (bf16[16,128,128]{2,1,0:T(8,128)(2,1)}, bf16[16,128,128]{2,1,0:T(8,128)(2,1)S(1)}, u32[]{:S(2)}, u32[]{:S(2)}) collective-permute-start(bf16[16,128,128]{2,1,0:T(8,128)(2,1)} %own_ref.1), channel_id=1, source_target_pairs={{0,4},{4,0},{8,12},{12,8},{16,20},{20,16},{24,28},{28,24},{32,36},... | collective-permute-start | bytes 1572872 | tf_op jit(solution)/shard_map/ppermute | solution.py:227
  8.8 0.0 copy-start.2
  8.8 0.7 copy-done.2
  9.5 0.7 ask.1
  10.2 10.9 %all-to-all-start = ((s32[64,1,128]{2,1,0:T(1,128)}), s32[64,1,128]{2,1,0:T(1,128)S(1)}, u32[]{:S(2)}, u32[]{:S(2)}) async-start(s32[64,1,128]{2,1,0:T(1,128)} %bitcast.3), calls=%async_computation | async-start | bytes 65536 | tf_op jit(solution)/shard_map/all_to_all | solution.py:206
  21.1 0.1 pad_add_fusion.place_ref
  21.2 0.0 collective-permute-done.3.other_ref
  21.2 0.0 copy-start
  21.2 1.0 copy-done
  22.3 0.9 prepare_integrals.1.tiles_ref
  23.1 8.7 %all-to-all-done = s32[64,1,128]{2,1,0:T(1,128)S(1)} async-done(((s32[64,1,128]{2,1,0:T(1,128)}), s32[64,1,128]{2,1,0:T(1,128)S(1)}, u32[]{:S(2)}, u32[]{:S(2)}) %all-to-all-start) | async-done | bytes 32800 | tf_op jit(solution)/shard_map/all_to_all | solution.py:206
  31.9 1.7 %pick.1 = bf16[64,64,128]{2,1,0:T(8,128)(2,1)} custom-call(s32[64,128]{1,0:T(8,128)S(1)} %bitcast.17, bf16[2,16,32,128]{3,2,1,0:T(8,128)(2,1)S(1)} %prepare_integrals.1.tiles_ref), custom_call_target="tpu_custom_call" | custom-call | tf_op jit(solution)/shard_map/pick/pallas_call | solution.py:237
  33.6 0.0 copy-start.3
  33.6 0.0 copy-start.4
  33.6 0.0 copy-start.5
  33.6 0.0 copy-start.1
  33.6 4.8 %all-to-all-start.1 = ((bf16[64,64,128]{2,1,0:T(8,128)(2,1)}), bf16[64,64,128]{2,1,0:T(8,128)(2,1)S(1)}, u32[]{:S(2)}, u32[]{:S(2)}) async-start(bf16[64,64,128]{2,1,0:T(8,128)(2,1)} %pick.1), calls=%async_computation.1 | async-start | bytes 2097152 | tf_op jit(solution)/shard_map/all_to_all | solution.py:250
  39.1 0.0 copy-done.3
  39.1 0.0 copy-done.4
  39.1 0.0 copy-done.5
  39.1 0.8 read_tasks.1.refs_0_
  40.0 4.4 %collective-permute-start.2 = (s32[1,128]{1,0:T(1,128)S(1)}, s32[1,128]{1,0:T(1,128)S(1)}, u32[]{:S(2)}, u32[]{:S(2)}) collective-permute-start(s32[1,128]{1,0:T(1,128)S(1)} %read_tasks.1.refs_0_), channel_id=1, source_target_pairs={{0,3},{1,0},{2,1},{3,2},{4,7},{5,4},{6,5},{7,6},{8,11},{9,8},{10,9... | collective-permute-start | bytes 1544 | tf_op jit(solution)/shard_map/ppermute | solution.py:24
  44.4 2.4 %collective-permute-start.1 = (s32[1,128]{1,0:T(1,128)S(1)}, s32[1,128]{1,0:T(1,128)S(1)}, u32[]{:S(2)}, u32[]{:S(2)}) collective-permute-start(s32[1,128]{1,0:T(1,128)S(1)} %read_tasks.1.refs_0_), channel_id=1, source_target_pairs={{0,2},{1,3},{2,0},{3,1},{4,6},{5,7},{6,4},{7,5},{8,10},{9,11},{10,... | collective-permute-start | bytes 1544 | tf_op jit(solution)/shard_map/ppermute | solution.py:24
  46.8 2.5 %collective-permute-start = (s32[1,128]{1,0:T(1,128)S(1)}, s32[1,128]{1,0:T(1,128)S(1)}, u32[]{:S(2)}, u32[]{:S(2)}) collective-permute-start(s32[1,128]{1,0:T(1,128)S(1)} %read_tasks.1.refs_0_), channel_id=1, source_target_pairs={{0,1},{1,2},{2,3},{3,0},{4,5},{5,6},{6,7},{7,4},{8,9},{9,10},{10,1... | collective-permute-start | bytes 1544 | tf_op jit(solution)/shard_map/ppermute | solution.py:24
  49.3 0.0 copy-done.1
  49.3 0.2 prepare_lambda.1.refs_4_
  49.5 0.0 collective-permute-done.2.refs_3_
  49.5 0.9 collective-permute-done.1.refs_2_
  50.4 2.1 %collective-permute-done.refs_1_ = s32[1,128]{1,0:T(1,128)S(1)} collective-permute-done((s32[1,128]{1,0:T(1,128)S(1)}, s32[1,128]{1,0:T(1,128)S(1)}, u32[]{:S(2)}, u32[]{:S(2)}) %collective-permute-start) | collective-permute-done | bytes 544 | tf_op jit(solution)/shard_map/ppermute | solution.py:24
  52.6 12.4 %all-to-all-done.1 = bf16[64,64,128]{2,1,0:T(8,128)(2,1)S(1)} async-done(((bf16[64,64,128]{2,1,0:T(8,128)(2,1)}), bf16[64,64,128]{2,1,0:T(8,128)(2,1)S(1)}, u32[]{:S(2)}, u32[]{:S(2)}) %all-to-all-start.1) | async-done | bytes 1048608 | tf_op jit(solution)/shard_map/all_to_all | solution.py:250
  65.0 3.5 %contract.1 = s32[2112,128]{1,0:T(8,128)S(1)} custom-call(s32[1,128]{1,0:T(1,128)S(1)} %read_tasks.1.refs_0_, s32[1,128]{1,0:T(1,128)S(1)} %collective-permute-done.refs_1_, s32[1,128]{1,0:T(1,128)S(1)} %collective-permute-done.1.refs_2_, s32[1,128]{1,0:T(1,128)S(1)} %collective-permute-done.2.refs_3_, bf16[33,128,128]{2,1,0:T(8,128)(2,1)S(1)} %prepare_lambda.1.refs_4_, ...), custom_call_target="tpu_custom_call" | custom-call | tf_op jit(solution)/shard_map/contract/pallas_call | solution.py:254
  68.5 36.5 %all_to_all.20 = s32[64,33,1,128]{3,2,1,0:T(1,128)S(1)} all-to-all(s32[64,33,1,128]{3,2,1,0:T(1,128)S(1)} %bitcast.14), channel_id=1, replica_groups={{0,8,16,24,32,40,48,56,64,72,80,88,96,104,112,120,128,136,144,152,160,1..., dimensions={0} | all-to-all | bytes 2162688 | tf_op jit(solution)/shard_map/all_to_all | solution.py:263
  105.0 1.1 add_slots.1
  106.1 13.2 %all_to_all.21.x_ref = f32[8,32,128]{2,1,0:T(8,128)S(1)} all-to-all(f32[8,32,128]{2,1,0:T(8,128)S(1)} %bitcast.16), channel_id=1, replica_groups={{0,1,2,3,4,5,6,7},{8,9,10,11,12,13,14,15},{16,17,18,19,20,21,22,23},{24..., dimensions={0} | all-to-all | bytes 262144 | tf_op jit(solution)/shard_map/all_to_all | solution.py:275
  119.3 0.7 finish.1
Async XLA Ops:
  0.0 21.2 %collective-permute-start.3 = (bf16[16,128,128]{2,1,0:T(8,128)(2,1)}, bf16[16,128,128]{2,1,0:T(8,128)(2,1)S(1)}, u32[]{:S(2)}, u32[]{:S(2)}) collective-permute-start(bf16[16,128,128]{2,1,0:T(8,128)(2,1)} %own_ref.1), channel_id=1, source_target_pairs={{0,4},{4,0},{8,12},{12,8},{16,20},{20,16},{24,28},{28,24},{32,36},... | collective-permute-start | bytes 1572872 | tf_op jit(solution)/shard_map/ppermute | solution.py:227
  8.8 0.7 copy-start.2
  10.2 21.7 %all-to-all-start = ((s32[64,1,128]{2,1,0:T(1,128)}), s32[64,1,128]{2,1,0:T(1,128)S(1)}, u32[]{:S(2)}, u32[]{:S(2)}) async-start(s32[64,1,128]{2,1,0:T(1,128)} %bitcast.3), calls=%async_computation | async-start | bytes 65536 | tf_op jit(solution)/shard_map/all_to_all | solution.py:206
  21.2 1.0 copy-start
  33.6 5.5 %copy-start.3 = (s32[128,4]{0,1:T(4,128)S(1)}, s32[128,4]{0,1:T(4,128)}, u32[]{:S(2)}) copy-start(s32[128,4]{0,1:T(4,128)} %param.8) | copy-start | bytes 6148
  33.6 5.5 %copy-start.4 = (s32[512]{0:T(512)S(1)}, s32[512]{0:T(512)}, u32[]{:S(2)}) copy-start(s32[512]{0:T(512)} %param.11) | copy-start | bytes 6148
  33.6 5.5 %copy-start.5 = (s32[16]{0:T(128)S(1)}, s32[16]{0:T(128)}, u32[]{:S(2)}) copy-start(s32[16]{0:T(128)} %mask_ref.1) | copy-start | bytes 196
  33.6 15.7 %copy-start.1 = (bf16[16,128,128]{2,1,0:T(8,128)(2,1)S(1)}, bf16[16,128,128]{2,1,0:T(8,128)(2,1)}, u32[]{:S(2)}) copy-start(bf16[16,128,128]{2,1,0:T(8,128)(2,1)} %lam_ref.1) | copy-start | bytes 1572868
  33.6 31.3 %all-to-all-start.1 = ((bf16[64,64,128]{2,1,0:T(8,128)(2,1)}), bf16[64,64,128]{2,1,0:T(8,128)(2,1)S(1)}, u32[]{:S(2)}, u32[]{:S(2)}) async-start(bf16[64,64,128]{2,1,0:T(8,128)(2,1)} %pick.1), calls=%async_computation.1 | async-start | bytes 2097152 | tf_op jit(solution)/shard_map/all_to_all | solution.py:250
  40.0 9.6 %collective-permute-start.2 = (s32[1,128]{1,0:T(1,128)S(1)}, s32[1,128]{1,0:T(1,128)S(1)}, u32[]{:S(2)}, u32[]{:S(2)}) collective-permute-start(s32[1,128]{1,0:T(1,128)S(1)} %read_tasks.1.refs_0_), channel_id=1, source_target_pairs={{0,3},{1,0},{2,1},{3,2},{4,7},{5,4},{6,5},{7,6},{8,11},{9,8},{10,9... | collective-permute-start | bytes 1544 | tf_op jit(solution)/shard_map/ppermute | solution.py:24
  44.4 6.1 %collective-permute-start.1 = (s32[1,128]{1,0:T(1,128)S(1)}, s32[1,128]{1,0:T(1,128)S(1)}, u32[]{:S(2)}, u32[]{:S(2)}) collective-permute-start(s32[1,128]{1,0:T(1,128)S(1)} %read_tasks.1.refs_0_), channel_id=1, source_target_pairs={{0,2},{1,3},{2,0},{3,1},{4,6},{5,7},{6,4},{7,5},{8,10},{9,11},{10,... | collective-permute-start | bytes 1544 | tf_op jit(solution)/shard_map/ppermute | solution.py:24
  46.8 5.8 %collective-permute-start = (s32[1,128]{1,0:T(1,128)S(1)}, s32[1,128]{1,0:T(1,128)S(1)}, u32[]{:S(2)}, u32[]{:S(2)}) collective-permute-start(s32[1,128]{1,0:T(1,128)S(1)} %read_tasks.1.refs_0_), channel_id=1, source_target_pairs={{0,1},{1,2},{2,3},{3,0},{4,5},{5,6},{6,7},{7,4},{8,9},{9,10},{10,1... | collective-permute-start | bytes 1544 | tf_op jit(solution)/shard_map/ppermute | solution.py:24
